TPU v7x, 256 devices: a whole 4x4x8 slice. The times are simulated.
256 devices in a mesh: patch: 64 (over y, z_lo, x), quad: 4 (over z_hi, core).
Axes of the slice: x: 4, y: 4, z: 8 (z_hi: 2, z_lo: 4; z = z_hi * 4 + z_lo), core: 2. Of those that a mesh axis runs over, the one named last changes fastest.
Arguments:
- vectors: float32 [64, 24, 128, 512], P('patch', None, 'quad'), may hold values from -6 to 6
- log_kappa: float32 [64, 128, 512], P('patch', 'quad'), may hold values from -3 to 3, as said below
Outputs:
- basis: float32 [64, 24, 128, 256], P('patch', None, 'quad')
- coupling: float32 [64, 2, 24, 24], P('patch')
Inputs may be any that keep to these rules, and one draw needn't show every extreme that they name: The patches are windows of one strip: log_kappa[p, r, 256 + c] equals log_kappa[p + 1, r, c] for 0 <= c < 256.
All inputs are finite; a program needn't handle non-finite values.
Results may differ from a plain program's by a relative error of at most 0.0003.
Values sent between devices are 32-bit elements; how exact they have to be, the bound alone decides.
No kernel may reach another device: no remote copies, remote signals or barrier semaphores. Data moves between devices by JAX's collectives and lax.ppermute only.
A program may use at most 64 MiB of HBM per device.

v0:
```python
import jax
import jax.numpy as jnp
from jax import lax
from jax.sharding import PartitionSpec as P

SWEEPS = 8


mass_term = 0.1
lower_bound = 0.05
upper_bound = 2.0
mid_value = 0.5 * (upper_bound + lower_bound)
half_width = 0.5 * (upper_bound - lower_bound)
ratio_start = mid_value / half_width
highest = lax.Precision.HIGHEST


def padded_2(x, sides, width):
    for axis, dim in sides:
        size, length = (lax.axis_size(axis), x.shape[dim])
        up = [(i, (i + 1) % size) for i in range(size - 1)]
        down = [(j, i) for i, j in up]
        last = lax.slice_in_dim(x, length - width, length, axis=dim)
        leading = lax.slice_in_dim(x, 0, width, axis=dim)
        before = lax.ppermute(last, axis, up)
        after = lax.ppermute(leading, axis, down)
        x = jnp.concatenate([before, x, after], axis=dim)
    return x


def shifted(block, axis, distance):
    devices = range(lax.axis_size(axis))
    route = [(i - distance, i) for i in devices if i - distance in devices]
    return lax.ppermute(block, axis, route)


def face_weights(kappa_pad, lo_row, hi_row):
    centre = kappa_pad[lo_row:hi_row, 1:-1]
    upper_face = 0.5 * (centre + kappa_pad[lo_row - 1 : hi_row - 1, 1:-1])
    lower_face = 0.5 * (centre + kappa_pad[lo_row + 1 : hi_row + 1, 1:-1])
    left_face = 0.5 * (centre + kappa_pad[lo_row:hi_row, :-2])
    right_face = 0.5 * (centre + kappa_pad[lo_row:hi_row, 2:])
    diagonal = upper_face + lower_face + left_face + right_face + mass_term * centre
    return (upper_face, lower_face, left_face, right_face, diagonal)


def apply_operator(padded, weights):
    upper_face, lower_face, left_face, right_face, diagonal = weights
    centre = padded[:, 1:-1, :]
    sideways = jnp.pad(centre, ((0, 0), (0, 0), (1, 1)))
    return diagonal * centre - (
        upper_face * padded[:, :-2, :]
        + lower_face * padded[:, 2:, :]
        + left_face * sideways[:, :, :-2]
        + right_face * sideways[:, :, 2:]
    )


def narrow_rim(values):
    return padded_2(values, (("quad", 1),), 1)


def gram_matrix(values, band_cols, half_cols):
    subdomain = values[:, :, band_cols : band_cols + half_cols].reshape(values.shape[0], -1)
    return jnp.dot(subdomain, subdomain.T, precision=highest)


def on_device(vectors, log_kappa):
    start_vectors = vectors[0]
    vec_count, height, width_all = start_vectors.shape
    half_cols = width_all // 2
    band_cols = width_all // 4
    log_rim = padded_2(log_kappa[0], (("quad", 0),), SWEEPS)
    kappa_pad = jnp.exp(jnp.pad(log_rim, ((0, 0), (1, 1))))
    inner_weights = face_weights(kappa_pad, SWEEPS - 0, height + SWEEPS + 0)
    iterate = start_vectors
    rho_now = 1.0 / ratio_start
    residual = -apply_operator(narrow_rim(iterate), inner_weights) / inner_weights[4]
    direction = residual / mid_value
    for turn_index in range(SWEEPS):
        iterate = iterate + direction
        if turn_index < SWEEPS - 1:
            residual = (
                residual - apply_operator(narrow_rim(direction), inner_weights) / inner_weights[4]
            )
            rho_next = 1.0 / (2.0 * ratio_start - rho_now)
            direction = rho_next * rho_now * direction + 2.0 * rho_next / half_width * residual
            rho_now = rho_next
    gram = lax.psum(gram_matrix(iterate, band_cols, half_cols), "quad")
    factor = jnp.linalg.cholesky(gram)
    finished = jax.scipy.linalg.solve_triangular(factor, iterate.reshape(vec_count, -1), lower=True)
    finished = finished.reshape(iterate.shape)
    from_right = shifted(finished[:, :, band_cols:half_cols], "patch", -1)
    from_left = shifted(finished[:, :, half_cols : half_cols + band_cols], "patch", 1)
    right_block = jnp.dot(
        finished[:, :, half_cols + band_cols :].reshape(vec_count, -1),
        from_right.reshape(vec_count, -1).T,
        precision=highest,
    )
    left_block = jnp.dot(
        finished[:, :, :band_cols].reshape(vec_count, -1),
        from_left.reshape(vec_count, -1).T,
        precision=highest,
    )
    coupling = lax.psum(jnp.stack((left_block, right_block)), "quad")
    return (finished[:, :, band_cols : band_cols + half_cols][None], coupling[None])


def solution(mesh):
    placed = (P("patch", None, "quad", None), P("patch", "quad", None))
    return jax.shard_map(
        on_device,
        mesh=mesh,
        in_specs=placed,
        out_specs=(P("patch", None, "quad", None), P("patch", None, None, None)),
        check_vma=False,
    )
```

profile of v0, /device:TPU:25, one launch (start us, length us, event | category | flops | bytes accessed | tf_op | source)
XLA Modules:
  0.0 190.8 jit_solution(16644153505104147667)
XLA Ops:
  0.6 0.7 slice_bitcast_fusion.2
  1.4 9.4 %collective-permute-start = (f32[8,512]{1,0:T(8,128)S(1)}, f32[8,512]{1,0:T(8,128)S(1)}, u32[]{:S(2)}, u32[]{:S(2)}) collective-permute-start(f32[8,512]{1,0:T(8,128)S(1)} %get-tuple-element.41), channel_id=1, source_target_pairs={{0,1},{1,2},{2,3},{4,5},{5,6},{6,7},{8,9},{9,10},{10,11},{12,13},{... | collective-permute-start | bytes 49160 | tf_op jit(solution)/shard_map/ppermute | solution.py:25
  10.8 2.1 %collective-permute-start.1 = (f32[8,512]{1,0:T(8,128)S(1)}, f32[8,512]{1,0:T(8,128)S(1)}, u32[]{:S(2)}, u32[]{:S(2)}) collective-permute-start(f32[8,512]{1,0:T(8,128)S(1)} %get-tuple-element.42), channel_id=1, source_target_pairs={{1,0},{2,1},{3,2},{5,4},{6,5},{7,6},{9,8},{10,9},{11,10},{13,12},{... | collective-permute-start | bytes 49160 | tf_op jit(solution)/shard_map/ppermute | solution.py:26
  12.8 2.3 %copy.32 = f32[1,24,32,512]{3,1,2,0:T(8,128)S(1)} copy(f32[1,24,32,512]{3,2,1,0:T(8,128)} %param.2) | data formatting | bytes 3145728 | tf_op args[0]
  15.2 7.5 %collective-permute-start.2 = (f32[24,1,512]{2,0,1:T(8,128)S(1)}, f32[24,1,512]{2,0,1:T(8,128)S(1)}, u32[]{:S(2)}, u32[]{:S(2)}) collective-permute-start(f32[24,1,512]{2,0,1:T(8,128)S(1)} %get-tuple-element.39), channel_id=1, source_target_pairs={{0,1},{1,2},{2,3},{4,5},{5,6},{6,7},{8,9},{9,10},{10,11},{12,13},{... | collective-permute-start | bytes 147464 | tf_op jit(solution)/shard_map/ppermute | solution.py:25
  22.7 1.9 %collective-permute-start.3 = (f32[24,1,512]{2,0,1:T(8,128)S(1)}, f32[24,1,512]{2,0,1:T(8,128)S(1)}, u32[]{:S(2)}, u32[]{:S(2)}) collective-permute-start(f32[24,1,512]{2,0,1:T(8,128)S(1)} %get-tuple-element.40), channel_id=1, source_target_pairs={{1,0},{2,1},{3,2},{5,4},{6,5},{7,6},{9,8},{10,9},{11,10},{13,12},{... | collective-permute-start | bytes 147464 | tf_op jit(solution)/shard_map/ppermute | solution.py:26
  25.0 7.0 %collective-permute-done.3 = f32[24,1,512]{2,0,1:T(8,128)S(1)} collective-permute-done((f32[24,1,512]{2,0,1:T(8,128)S(1)}, f32[24,1,512]{2,0,1:T(8,128)S(1)}, u32[]{:S(2)}, u32[]{:S(2)}) %collective-permute-start.3) | collective-permute-done | bytes 49184 | tf_op jit(solution)/shard_map/ppermute | solution.py:26
  32.0 1.0 broadcast_multiply_fusion
  33.1 1.9 %collective-permute-start.4 = (f32[24,1,512]{2,0,1:T(8,128)S(1)}, f32[24,1,512]{2,0,1:T(8,128)S(1)}, u32[]{:S(2)}, u32[]{:S(2)}) collective-permute-start(f32[24,1,512]{2,0,1:T(8,128)S(1)} %get-tuple-element.37), channel_id=1, source_target_pairs={{0,1},{1,2},{2,3},{4,5},{5,6},{6,7},{8,9},{9,10},{10,11},{12,13},{... | collective-permute-start | bytes 147464 | tf_op jit(solution)/shard_map/ppermute | solution.py:25
  35.0 2.4 %collective-permute-start.5 = (f32[24,1,512]{2,0,1:T(8,128)S(1)}, f32[24,1,512]{2,0,1:T(8,128)S(1)}, u32[]{:S(2)}, u32[]{:S(2)}) collective-permute-start(f32[24,1,512]{2,0,1:T(8,128)S(1)} %get-tuple-element.38), channel_id=1, source_target_pairs={{1,0},{2,1},{3,2},{5,4},{6,5},{7,6},{9,8},{10,9},{11,10},{13,12},{... | collective-permute-start | bytes 147464 | tf_op jit(solution)/shard_map/ppermute | solution.py:26
  37.4 6.9 %collective-permute-done.5 = f32[24,1,512]{2,0,1:T(8,128)S(1)} collective-permute-done((f32[24,1,512]{2,0,1:T(8,128)S(1)}, f32[24,1,512]{2,0,1:T(8,128)S(1)}, u32[]{:S(2)}, u32[]{:S(2)}) %collective-permute-start.5) | collective-permute-done | bytes 49184 | tf_op jit(solution)/shard_map/ppermute | solution.py:26
  44.3 2.0 %multiply_add_fusion.5 = (f32[24,32,512]{2,0,1:T(8,128)S(1)}, f32[24,32,512]{2,0,1:T(8,128)S(1)}) fusion(f32[24,32,512]{2,0,1:T(8,128)S(1)} %get-tuple-element.22, f32[32,512]{1,0:T(8,128)S(1)} %multiply_add_fusion.6, f32[32,512]{1,0:T(8,128)S(1)} %get-tuple-element.20, f32[24,32,512]{2,0,1:T(8,128)S(1)} %get-tuple-element.21, ...), kind=kLoop, calls=%fused_computation.122 | loop fusion | flops 6291456 | bytes 6782976 | tf_op jit(solution)/shard_map/add | solution.py:87
  46.3 1.9 %collective-permute-start.6 = (f32[24,1,512]{2,0,1:T(8,128)S(1)}, f32[24,1,512]{2,0,1:T(8,128)S(1)}, u32[]{:S(2)}, u32[]{:S(2)}) collective-permute-start(f32[24,1,512]{2,0,1:T(8,128)S(1)} %get-tuple-element.35), channel_id=1, source_target_pairs={{0,1},{1,2},{2,3},{4,5},{5,6},{6,7},{8,9},{9,10},{10,11},{12,13},{... | collective-permute-start | bytes 147464 | tf_op jit(solution)/shard_map/ppermute | solution.py:25
  48.3 2.4 %collective-permute-start.7 = (f32[24,1,512]{2,0,1:T(8,128)S(1)}, f32[24,1,512]{2,0,1:T(8,128)S(1)}, u32[]{:S(2)}, u32[]{:S(2)}) collective-permute-start(f32[24,1,512]{2,0,1:T(8,128)S(1)} %get-tuple-element.36), channel_id=1, source_target_pairs={{1,0},{2,1},{3,2},{5,4},{6,5},{7,6},{9,8},{10,9},{11,10},{13,12},{... | collective-permute-start | bytes 147464 | tf_op jit(solution)/shard_map/ppermute | solution.py:26
  50.7 6.9 %collective-permute-done.7 = f32[24,1,512]{2,0,1:T(8,128)S(1)} collective-permute-done((f32[24,1,512]{2,0,1:T(8,128)S(1)}, f32[24,1,512]{2,0,1:T(8,128)S(1)}, u32[]{:S(2)}, u32[]{:S(2)}) %collective-permute-start.7) | collective-permute-done | bytes 49184 | tf_op jit(solution)/shard_map/ppermute | solution.py:26
  57.6 1.5 multiply_add_fusion.4
  59.1 1.9 %collective-permute-start.8 = (f32[24,1,512]{2,0,1:T(8,128)S(1)}, f32[24,1,512]{2,0,1:T(8,128)S(1)}, u32[]{:S(2)}, u32[]{:S(2)}) collective-permute-start(f32[24,1,512]{2,0,1:T(8,128)S(1)} %get-tuple-element.33), channel_id=1, source_target_pairs={{0,1},{1,2},{2,3},{4,5},{5,6},{6,7},{8,9},{9,10},{10,11},{12,13},{... | collective-permute-start | bytes 147464 | tf_op jit(solution)/shard_map/ppermute | solution.py:25
  61.0 2.4 %collective-permute-start.9 = (f32[24,1,512]{2,0,1:T(8,128)S(1)}, f32[24,1,512]{2,0,1:T(8,128)S(1)}, u32[]{:S(2)}, u32[]{:S(2)}) collective-permute-start(f32[24,1,512]{2,0,1:T(8,128)S(1)} %get-tuple-element.34), channel_id=1, source_target_pairs={{1,0},{2,1},{3,2},{5,4},{6,5},{7,6},{9,8},{10,9},{11,10},{13,12},{... | collective-permute-start | bytes 147464 | tf_op jit(solution)/shard_map/ppermute | solution.py:26
  63.5 6.9 %collective-permute-done.9 = f32[24,1,512]{2,0,1:T(8,128)S(1)} collective-permute-done((f32[24,1,512]{2,0,1:T(8,128)S(1)}, f32[24,1,512]{2,0,1:T(8,128)S(1)}, u32[]{:S(2)}, u32[]{:S(2)}) %collective-permute-start.9) | collective-permute-done | bytes 49184 | tf_op jit(solution)/shard_map/ppermute | solution.py:26
  70.4 1.5 multiply_add_fusion.3
  71.9 1.9 %collective-permute-start.10 = (f32[24,1,512]{2,0,1:T(8,128)S(1)}, f32[24,1,512]{2,0,1:T(8,128)S(1)}, u32[]{:S(2)}, u32[]{:S(2)}) collective-permute-start(f32[24,1,512]{2,0,1:T(8,128)S(1)} %get-tuple-element.31), channel_id=1, source_target_pairs={{0,1},{1,2},{2,3},{4,5},{5,6},{6,7},{8,9},{9,10},{10,11},{12,13},{... | collective-permute-start | bytes 147464 | tf_op jit(solution)/shard_map/ppermute | solution.py:25
  73.8 2.4 %collective-permute-start.11 = (f32[24,1,512]{2,0,1:T(8,128)S(1)}, f32[24,1,512]{2,0,1:T(8,128)S(1)}, u32[]{:S(2)}, u32[]{:S(2)}) collective-permute-start(f32[24,1,512]{2,0,1:T(8,128)S(1)} %get-tuple-element.32), channel_id=1, source_target_pairs={{1,0},{2,1},{3,2},{5,4},{6,5},{7,6},{9,8},{10,9},{11,10},{13,12},{... | collective-permute-start | bytes 147464 | tf_op jit(solution)/shard_map/ppermute | solution.py:26
  76.2 6.9 %collective-permute-done.11 = f32[24,1,512]{2,0,1:T(8,128)S(1)} collective-permute-done((f32[24,1,512]{2,0,1:T(8,128)S(1)}, f32[24,1,512]{2,0,1:T(8,128)S(1)}, u32[]{:S(2)}, u32[]{:S(2)}) %collective-permute-start.11) | collective-permute-done | bytes 49184 | tf_op jit(solution)/shard_map/ppermute | solution.py:26
  83.1 1.5 multiply_add_fusion.2
  84.6 1.9 %collective-permute-start.12 = (f32[24,1,512]{2,0,1:T(8,128)S(1)}, f32[24,1,512]{2,0,1:T(8,128)S(1)}, u32[]{:S(2)}, u32[]{:S(2)}) collective-permute-start(f32[24,1,512]{2,0,1:T(8,128)S(1)} %get-tuple-element.29), channel_id=1, source_target_pairs={{0,1},{1,2},{2,3},{4,5},{5,6},{6,7},{8,9},{9,10},{10,11},{12,13},{... | collective-permute-start | bytes 147464 | tf_op jit(solution)/shard_map/ppermute | solution.py:25
  86.6 2.4 %collective-permute-start.13 = (f32[24,1,512]{2,0,1:T(8,128)S(1)}, f32[24,1,512]{2,0,1:T(8,128)S(1)}, u32[]{:S(2)}, u32[]{:S(2)}) collective-permute-start(f32[24,1,512]{2,0,1:T(8,128)S(1)} %get-tuple-element.30), channel_id=1, source_target_pairs={{1,0},{2,1},{3,2},{5,4},{6,5},{7,6},{9,8},{10,9},{11,10},{13,12},{... | collective-permute-start | bytes 147464 | tf_op jit(solution)/shard_map/ppermute | solution.py:26
  89.0 6.9 %collective-permute-done.13 = f32[24,1,512]{2,0,1:T(8,128)S(1)} collective-permute-done((f32[24,1,512]{2,0,1:T(8,128)S(1)}, f32[24,1,512]{2,0,1:T(8,128)S(1)}, u32[]{:S(2)}, u32[]{:S(2)}) %collective-permute-start.13) | collective-permute-done | bytes 49184 | tf_op jit(solution)/shard_map/ppermute | solution.py:26
  95.9 1.5 multiply_add_fusion.1
  97.4 1.9 %collective-permute-start.14 = (f32[24,1,512]{2,0,1:T(8,128)S(1)}, f32[24,1,512]{2,0,1:T(8,128)S(1)}, u32[]{:S(2)}, u32[]{:S(2)}) collective-permute-start(f32[24,1,512]{2,0,1:T(8,128)S(1)} %get-tuple-element.27), channel_id=1, source_target_pairs={{0,1},{1,2},{2,3},{4,5},{5,6},{6,7},{8,9},{9,10},{10,11},{12,13},{... | collective-permute-start | bytes 147464 | tf_op jit(solution)/shard_map/ppermute | solution.py:25
  99.3 2.4 %collective-permute-start.15 = (f32[24,1,512]{2,0,1:T(8,128)S(1)}, f32[24,1,512]{2,0,1:T(8,128)S(1)}, u32[]{:S(2)}, u32[]{:S(2)}) collective-permute-start(f32[24,1,512]{2,0,1:T(8,128)S(1)} %get-tuple-element.28), channel_id=1, source_target_pairs={{1,0},{2,1},{3,2},{5,4},{6,5},{7,6},{9,8},{10,9},{11,10},{13,12},{... | collective-permute-start | bytes 147464 | tf_op jit(solution)/shard_map/ppermute | solution.py:26
  101.8 6.9 %collective-permute-done.15 = f32[24,1,512]{2,0,1:T(8,128)S(1)} collective-permute-done((f32[24,1,512]{2,0,1:T(8,128)S(1)}, f32[24,1,512]{2,0,1:T(8,128)S(1)}, u32[]{:S(2)}, u32[]{:S(2)}) %collective-permute-start.15) | collective-permute-done | bytes 49184 | tf_op jit(solution)/shard_map/ppermute | solution.py:26
  108.7 1.5 multiply_add_fusion
  110.2 1.9 %collective-permute-start.16 = (f32[24,1,512]{2,0,1:T(8,128)S(1)}, f32[24,1,512]{2,0,1:T(8,128)S(1)}, u32[]{:S(2)}, u32[]{:S(2)}) collective-permute-start(f32[24,1,512]{2,0,1:T(8,128)S(1)} %get-tuple-element.25), channel_id=1, source_target_pairs={{0,1},{1,2},{2,3},{4,5},{5,6},{6,7},{8,9},{9,10},{10,11},{12,13},{... | collective-permute-start | bytes 147464 | tf_op jit(solution)/shard_map/ppermute | solution.py:25
  112.1 2.6 %collective-permute-start.17 = (f32[24,1,512]{2,0,1:T(8,128)S(1)}, f32[24,1,512]{2,0,1:T(8,128)S(1)}, u32[]{:S(2)}, u32[]{:S(2)}) collective-permute-start(f32[24,1,512]{2,0,1:T(8,128)S(1)} %get-tuple-element.26), channel_id=1, source_target_pairs={{1,0},{2,1},{3,2},{5,4},{6,5},{7,6},{9,8},{10,9},{11,10},{13,12},{... | collective-permute-start | bytes 147464 | tf_op jit(solution)/shard_map/ppermute | solution.py:26
  114.7 6.7 %collective-permute-done.17 = f32[24,1,512]{2,0,1:T(8,128)S(1)} collective-permute-done((f32[24,1,512]{2,0,1:T(8,128)S(1)}, f32[24,1,512]{2,0,1:T(8,128)S(1)}, u32[]{:S(2)}, u32[]{:S(2)}) %collective-permute-start.17) | collective-permute-done | bytes 49184 | tf_op jit(solution)/shard_map/ppermute | solution.py:26
  121.4 6.4 %add_add_fusion = f32[24,32,512]{2,0,1:T(8,128)S(1)} fusion(f32[24,32,512]{2,0,1:T(8,128)S(1)} %multiply_add_fusion, f32[24,1,512]{2,0,1:T(8,128)S(1)} %collective-permute-done.17, f32[24,1,512]{2,0,1:T(8,128)S(1)} %collective-permute-done.16, f32[24,32,512]{2,0,1:T(8,128)S(1)} %get-tuple-element.6, f32[24,32,512]{2,0,1:T(8,128)S(1)} %get-tuple-element.8, ...), kind=kLoop, calls=%fused_computation.116 | loop fusion | flops 14942208 | bytes 16252928 | tf_op jit(solution)/shard_map/add | solution.py:81
  127.9 0.9 convolution_bitcast_fusion
  128.8 17.2 %psum.14 = f32[24,24]{0,1:T(8,128)S(1)} all-reduce(f32[24,24]{0,1:T(8,128)S(1)} %convolution_bitcast_fusion), channel_id=1, replica_groups=mesh['patch'=64,'quad'=4] {'quad'}, use_global_device_ids=true, to_apply=%region_0.1 | all-reduce | flops 576 | bytes 4608 | tf_op jit(solution)/shard_map/psum | solution.py:89
  146.1 2.2 %cholesky.16 = f32[24,24]{1,0:T(8,128)S(1)} custom-call(f32[24,24]{1,0:T(8,128)S(1)} %fusion.95), custom_call_target="Cholesky" | custom-call | tf_op jit(solution)/shard_map/jit(cholesky)/cholesky | solution.py:90
  148.3 0.6 compare_reduce_fusion
  148.9 0.6 fusion.93
  149.6 1.8 custom-call.7
  151.4 1.4 fusion.56
  152.9 3.1 %collective-permute-start.18 = (f32[24,32,128]{2,0,1:T(8,128)S(1)}, f32[24,32,128]{2,0,1:T(8,128)S(1)}, u32[]{:S(2)}, u32[]{:S(2)}) collective-permute-start(f32[24,32,128]{2,0,1:T(8,128)S(1)} %get-tuple-element.23), channel_id=1, source_target_pairs={{0,4},{4,8},{8,12},{12,16},{16,20},{20,24},{24,28},{28,32},{32,36}... | collective-permute-start | bytes 1179656 | tf_op jit(solution)/shard_map/ppermute | solution.py:34
  156.1 7.0 %collective-permute-start.19 = (f32[24,32,128]{2,0,1:T(8,128)S(1)}, f32[24,32,128]{2,0,1:T(8,128)S(1)}, u32[]{:S(2)}, u32[]{:S(2)}) collective-permute-start(f32[24,32,128]{2,0,1:T(8,128)S(1)} %get-tuple-element.24), channel_id=1, source_target_pairs={{4,0},{8,4},{12,8},{16,12},{20,16},{24,20},{28,24},{32,28},{36,32}... | collective-permute-start | bytes 1179656 | tf_op jit(solution)/shard_map/ppermute | solution.py:34
  163.1 1.1 copy.15
  164.3 5.0 %collective-permute-done.18 = f32[24,32,128]{2,0,1:T(8,128)S(1)} collective-permute-done((f32[24,32,128]{2,0,1:T(8,128)S(1)}, f32[24,32,128]{2,0,1:T(8,128)S(1)}, u32[]{:S(2)}, u32[]{:S(2)}) %collective-permute-start.18) | collective-permute-done | bytes 393248 | tf_op jit(solution)/shard_map/ppermute | solution.py:34
  170.7 20.1 %psum.15 = f32[1,2,24,24]{3,2,1,0:T(8,128)} all-reduce(f32[1,2,24,24]{3,2,1,0:T(8,128)S(1)} %maximum_bitcast_fusion), channel_id=1, replica_groups=mesh['patch'=64,'quad'=4] {'quad'}, use_global_device_ids=true, to_apply=%region_3.4 | all-reduce | flops 1152 | bytes 9216 | tf_op jit(solution)/shard_map/psum | solution.py:105
  (34 shorter events, 2.1 us)
Async XLA Ops:
  1.4 23.3 %collective-permute-start = (f32[8,512]{1,0:T(8,128)S(1)}, f32[8,512]{1,0:T(8,128)S(1)}, u32[]{:S(2)}, u32[]{:S(2)}) collective-permute-start(f32[8,512]{1,0:T(8,128)S(1)} %get-tuple-element.41), channel_id=1, source_target_pairs={{0,1},{1,2},{2,3},{4,5},{5,6},{6,7},{8,9},{9,10},{10,11},{12,13},{... | collective-permute-start | bytes 49160 | tf_op jit(solution)/shard_map/ppermute | solution.py:25
  10.7 13.9 %copy-start.1 = (f32[1,32,512]{2,1,0:T(8,128)S(1)}, f32[1,32,512]{2,1,0:T(8,128)}, u32[]{:S(2)}) copy-start(f32[1,32,512]{2,1,0:T(8,128)} %param.3) | copy-start | bytes 196612
  10.8 13.9 %collective-permute-start.1 = (f32[8,512]{1,0:T(8,128)S(1)}, f32[8,512]{1,0:T(8,128)S(1)}, u32[]{:S(2)}, u32[]{:S(2)}) collective-permute-start(f32[8,512]{1,0:T(8,128)S(1)} %get-tuple-element.42), channel_id=1, source_target_pairs={{1,0},{2,1},{3,2},{5,4},{6,5},{7,6},{9,8},{10,9},{11,10},{13,12},{... | collective-permute-start | bytes 49160 | tf_op jit(solution)/shard_map/ppermute | solution.py:26
  15.2 9.9 %collective-permute-start.2 = (f32[24,1,512]{2,0,1:T(8,128)S(1)}, f32[24,1,512]{2,0,1:T(8,128)S(1)}, u32[]{:S(2)}, u32[]{:S(2)}) collective-permute-start(f32[24,1,512]{2,0,1:T(8,128)S(1)} %get-tuple-element.39), channel_id=1, source_target_pairs={{0,1},{1,2},{2,3},{4,5},{5,6},{6,7},{8,9},{9,10},{10,11},{12,13},{... | collective-permute-start | bytes 147464 | tf_op jit(solution)/shard_map/ppermute | solution.py:25
  22.7 9.3 %collective-permute-start.3 = (f32[24,1,512]{2,0,1:T(8,128)S(1)}, f32[24,1,512]{2,0,1:T(8,128)S(1)}, u32[]{:S(2)}, u32[]{:S(2)}) collective-permute-start(f32[24,1,512]{2,0,1:T(8,128)S(1)} %get-tuple-element.40), channel_id=1, source_target_pairs={{1,0},{2,1},{3,2},{5,4},{6,5},{7,6},{9,8},{10,9},{11,10},{13,12},{... | collective-permute-start | bytes 147464 | tf_op jit(solution)/shard_map/ppermute | solution.py:26
  33.1 4.3 %collective-permute-start.4 = (f32[24,1,512]{2,0,1:T(8,128)S(1)}, f32[24,1,512]{2,0,1:T(8,128)S(1)}, u32[]{:S(2)}, u32[]{:S(2)}) collective-permute-start(f32[24,1,512]{2,0,1:T(8,128)S(1)} %get-tuple-element.37), channel_id=1, source_target_pairs={{0,1},{1,2},{2,3},{4,5},{5,6},{6,7},{8,9},{9,10},{10,11},{12,13},{... | collective-permute-start | bytes 147464 | tf_op jit(solution)/shard_map/ppermute | solution.py:25
  35.0 9.3 %collective-permute-start.5 = (f32[24,1,512]{2,0,1:T(8,128)S(1)}, f32[24,1,512]{2,0,1:T(8,128)S(1)}, u32[]{:S(2)}, u32[]{:S(2)}) collective-permute-start(f32[24,1,512]{2,0,1:T(8,128)S(1)} %get-tuple-element.38), channel_id=1, source_target_pairs={{1,0},{2,1},{3,2},{5,4},{6,5},{7,6},{9,8},{10,9},{11,10},{13,12},{... | collective-permute-start | bytes 147464 | tf_op jit(solution)/shard_map/ppermute | solution.py:26
  46.3 4.3 %collective-permute-start.6 = (f32[24,1,512]{2,0,1:T(8,128)S(1)}, f32[24,1,512]{2,0,1:T(8,128)S(1)}, u32[]{:S(2)}, u32[]{:S(2)}) collective-permute-start(f32[24,1,512]{2,0,1:T(8,128)S(1)} %get-tuple-element.35), channel_id=1, source_target_pairs={{0,1},{1,2},{2,3},{4,5},{5,6},{6,7},{8,9},{9,10},{10,11},{12,13},{... | collective-permute-start | bytes 147464 | tf_op jit(solution)/shard_map/ppermute | solution.py:25
  48.3 9.3 %collective-permute-start.7 = (f32[24,1,512]{2,0,1:T(8,128)S(1)}, f32[24,1,512]{2,0,1:T(8,128)S(1)}, u32[]{:S(2)}, u32[]{:S(2)}) collective-permute-start(f32[24,1,512]{2,0,1:T(8,128)S(1)} %get-tuple-element.36), channel_id=1, source_target_pairs={{1,0},{2,1},{3,2},{5,4},{6,5},{7,6},{9,8},{10,9},{11,10},{13,12},{... | collective-permute-start | bytes 147464 | tf_op jit(solution)/shard_map/ppermute | solution.py:26
  59.1 4.3 %collective-permute-start.8 = (f32[24,1,512]{2,0,1:T(8,128)S(1)}, f32[24,1,512]{2,0,1:T(8,128)S(1)}, u32[]{:S(2)}, u32[]{:S(2)}) collective-permute-start(f32[24,1,512]{2,0,1:T(8,128)S(1)} %get-tuple-element.33), channel_id=1, source_target_pairs={{0,1},{1,2},{2,3},{4,5},{5,6},{6,7},{8,9},{9,10},{10,11},{12,13},{... | collective-permute-start | bytes 147464 | tf_op jit(solution)/shard_map/ppermute | solution.py:25
  61.0 9.3 %collective-permute-start.9 = (f32[24,1,512]{2,0,1:T(8,128)S(1)}, f32[24,1,512]{2,0,1:T(8,128)S(1)}, u32[]{:S(2)}, u32[]{:S(2)}) collective-permute-start(f32[24,1,512]{2,0,1:T(8,128)S(1)} %get-tuple-element.34), channel_id=1, source_target_pairs={{1,0},{2,1},{3,2},{5,4},{6,5},{7,6},{9,8},{10,9},{11,10},{13,12},{... | collective-permute-start | bytes 147464 | tf_op jit(solution)/shard_map/ppermute | solution.py:26
  71.9 4.3 %collective-permute-start.10 = (f32[24,1,512]{2,0,1:T(8,128)S(1)}, f32[24,1,512]{2,0,1:T(8,128)S(1)}, u32[]{:S(2)}, u32[]{:S(2)}) collective-permute-start(f32[24,1,512]{2,0,1:T(8,128)S(1)} %get-tuple-element.31), channel_id=1, source_target_pairs={{0,1},{1,2},{2,3},{4,5},{5,6},{6,7},{8,9},{9,10},{10,11},{12,13},{... | collective-permute-start | bytes 147464 | tf_op jit(solution)/shard_map/ppermute | solution.py:25
  73.8 9.3 %collective-permute-start.11 = (f32[24,1,512]{2,0,1:T(8,128)S(1)}, f32[24,1,512]{2,0,1:T(8,128)S(1)}, u32[]{:S(2)}, u32[]{:S(2)}) collective-permute-start(f32[24,1,512]{2,0,1:T(8,128)S(1)} %get-tuple-element.32), channel_id=1, source_target_pairs={{1,0},{2,1},{3,2},{5,4},{6,5},{7,6},{9,8},{10,9},{11,10},{13,12},{... | collective-permute-start | bytes 147464 | tf_op jit(solution)/shard_map/ppermute | solution.py:26
  84.6 4.3 %collective-permute-start.12 = (f32[24,1,512]{2,0,1:T(8,128)S(1)}, f32[24,1,512]{2,0,1:T(8,128)S(1)}, u32[]{:S(2)}, u32[]{:S(2)}) collective-permute-start(f32[24,1,512]{2,0,1:T(8,128)S(1)} %get-tuple-element.29), channel_id=1, source_target_pairs={{0,1},{1,2},{2,3},{4,5},{5,6},{6,7},{8,9},{9,10},{10,11},{12,13},{... | collective-permute-start | bytes 147464 | tf_op jit(solution)/shard_map/ppermute | solution.py:25
  86.6 9.3 %collective-permute-start.13 = (f32[24,1,512]{2,0,1:T(8,128)S(1)}, f32[24,1,512]{2,0,1:T(8,128)S(1)}, u32[]{:S(2)}, u32[]{:S(2)}) collective-permute-start(f32[24,1,512]{2,0,1:T(8,128)S(1)} %get-tuple-element.30), channel_id=1, source_target_pairs={{1,0},{2,1},{3,2},{5,4},{6,5},{7,6},{9,8},{10,9},{11,10},{13,12},{... | collective-permute-start | bytes 147464 | tf_op jit(solution)/shard_map/ppermute | solution.py:26
  97.4 4.3 %collective-permute-start.14 = (f32[24,1,512]{2,0,1:T(8,128)S(1)}, f32[24,1,512]{2,0,1:T(8,128)S(1)}, u32[]{:S(2)}, u32[]{:S(2)}) collective-permute-start(f32[24,1,512]{2,0,1:T(8,128)S(1)} %get-tuple-element.27), channel_id=1, source_target_pairs={{0,1},{1,2},{2,3},{4,5},{5,6},{6,7},{8,9},{9,10},{10,11},{12,13},{... | collective-permute-start | bytes 147464 | tf_op jit(solution)/shard_map/ppermute | solution.py:25
  99.3 9.3 %collective-permute-start.15 = (f32[24,1,512]{2,0,1:T(8,128)S(1)}, f32[24,1,512]{2,0,1:T(8,128)S(1)}, u32[]{:S(2)}, u32[]{:S(2)}) collective-permute-start(f32[24,1,512]{2,0,1:T(8,128)S(1)} %get-tuple-element.28), channel_id=1, source_target_pairs={{1,0},{2,1},{3,2},{5,4},{6,5},{7,6},{9,8},{10,9},{11,10},{13,12},{... | collective-permute-start | bytes 147464 | tf_op jit(solution)/shard_map/ppermute | solution.py:26
  108.7 12.8 %copy-start = (f32[1,24,32,512]{3,2,1,0:T(8,128)S(1)}, f32[1,24,32,512]{3,2,1,0:T(8,128)}, u32[]{:S(2)}) copy-start(f32[1,24,32,512]{3,2,1,0:T(8,128)} %param.2) | copy-start | bytes 4718596
  110.2 4.5 %collective-permute-start.16 = (f32[24,1,512]{2,0,1:T(8,128)S(1)}, f32[24,1,512]{2,0,1:T(8,128)S(1)}, u32[]{:S(2)}, u32[]{:S(2)}) collective-permute-start(f32[24,1,512]{2,0,1:T(8,128)S(1)} %get-tuple-element.25), channel_id=1, source_target_pairs={{0,1},{1,2},{2,3},{4,5},{5,6},{6,7},{8,9},{9,10},{10,11},{12,13},{... | collective-permute-start | bytes 147464 | tf_op jit(solution)/shard_map/ppermute | solution.py:25
  112.1 9.3 %collective-permute-start.17 = (f32[24,1,512]{2,0,1:T(8,128)S(1)}, f32[24,1,512]{2,0,1:T(8,128)S(1)}, u32[]{:S(2)}, u32[]{:S(2)}) collective-permute-start(f32[24,1,512]{2,0,1:T(8,128)S(1)} %get-tuple-element.26), channel_id=1, source_target_pairs={{1,0},{2,1},{3,2},{5,4},{6,5},{7,6},{9,8},{10,9},{11,10},{13,12},{... | collective-permute-start | bytes 147464 | tf_op jit(solution)/shard_map/ppermute | solution.py:26
  152.9 16.3 %collective-permute-start.18 = (f32[24,32,128]{2,0,1:T(8,128)S(1)}, f32[24,32,128]{2,0,1:T(8,128)S(1)}, u32[]{:S(2)}, u32[]{:S(2)}) collective-permute-start(f32[24,32,128]{2,0,1:T(8,128)S(1)} %get-tuple-element.23), channel_id=1, source_target_pairs={{0,4},{4,8},{8,12},{12,16},{16,20},{20,24},{24,28},{28,32},{32,36}... | collective-permute-start | bytes 1179656 | tf_op jit(solution)/shard_map/ppermute | solution.py:34
  156.1 14.0 %collective-permute-start.19 = (f32[24,32,128]{2,0,1:T(8,128)S(1)}, f32[24,32,128]{2,0,1:T(8,128)S(1)}, u32[]{:S(2)}, u32[]{:S(2)}) collective-permute-start(f32[24,32,128]{2,0,1:T(8,128)S(1)} %get-tuple-element.24), channel_id=1, source_target_pairs={{4,0},{8,4},{12,8},{16,12},{20,16},{24,20},{28,24},{32,28},{36,32}... | collective-permute-start | bytes 1179656 | tf_op jit(solution)/shard_map/ppermute | solution.py:34
where the time goes:
time: 193 us; the launch traced here: 191 us
  starting transfers between devices  61.4 us (32%)
  waiting for transfers between devices  60.5 us (31%)
  blocking collectives  37.3 us (19%)
  other arithmetic  22.6 us (12%)
  local copies, waits for them, and re-layouts  4.47 us (2%)
  matrix products  3.34 us (2%)
    ppermute x9, waiting for transfers between devices, padded_2(): after = lax.ppermute(leading, axis, down)  55.1 us
    ppermute x9, starting transfers between devices, padded_2(): before = lax.ppermute(last, axis, up)  30.4 us
    ppermute x9, starting transfers between devices, padded_2(): after = lax.ppermute(leading, axis, down)  21 us
    psum x1, blocking collectives, on_device(): coupling = lax.psum(jnp.stack((left_block, right_block)), 'quad')  20.1 us
    psum x1, blocking collectives, on_device(): gram = lax.psum(gram_matrix(iterate, band_cols, half_cols), 'quad')  17.2 us
    ppermute x2, starting transfers between devices, shifted(): return lax.ppermute(block, axis, route)  10.1 us
    add x6, other arithmetic, on_device(): rho_next * rho_now * direction + 2.0 * rho_next / half_width * residual  9.46 us
    add x1, other arithmetic, on_device(): iterate = iterate + direction  6.42 us
  transfers between devices with their start and end apart: 20, of which 10 were waited for; matrix products, arithmetic and copies ran while one was open for 2% of the time, Pallas kernels for 0%

commit v1 on v0

v1 whole, which is shorter than its diff:
```python
import functools
import math

import jax
import jax.numpy as jnp
from jax import lax
from jax.experimental import pallas as pl
from jax.experimental.pallas import tpu as pltpu
from jax.sharding import PartitionSpec as P

SWEEPS = 8

mass_term = 0.1
lower_bound = 0.05
upper_bound = 2.0
mid_value = 0.5 * (upper_bound + lower_bound)
half_width = 0.5 * (upper_bound - lower_bound)
highest = lax.Precision.HIGHEST

CENTRE = 2.0 * (mid_value - 1.0) / half_width
FACE = 2.0 / half_width

PARAMS = pltpu.CompilerParams(vmem_limit_bytes=40 * 1024 * 1024)


def dot_nt(a, b):
    return lax.dot_general(
        a, b, (((1,), (1,)), ((), ())), precision=highest, preferred_element_type=jnp.float32
    )


def dot_nn(a, b):
    return lax.dot_general(
        a, b, (((1,), (0,)), ((), ())), precision=highest, preferred_element_type=jnp.float32
    )


def shift_columns(x, towards_right):
    axis = x.ndim - 1
    return pltpu.roll(x, 1 if towards_right else x.shape[axis] - 1, axis)


def store_weights(log_row, weights, first, last, alive_of):
    width = weights.shape[-1]
    lane = lax.broadcasted_iota(jnp.int32, (8, width), 1)
    is_first, is_last = lane == 0, lane == width - 1

    def kappa(row):
        return jnp.exp(jnp.broadcast_to(log_row(row), (8, width)))

    def body(row, carry):
        before, centre = carry
        after = kappa(row + 1)
        left = jnp.where(is_first, 1.0, shift_columns(centre, True))
        right = jnp.where(is_last, 1.0, shift_columns(centre, False))
        upper_face = 0.5 * (centre + before)
        lower_face = 0.5 * (centre + after)
        left_face = 0.5 * (centre + left)
        right_face = 0.5 * (centre + right)
        diagonal = upper_face + lower_face + left_face + right_face + mass_term * centre
        scale = FACE * alive_of(row) / diagonal
        weights[row - first, 0] = upper_face * scale
        weights[row - first, 1] = lower_face * scale
        weights[row - first, 2] = jnp.where(is_first, 0.0, left_face * scale)
        weights[row - first, 3] = jnp.where(is_last, 0.0, right_face * scale)
        return centre, after

    lax.fori_loop(first, last + 1, body, (kappa(first - 1), kappa(first)))


def apply_row(now, row, weights, wrow):
    centre = now[row]
    return (
        CENTRE * centre
        + weights[wrow, 0] * now[row - 1]
        + weights[wrow, 1] * now[row + 1]
        + weights[wrow, 2] * shift_columns(centre, True)
        + weights[wrow, 3] * shift_columns(centre, False)
    )


def prepare_kernel(quad, vec, log_kappa, send_a, send_b, sems):
    odd = lax.rem(lax.axis_index(quad), 2)
    count, height, _ = vec.shape
    far = height - SWEEPS
    row_a = pl.multiple_of((1 - odd) * far, 8)
    row_b = pl.multiple_of(odd * far, 8)
    copies = []
    for k, (row, dst) in enumerate(((row_b, send_b), (row_a, send_a))):
        copies.append(
            pltpu.make_async_copy(
                vec.at[:, pl.ds(row, SWEEPS), :], dst.at[pl.ds(0, count)], sems.at[2 * k]
            )
        )
        copies.append(
            pltpu.make_async_copy(
                log_kappa.at[pl.ds(row, SWEEPS), :], dst.at[count], sems.at[2 * k + 1]
            )
        )
    for c in copies:
        c.start()
    for c in copies:
        c.wait()


def blocks_of(value):
    flat = value.reshape(-1, value.shape[-1])
    band = flat.shape[-1] // 4
    return [flat[:, k * band : (k + 1) * band] for k in range(4)]


def fetch_columns(source, slabs, sems):
    copies = []
    for k in range(slabs.shape[0]):
        copy = pltpu.make_async_copy(
            source.at[:, :, pl.ds(128 * k, 128)], slabs.at[k], sems.at[k]
        )
        copy.start()
        copies.append(copy)
    return copies


def field_rows(slabs, group, row):
    height = slabs.shape[2]
    parts = []
    for k in range(slabs.shape[0]):
        flat = slabs.at[k].reshape(slabs.shape[1] * height, 128)
        parts.append(flat[pl.ds(8 * height * group + row, 8, stride=height), :])
    return jnp.concatenate(parts, axis=1)


def field_row(slabs, field, row):
    return jnp.concatenate(
        [slabs[k, field, pl.ds(row, 1), :] for k in range(slabs.shape[0])], axis=1
    )


def inner_kernel(
    quad, vec, halo_a, log_kappa, o0, o1, o2, o3, rim, gram,
    even, odd_buf, weights, vec_slabs, halo_slabs, sems,
):
    odd = lax.rem(lax.axis_index(quad), 2)
    total = even.shape[0]
    groups = even.shape[1]
    height = total - SWEEPS
    count = 8 * groups

    def own_row(row):
        return jnp.where(odd == 1, height - 1 - row, row)

    def halo_row(k):
        return jnp.where(odd == 1, SWEEPS - 1 - k, k)

    copies = fetch_columns(vec, vec_slabs, sems.at[0])
    copies += fetch_columns(halo_a, halo_slabs, sems.at[1])
    for copy in copies:
        copy.wait()

    def load_own(row, carry):
        r = own_row(row)
        for g in range(groups):
            even[row, g] = field_rows(vec_slabs, g, r)
        return carry

    lax.fori_loop(0, height, load_own, 0)

    def load_halo(k, carry):
        r = halo_row(k)
        for g in range(groups):
            even[height + k, g] = field_rows(halo_slabs, g, r)
        return carry

    lax.fori_loop(0, SWEEPS, load_halo, 0)

    def log_row(row):
        inside = log_kappa[pl.ds(own_row(jnp.minimum(row, height - 1)), 1), :]
        outside = field_row(halo_slabs, count, halo_row(jnp.maximum(row - height, 0)))
        return jnp.where(row < height, inside, outside)

    has_a = 1.0
    store_weights(log_row, weights, 1, total - 2, lambda row: has_a)

    bufs = (even, odd_buf)
    for level in range(1, SWEEPS + 1):
        now, new = bufs[(level - 1) % 2], bufs[level % 2]
        rim[level - 1, 0] = now[level - 1]
        rim[level - 1, 1] = now[level]

        def body(row, carry):
            value = apply_row(now, row, weights, row - 1)
            if level == 1:
                new[row] = 0.5 * value
            else:
                new[row] = value - new[row]
            return carry

        lax.fori_loop(level, total - level, body, 0, unroll=2)

    final = bufs[SWEEPS % 2]

    def finish(row, acc):
        parts = blocks_of(final[row + SWEEPS])
        for out, part in zip((o0, o1, o2, o3), parts):
            out[row] = part
        sub = jnp.concatenate(parts[1:3], axis=1)
        return acc + dot_nt(sub, sub)

    gram[...] = lax.fori_loop(
        0, height - SWEEPS, finish, jnp.zeros((count, count), jnp.float32)
    )


def edge_kernel(
    quad, halo_b, log_kappa, rim, gram_inner, o0, o1, o2, o3, gram,
    even, odd_buf, weights, halo_slabs, sems,
):
    index = lax.axis_index(quad)
    odd = lax.rem(index, 2)
    size = lax.axis_size(quad)
    alive = jnp.where(jnp.logical_or(index == 0, index == size - 1), 0.0, 1.0)
    groups = even.shape[1]
    height = log_kappa.shape[0]
    count = 8 * groups

    def halo_row(row):
        return jnp.where(odd == 1, -1 - row, SWEEPS + row)

    for copy in fetch_columns(halo_b, halo_slabs, sems):
        copy.wait()

    def load_halo(k, carry):
        r = halo_row(k - SWEEPS)
        for g in range(groups):
            even[k, g] = field_rows(halo_slabs, g, r)
        return carry

    lax.fori_loop(0, SWEEPS, load_halo, 0)

    def log_row(row):
        own = jnp.maximum(row, 0)
        inside = log_kappa[pl.ds(jnp.where(odd == 1, height - 1 - own, own), 1), :]
        outside = field_row(halo_slabs, count, halo_row(jnp.minimum(row, -1)))
        return jnp.where(row >= 0, inside, outside)

    store_weights(
        log_row, weights, 1 - SWEEPS, SWEEPS - 1, lambda row: jnp.where(row < 0, alive, 1.0)
    )

    bufs = (even, odd_buf)
    for level in range(1, SWEEPS + 1):
        now, new = bufs[(level - 1) % 2], bufs[level % 2]
        now[level + SWEEPS - 1] = rim[level - 1, 0]
        now[level + SWEEPS] = rim[level - 1, 1]

        def body(row, carry):
            value = apply_row(now, row, weights, row - 1)
            if level == 1:
                new[row] = 0.5 * value
            else:
                new[row] = value - new[row]
            return carry

        lax.fori_loop(level, level + SWEEPS, body, 0, unroll=2)

    final = bufs[SWEEPS % 2]
    acc = gram_inner[...]
    for row in range(SWEEPS):
        parts = blocks_of(final[row + SWEEPS])
        for out, part in zip((o0, o1, o2, o3), parts):
            out[row] = part
        sub = jnp.concatenate(parts[1:3], axis=1)
        acc = acc + dot_nt(sub, sub)
    gram[:, : gram.shape[1]] = jnp.zeros(gram.shape, jnp.float32)
    gram[:, :count] = acc


def product_kernel(
    left_in, left_edge, right_in, right_edge, from_left, from_left_edge, from_right,
    from_right_edge, gram, gram_left, gram_right, out,
):
    count = out.shape[0]

    def products(inner, edge, theirs, theirs_edge):
        def pair(a, b, k):
            x = jnp.concatenate([a[2 * k], a[2 * k + 1]], axis=1)
            y = jnp.concatenate([b[2 * k], b[2 * k + 1]], axis=1)
            return dot_nt(x, y)

        acc = lax.fori_loop(
            0,
            inner.shape[0] // 2,
            lambda k, acc: acc + pair(inner, theirs, k),
            jnp.zeros((count, count), jnp.float32),
        )
        for k in range(edge.shape[0] // 2):
            acc = acc + pair(edge, theirs_edge, k)
        return acc

    left = products(left_in, left_edge, from_left, from_left_edge)
    right = products(right_in, right_edge, from_right, from_right_edge)
    out[...] = jnp.zeros(out.shape, jnp.float32)
    mats = (gram[:, :count], gram_left[:, :count], gram_right[:, :count], left, right)
    for k, mat in enumerate(mats):
        out[:, k * count : (k + 1) * count] = mat


def final_kernel(
    quad, patch, gathered, s1, s1_edge, s2, s2_edge, basis, coupling, slabs, sems
):
    odd = lax.rem(lax.axis_index(quad), 2)
    place = lax.axis_index(patch)
    last = lax.axis_size(patch) - 1
    inner_rows, count, band = s1.shape
    height = inner_rows + SWEEPS
    total = gathered[0]
    for k in range(1, gathered.shape[0]):
        total = total + gathered[k]
    lanes = total.shape[1]
    mats = [total[:, k * count : (k + 1) * count] for k in range(5)]
    eye = (
        lax.broadcasted_iota(jnp.int32, (count, count), 0)
        == lax.broadcasted_iota(jnp.int32, (count, count), 1)
    ).astype(jnp.float32)
    missing = (None, place == 0, place == last)
    sub = lax.broadcasted_iota(jnp.int32, (count, lanes), 0)
    lane = lax.broadcasted_iota(jnp.int32, (count, lanes), 1)
    inverses = []
    for k in range(3):
        mat = mats[k] if missing[k] is None else jnp.where(missing[k], eye, mats[k])
        work = jnp.concatenate(
            [mat, eye, jnp.zeros((count, lanes - 2 * count), jnp.float32)], axis=1
        )
        for j in range(count - 1):
            pivot = work[j : j + 1, :]
            column = work[:, j : j + 1]
            ratio = jnp.where(sub > j, column / work[j : j + 1, j : j + 1], 0.0)
            work = work - ratio * pivot
        diagonal = jnp.sum(jnp.where(sub == lane, work, 0.0), axis=1, keepdims=True)
        inverses.append((work / jnp.sqrt(diagonal))[:, count : 2 * count])
    own, left, right = inverses
    coupling[0] = dot_nt(dot_nn(own, mats[3]), left)
    coupling[1] = dot_nt(dot_nn(own, mats[4]), right)

    def write(first, row, a, b):
        place_row = first + row
        r = jnp.where(odd == 1, height - 1 - place_row, place_row)
        value = dot_nn(own, jnp.concatenate([a[row], b[row]], axis=1))
        for k in range(2):
            flat = slabs.at[k].reshape(count * height, 128)
            for g in range(count // 8):
                flat[pl.ds(8 * height * g + r, 8, stride=height), :] = value[
                    8 * g : 8 * g + 8, 128 * k : 128 * k + 128
                ]

    lax.fori_loop(0, SWEEPS, lambda row, c: (write(0, row, s1_edge, s2_edge), c)[1], 0)
    lax.fori_loop(0, inner_rows, lambda row, c: (write(SWEEPS, row, s1, s2), c)[1], 0)
    copies = [
        pltpu.make_async_copy(slabs.at[k], basis.at[:, :, pl.ds(128 * k, 128)], sems.at[k])
        for k in range(2)
    ]
    for copy in copies:
        copy.start()
    for copy in copies:
        copy.wait()


def on_device(vectors, log_kappa):
    vec = vectors[0]
    log_own = log_kappa[0]
    count, height, width = vec.shape
    band = width // 4
    groups = count // 8
    f32 = jnp.float32
    patch_size, quad_size = lax.axis_size("patch"), lax.axis_size("quad")

    def shape(*dims):
        return jax.ShapeDtypeStruct(dims, f32)

    any_space = pl.BlockSpec(memory_space=pl.ANY)
    vmem_space = pl.BlockSpec(memory_space=pltpu.VMEM)
    send_a, send_b = pl.pallas_call(
        functools.partial(prepare_kernel, "quad"),
        out_shape=(shape(count + 1, SWEEPS, width),) * 2,
        in_specs=[any_space, any_space],
        out_specs=(any_space, any_space),
        scratch_shapes=[pltpu.SemaphoreType.DMA((4,))],
    )(vec, log_own)
    same_chip = [(i, i ^ 1) for i in range(quad_size)]
    other_chip = [
        (i, j)
        for i in range(quad_size)
        for j in (i - 1, i + 1)
        if 0 <= j < quad_size and i // 2 != j // 2
    ]
    halo_a = lax.ppermute(send_a, "quad", same_chip)
    halo_b = lax.ppermute(send_b, "quad", other_chip)
    inner = height - SWEEPS
    total = height + SWEEPS
    cost = 12 * count * width * SWEEPS * height
    *inner_parts, rim, gram_inner = pl.pallas_call(
        functools.partial(inner_kernel, "quad"),
        out_shape=(shape(inner, count, band),) * 4
        + (shape(SWEEPS, 2, groups, 8, width), shape(count, count)),
        scratch_shapes=[
            pltpu.VMEM((total, groups, 8, width), f32),
            pltpu.VMEM((total, groups, 8, width), f32),
            pltpu.VMEM((total - 2, 4, 8, width), f32),
            pltpu.VMEM((4, count, height, 128), f32),
            pltpu.VMEM((4, count + 1, SWEEPS, 128), f32),
            pltpu.SemaphoreType.DMA((2, 4)),
        ],
        in_specs=[any_space, any_space, vmem_space],
        compiler_params=PARAMS,
        cost_estimate=pl.CostEstimate(flops=cost, bytes_accessed=5 << 20, transcendentals=0),
    )(vec, halo_a, log_own)
    from_right_in = shifted(inner_parts[1], "patch", -1)
    from_left_in = shifted(inner_parts[2], "patch", 1)
    *edge_parts, gram = pl.pallas_call(
        functools.partial(edge_kernel, "quad"),
        out_shape=(shape(SWEEPS, count, band),) * 4 + (shape(count, 128),),
        scratch_shapes=[
            pltpu.VMEM((2 * SWEEPS + 1, groups, 8, width), f32),
            pltpu.VMEM((2 * SWEEPS + 1, groups, 8, width), f32),
            pltpu.VMEM((2 * SWEEPS - 1, 4, 8, width), f32),
            pltpu.VMEM((4, count + 1, SWEEPS, 128), f32),
            pltpu.SemaphoreType.DMA((4,)),
        ],
        in_specs=[any_space] + [vmem_space] * 3,
        compiler_params=PARAMS,
    )(halo_b, log_own, rim, gram_inner)
    right_pack = jnp.concatenate([edge_parts[1], gram[None]], axis=0)
    left_pack = jnp.concatenate([edge_parts[2], gram[None]], axis=0)
    from_right_edge = shifted(right_pack, "patch", -1)
    from_left_edge = shifted(left_pack, "patch", 1)
    packed = pl.pallas_call(
        product_kernel,
        out_shape=shape(count, 128),
        compiler_params=PARAMS,
    )(
        inner_parts[0], edge_parts[0], inner_parts[3], edge_parts[3],
        from_left_in, from_left_edge[:SWEEPS], from_right_in, from_right_edge[:SWEEPS],
        gram, from_left_edge[SWEEPS], from_right_edge[SWEEPS],
    )
    gathered = lax.all_gather(packed, "quad")
    basis, coupling = pl.pallas_call(
        functools.partial(final_kernel, "quad", "patch"),
        out_shape=(shape(count, height, 2 * band), shape(2, count, count)),
        out_specs=(any_space, vmem_space),
        scratch_shapes=[
            pltpu.VMEM((2, count, height, 128), f32),
            pltpu.SemaphoreType.DMA((2,)),
        ],
        compiler_params=PARAMS,
    )(gathered, inner_parts[1], edge_parts[1], inner_parts[2], edge_parts[2])
    return basis[None], coupling[None]


def shifted(block, axis, distance):
    devices = range(lax.axis_size(axis))
    route = [(i - distance, i) for i in devices if i - distance in devices]
    return lax.ppermute(block, axis, route)


def solution(mesh):
    placed = (P("patch", None, "quad", None), P("patch", "quad", None))
    return jax.shard_map(
        on_device,
        mesh=mesh,
        in_specs=placed,
        out_specs=(P("patch", None, "quad", None), P("patch", None, None, None)),
        check_vma=False,
    )
```

time: 193 us -> 111 us (0.58)
  Pallas kernels: 0 us -> 70.5 us
  waiting for transfers between devices: 60.5 us -> 3.65 us
  starting transfers between devices: 61.4 us -> 27.4 us
  blocking collectives: 37.3 us -> 7.98 us
  other arithmetic: 22.6 us -> 0.02 us
  local copies, waits for them, and re-layouts: 4.47 us -> 0.03 us
  matrix products: 3.34 us -> 0 us
    pallas_call x0 -> x5, Pallas kernels: none -> 70.5 us  [the longest x1 26 us: on_device(): pl.pallas_call(functools.partial(prepare_kernel, 'quad'), out_shape=(shap...]
    ppermute x18 -> x2, waiting for transfers between devices: 55.1 us -> 0.01 us  [the longest x1 0.01 us: on_device(): halo_a = lax.ppermute(send_a, 'quad', same_chip)]
    ppermute x18 -> x2, starting transfers between devices: 51.3 us -> 9.48 us  [the longest x1 8.72 us: on_device(): halo_b = lax.ppermute(send_b, 'quad', other_chip)]
    psum x2 -> x0, blocking collectives: 37.3 us -> none  [the longest x1 20.1 us: on_device(): coupling = lax.psum(jnp.stack((left_block, right_block)), 'quad')]
    add x8 -> x0, other arithmetic: 16 us -> none  [the longest x6 9.46 us: on_device(): rho_next * rho_now * direction + 2.0 * rho_next / half_width * residual]
    all_gather x0 -> x1, blocking collectives: none -> 7.98 us  [on_device(): gathered = lax.all_gather(packed, 'quad')]
    ppermute x2 -> x4, starting transfers between devices: 10.1 us -> 17.9 us  [shifted(): return lax.ppermute(block, axis, route)]
    another operation x5 -> x0, other arithmetic: 5.34 us -> none  [the longest x3 2.86 us: on_device(): factor = jnp.linalg.cholesky(gram)]
  transfers between devices with their start and end apart: 20 -> 6, of which waited for: 10 -> 2; matrix products, arithmetic and copies ran while one was open for 2% -> 0% of each run, Pallas kernels for 0% -> 22%
where the time goes in v1:
time: 111 us; the launch traced here: 110 us
  Pallas kernels  70.5 us (64%)
  starting transfers between devices  27.4 us (25%)
  blocking collectives  7.98 us (7%)
  waiting for transfers between devices  3.65 us (3%)
    pallas_call x1, Pallas kernels, on_device(): pl.pallas_call(functools.partial(prepare_kernel, 'quad'), out_shape=(shap...  26 us
    pallas_call x1, Pallas kernels, on_device(): pl.pallas_call(functools.partial(inner_kernel, 'quad'), out_shape=(shape(...  24.8 us
    ppermute x4, starting transfers between devices, shifted(): return lax.ppermute(block, axis, route)  17.9 us
    pallas_call x1, Pallas kernels, on_device(): pl.pallas_call(functools.partial(final_kernel, 'quad', 'patch'), out_shap...  9.5 us
    ppermute x1, starting transfers between devices, on_device(): halo_b = lax.ppermute(send_b, 'quad', other_chip)  8.72 us
    all_gather x1, blocking collectives, on_device(): gathered = lax.all_gather(packed, 'quad')  7.98 us
    pallas_call x1, Pallas kernels, on_device(): pl.pallas_call(functools.partial(edge_kernel, 'quad'), out_shape=(shape(S...  5.98 us
    pallas_call x1, Pallas kernels, on_device(): pl.pallas_call(product_kernel, out_shape=shape(count, 128), compiler_para...  4.28 us
  transfers between devices with their start and end apart: 6, of which 2 were waited for; matrix products, arithmetic and copies ran while one was open for 0% of the time, Pallas kernels for 22%

profile of v1, /device:TPU:25, one launch (start us, length us, event | category | flops | bytes accessed | tf_op | source)
XLA Modules:
  0.0 110.4 jit_solution(8502097536397029744)
XLA Ops:
  0.6 0.0 copy-start.1
  0.6 0.0 copy-start
  0.6 26.0 %shard_map.41 = (f32[25,8,512]{2,1,0:T(8,128)}, f32[25,8,512]{2,1,0:T(8,128)}) custom-call(f32[24,32,512]{2,1,0:T(8,128)} %bitcast.10, f32[32,512]{1,0:T(8,128)} %bitcast.12), custom_call_target="tpu_custom_call" | custom-call | tf_op jit(solution)/shard_map/pallas_call | solution.py:381
  26.6 0.8 collective-permute-start
  27.4 8.7 %collective-permute-start.1 = (f32[25,8,512]{2,1,0:T(8,128)}, f32[25,8,512]{2,1,0:T(8,128)S(1)}, u32[]{:S(2)}, u32[]{:S(2)}) collective-permute-start(f32[25,8,512]{2,1,0:T(8,128)} %get-tuple-element.19), channel_id=1, source_target_pairs={{1,2},{2,1},{5,6},{6,5},{9,10},{10,9},{13,14},{14,13},{17,18},{18,... | collective-permute-start | bytes 1228808 | tf_op jit(solution)/shard_map/ppermute | solution.py:396
  36.1 0.0 collective-permute-done.halo_a
  36.1 0.0 copy-done.1
  36.1 0.0 copy-done
  36.1 24.8 %shard_map.42 = (f32[24,24,128]{2,1,0:T(8,128)S(1)}, f32[24,24,128]{2,1,0:T(8,128)S(1)}, f32[24,24,128]{2,1,0:T(8,128)S(1)}, f32[24,24,128]{2,1,0:T(8,128)S(1)},...) custom-call(f32[24,32,512]{2,1,0:T(8,128)S(1)} %bitcast.11, f32[25,8,512]{2,1,0:T(8,128)S(1)} %collective-permute-done.halo_a, ...), custom_call_target="tpu_custom_call" | custom-call | flops 37748736 | bytes 5242880 | tf_op jit(solution)/shard_map/pallas_call | solution.py:400
  61.0 0.0 collective-permute-done.1.halo_b
  61.0 6.0 %shard_map.43 = (f32[8,24,128]{2,1,0:T(8,128)S(1)}, f32[8,24,128]{2,1,0:T(8,128)S(1)}, f32[8,24,128]{2,1,0:T(8,128)S(1)}, f32[8,24,128]{2,1,0:T(8,128)S(1)}, f32[24,128]{1,0:T(8,128)S(1)}) custom-call(f32[25,8,512]{2,1,0:T(8,128)S(1)} %collective-permute-done.1.halo_b, f32[32,512]{1,0:T(8,128)S(1)} %bitcast.14, ...), custom_call_target="tpu_custom_call" | custom-call | tf_op jit(solution)/shard_map/pallas_call | solution.py:418
  67.0 5.9 %collective-permute-start.5 = (f32[9,24,128]{2,1,0:T(8,128)S(1)}, f32[9,24,128]{2,1,0:T(8,128)S(1)}, u32[]{:S(2)}, u32[]{:S(2)}) collective-permute-start(f32[9,24,128]{2,1,0:T(8,128)S(1)} %get-tuple-element.32), channel_id=1, source_target_pairs={{4,0},{8,4},{12,8},{16,12},{20,16},{24,20},{28,24},{32,28},{36,32}... | collective-permute-start | bytes 331784 | tf_op jit(solution)/shard_map/ppermute | solution.py:461
  72.9 1.9 %collective-permute-start.3 = (f32[9,24,128]{2,1,0:T(8,128)S(1)}, f32[9,24,128]{2,1,0:T(8,128)S(1)}, u32[]{:S(2)}, u32[]{:S(2)}) collective-permute-start(f32[9,24,128]{2,1,0:T(8,128)S(1)} %get-tuple-element.33), channel_id=1, source_target_pairs={{0,4},{4,8},{8,12},{12,16},{16,20},{20,24},{24,28},{28,32},{32,36}... | collective-permute-start | bytes 331784 | tf_op jit(solution)/shard_map/ppermute | solution.py:461
  74.8 1.9 %collective-permute-start.2 = (f32[24,24,128]{2,1,0:T(8,128)S(1)}, f32[24,24,128]{2,1,0:T(8,128)S(1)}, u32[]{:S(2)}, u32[]{:S(2)}) collective-permute-start(f32[24,24,128]{2,1,0:T(8,128)S(1)} %get-tuple-element.25.s2), channel_id=1, source_target_pairs={{0,4},{4,8},{8,12},{12,16},{16,20},{20,24},{24,28},{28,32},{32,36}... | collective-permute-start | bytes 884744 | tf_op jit(solution)/shard_map/ppermute | solution.py:461
  76.8 8.2 %collective-permute-start.4 = (f32[24,24,128]{2,1,0:T(8,128)S(1)}, f32[24,24,128]{2,1,0:T(8,128)S(1)}, u32[]{:S(2)}, u32[]{:S(2)}) collective-permute-start(f32[24,24,128]{2,1,0:T(8,128)S(1)} %get-tuple-element.28.s1), channel_id=1, source_target_pairs={{4,0},{8,4},{12,8},{16,12},{20,16},{24,20},{28,24},{32,28},{36,32}... | collective-permute-start | bytes 884744 | tf_op jit(solution)/shard_map/ppermute | solution.py:461
  85.0 0.0 collective-permute-done.5
  85.0 0.0 collective-permute-done.3
  85.0 3.1 %collective-permute-done.2.from_left = f32[24,24,128]{2,1,0:T(8,128)S(1)} collective-permute-done((f32[24,24,128]{2,1,0:T(8,128)S(1)}, f32[24,24,128]{2,1,0:T(8,128)S(1)}, u32[]{:S(2)}, u32[]{:S(2)}) %collective-permute-start.2) | collective-permute-done | bytes 294944 | tf_op jit(solution)/shard_map/ppermute | solution.py:461
  88.1 0.6 collective-permute-done.4.from_right
  88.7 4.3 %shard_map.44 = f32[24,128]{1,0:T(8,128)S(1)} custom-call(f32[24,24,128]{2,1,0:T(8,128)S(1)} %get-tuple-element.18.left_in, f32[8,24,128]{2,1,0:T(8,128)S(1)} %get-tuple-element.22.left_edge, f32[24,24,128]{2,1,0:T(8,128)S(1)} %get-tuple-element.23.right_in, f32[8,24,128]{2,1,0:T(8,128)S(1)} %get-tuple-element.24.right_edge, ...), custom_call_target="tpu_custom_call" | custom-call | tf_op jit(solution)/shard_map/pallas_call | solution.py:435
  92.9 8.0 %all-gather = f32[96,128]{1,0:T(8,128)S(1)} all-gather(f32[24,128]{1,0:T(8,128)S(1)} %shard_map.44), channel_id=2, replica_groups=mesh['patch'=64,'quad'=4] {'quad'}, dimensions={0}, use_global_device_ids=true | all-gather | bytes 61440 | tf_op jit(solution)/shard_map/all_gather | solution.py:444
  100.9 9.5 %shard_map.45 = (f32[24,32,256]{2,1,0:T(8,128)}, f32[2,24,24]{2,1,0:T(8,128)}) custom-call(f32[4,24,128]{2,1,0:T(8,128)S(1)} %bitcast.15, f32[24,24,128]{2,1,0:T(8,128)S(1)} %get-tuple-element.28.s1, f32[8,24,128]{2,1,0:T(8,128)S(1)} %get-tuple-element.29.s1_edge, f32[24,24,128]{2,1,0:T(8,128)S(1)} %get-tuple-element.25.s2, ...), custom_call_target="tpu_custom_call" | custom-call | tf_op jit(solution)/shard_map/pallas_call | solution.py:445
  (5 shorter events, 0.0 us)
Async XLA Ops:
  0.6 35.5 %copy-start.1 = (f32[1,32,512]{2,1,0:T(8,128)S(1)}, f32[1,32,512]{2,1,0:T(8,128)}, u32[]{:S(2)}) copy-start(f32[1,32,512]{2,1,0:T(8,128)} %param.3) | copy-start | bytes 196612
  0.6 35.5 %copy-start = (f32[1,24,32,512]{3,2,1,0:T(8,128)S(1)}, f32[1,24,32,512]{3,2,1,0:T(8,128)}, u32[]{:S(2)}) copy-start(f32[1,24,32,512]{3,2,1,0:T(8,128)} %param.2) | copy-start | bytes 4718596
  26.6 9.5 %collective-permute-start = (f32[25,8,512]{2,1,0:T(8,128)}, f32[25,8,512]{2,1,0:T(8,128)S(1)}, u32[]{:S(2)}, u32[]{:S(2)}) collective-permute-start(f32[25,8,512]{2,1,0:T(8,128)} %get-tuple-element.17), channel_id=1, source_target_pairs={{0,1},{1,0},{2,3},{3,2},{4,5},{5,4},{6,7},{7,6},{8,9},{9,8},{10,11... | collective-permute-start | bytes 1228808 | tf_op jit(solution)/shard_map/ppermute | solution.py:395
  27.4 33.6 %collective-permute-start.1 = (f32[25,8,512]{2,1,0:T(8,128)}, f32[25,8,512]{2,1,0:T(8,128)S(1)}, u32[]{:S(2)}, u32[]{:S(2)}) collective-permute-start(f32[25,8,512]{2,1,0:T(8,128)} %get-tuple-element.19), channel_id=1, source_target_pairs={{1,2},{2,1},{5,6},{6,5},{9,10},{10,9},{13,14},{14,13},{17,18},{18,... | collective-permute-start | bytes 1228808 | tf_op jit(solution)/shard_map/ppermute | solution.py:396
  67.0 18.0 %collective-permute-start.5 = (f32[9,24,128]{2,1,0:T(8,128)S(1)}, f32[9,24,128]{2,1,0:T(8,128)S(1)}, u32[]{:S(2)}, u32[]{:S(2)}) collective-permute-start(f32[9,24,128]{2,1,0:T(8,128)S(1)} %get-tuple-element.32), channel_id=1, source_target_pairs={{4,0},{8,4},{12,8},{16,12},{20,16},{24,20},{28,24},{32,28},{36,32}... | collective-permute-start | bytes 331784 | tf_op jit(solution)/shard_map/ppermute | solution.py:461
  72.9 12.1 %collective-permute-start.3 = (f32[9,24,128]{2,1,0:T(8,128)S(1)}, f32[9,24,128]{2,1,0:T(8,128)S(1)}, u32[]{:S(2)}, u32[]{:S(2)}) collective-permute-start(f32[9,24,128]{2,1,0:T(8,128)S(1)} %get-tuple-element.33), channel_id=1, source_target_pairs={{0,4},{4,8},{8,12},{12,16},{16,20},{20,24},{24,28},{28,32},{32,36}... | collective-permute-start | bytes 331784 | tf_op jit(solution)/shard_map/ppermute | solution.py:461
  74.8 13.2 %collective-permute-start.2 = (f32[24,24,128]{2,1,0:T(8,128)S(1)}, f32[24,24,128]{2,1,0:T(8,128)S(1)}, u32[]{:S(2)}, u32[]{:S(2)}) collective-permute-start(f32[24,24,128]{2,1,0:T(8,128)S(1)} %get-tuple-element.25.s2), channel_id=1, source_target_pairs={{0,4},{4,8},{8,12},{12,16},{16,20},{20,24},{24,28},{28,32},{32,36}... | collective-permute-start | bytes 884744 | tf_op jit(solution)/shard_map/ppermute | solution.py:461
  76.8 11.9 %collective-permute-start.4 = (f32[24,24,128]{2,1,0:T(8,128)S(1)}, f32[24,24,128]{2,1,0:T(8,128)S(1)}, u32[]{:S(2)}, u32[]{:S(2)}) collective-permute-start(f32[24,24,128]{2,1,0:T(8,128)S(1)} %get-tuple-element.28.s1), channel_id=1, source_target_pairs={{4,0},{8,4},{12,8},{16,12},{20,16},{24,20},{28,24},{32,28},{36,32}... | collective-permute-start | bytes 884744 | tf_op jit(solution)/shard_map/ppermute | solution.py:461

commit v2 on v0

v2 whole, which is shorter than its diff:
```python
import functools

import jax
import jax.numpy as jnp
from jax import lax
from jax.experimental import pallas as pl
from jax.experimental.pallas import tpu as pltpu
from jax.sharding import PartitionSpec as P

SWEEPS = 8

mass_term = 0.1
lower_bound = 0.05
upper_bound = 2.0
mid_value = 0.5 * (upper_bound + lower_bound)
half_width = 0.5 * (upper_bound - lower_bound)
highest = lax.Precision.HIGHEST
f32 = jnp.float32
bf16 = jnp.bfloat16

CENTRE = 2.0 * (mid_value - 1.0) / half_width
FACE = 2.0 / half_width

BLOCKS = 4
LANES = 128

PARAMS = pltpu.CompilerParams(vmem_limit_bytes=40 * 1024 * 1024)
ANY = pl.BlockSpec(memory_space=pl.ANY)
VMEM = pl.BlockSpec(memory_space=pltpu.VMEM)


def shape(*dims):
    return jax.ShapeDtypeStruct(dims, f32)


def dot_nt(a, b, precision=None):
    return lax.dot_general(
        a, b, (((1,), (1,)), ((), ())), precision=precision, preferred_element_type=f32
    )


def dot_nn(a, b, precision=None):
    return lax.dot_general(
        a, b, (((1,), (0,)), ((), ())), precision=precision, preferred_element_type=f32
    )


def three_parts(x):
    high = x.astype(bf16).astype(f32)
    rest = x - high
    middle = rest.astype(bf16).astype(f32)
    return jnp.concatenate([high, middle, rest - middle], axis=0).astype(bf16)


def two_parts(x):
    high = x.astype(bf16).astype(f32)
    return jnp.concatenate([high, x - high], axis=0).astype(bf16)


def gram_product(x, y):
    n, m = x.shape[0], y.shape[0]
    full = dot_nt(two_parts(x), two_parts(y))
    return (full[:n, :m] + full[n:, :m]) + (full[:n, m:] + full[n:, m:])


def permutation(width, inverse):
    row = lax.broadcasted_iota(jnp.int32, (width, width), 0)
    col = lax.broadcasted_iota(jnp.int32, (width, width), 1)
    if inverse:
        row, col = col, row
    target = (row % BLOCKS) * LANES + row // BLOCKS
    return jnp.where(target == col, 1.0, 0.0).astype(bf16)


def permute_columns(x, matrix):
    n = x.shape[0]
    out = dot_nn(three_parts(x), matrix)
    return (out[:n] + out[n : 2 * n]) + out[2 * n :]


def blocks_of(value):
    return [value[..., k * LANES : (k + 1) * LANES] for k in range(BLOCKS)]


def left_neighbour(x):
    b = blocks_of(x)
    axis = x.ndim - 1
    return jnp.concatenate([pltpu.roll(b[-1], 1, axis)] + b[:-1], axis=axis)


def right_neighbour(x):
    b = blocks_of(x)
    axis = x.ndim - 1
    return jnp.concatenate(b[1:] + [pltpu.roll(b[0], LANES - 1, axis)], axis=axis)


def face_weights(logs, alive):
    n, width = logs.shape
    kappa = jnp.exp(logs)
    rows = lax.slice_in_dim
    centre = rows(kappa, 8, n - 8, axis=0)
    before = rows(kappa, 7, n - 9, axis=0)
    after = rows(kappa, 9, n - 7, axis=0)
    lane = lax.broadcasted_iota(jnp.int32, centre.shape, 1)
    is_first, is_last = lane == 0, lane == width - 1
    left = jnp.where(is_first, 1.0, left_neighbour(centre))
    right = jnp.where(is_last, 1.0, right_neighbour(centre))
    upper_face = 0.5 * (centre + before)
    lower_face = 0.5 * (centre + after)
    left_face = 0.5 * (centre + left)
    right_face = 0.5 * (centre + right)
    diagonal = upper_face + lower_face + left_face + right_face + mass_term * centre
    scale = FACE * alive / diagonal
    return (
        upper_face * scale,
        lower_face * scale,
        jnp.where(is_first, 0.0, left_face * scale),
        jnp.where(is_last, 0.0, right_face * scale),
    )


def spread_weights(natural, weights, count, natural_row, odd):
    width = weights.shape[-1]

    def body(k, carry):
        r = natural_row(k)
        for i in range(4):
            source = jnp.where(odd == 1, 1 - i, i) if i < 2 else i
            weights[k, i] = jnp.broadcast_to(natural[source, pl.ds(r, 1), :], (8, width))
        return carry

    lax.fori_loop(0, count, body, 0, unroll=2)


def apply_row(now, row, weights, wrow):
    centre = now[row]
    return (
        CENTRE * centre
        + weights[wrow, 0] * now[row - 1]
        + weights[wrow, 1] * now[row + 1]
        + (weights[wrow, 2] * left_neighbour(centre) + weights[wrow, 3] * right_neighbour(centre))
    )


def sweep(level, now, new, weights, first, last, wfirst):
    def body(row, carry):
        value = apply_row(now, row, weights, row - wfirst)
        if level == 1:
            new[row] = 0.5 * value
        else:
            new[row] = value - new[row]
        return carry

    lax.fori_loop(first, last, body, 0, unroll=2)


def fetch_columns(source, slabs, sems):
    copies = []
    for k in range(slabs.shape[0]):
        copy = pltpu.make_async_copy(
            source.at[:, :, pl.ds(LANES * k, LANES)], slabs.at[k], sems.at[k]
        )
        copy.start()
        copies.append(copy)
    return copies


def rows_of_fields(slabs, rows, groups):
    height = slabs.shape[2]
    pieces = []
    for r in rows:
        for g in range(groups):
            parts = []
            for k in range(slabs.shape[0]):
                flat = slabs.at[k].reshape(slabs.shape[1] * height, LANES)
                parts.append(flat[pl.ds(8 * height * g + r, 8, stride=height), :])
            pieces.append(jnp.concatenate(parts, axis=1))
    return jnp.concatenate(pieces, axis=0)


def field_block(slabs, field):
    return jnp.concatenate([slabs[k, field] for k in range(slabs.shape[0])], axis=1)


def load_rows(slabs, target, first, natural_row, groups, matrix):
    rows = [natural_row(k) for k in range(8)]
    x = permute_columns(rows_of_fields(slabs, rows, groups), matrix)
    width = x.shape[1]
    target[pl.ds(first, 8)] = x.reshape(8, groups, 8, width)


def emit(final, first, count, groups, matrix, swap, outs, out_first):
    outer_left, outer_right, sub, send_right_pair, send_left_pair = outs
    width = final.shape[-1]
    x = final[pl.ds(first, 8)].reshape(8 * count, width)
    x = permute_columns(x, matrix).reshape(8, count, width)
    b = blocks_of(x)
    at = pl.ds(out_first, 8)
    outer_left[at] = b[0]
    outer_right[at] = b[3]
    sub[at] = jnp.concatenate(b[1:3], axis=2)
    send_right_pair[at] = jnp.where(swap, b[1], b[2])
    send_left_pair[at] = jnp.where(swap, b[2], b[1])


def rows_as_columns(ref, first, count):
    return jnp.concatenate([ref[first + k] for k in range(count)], axis=1)


def prepare_kernel(quad, vec, log_kappa, send_a, send_b, sems):
    odd = lax.rem(lax.axis_index(quad), 2)
    count, height, _ = vec.shape
    far = height - SWEEPS
    row_a = pl.multiple_of((1 - odd) * far, 8)
    row_b = pl.multiple_of(odd * far, 8)
    copies = []
    for k, (row, dst) in enumerate(((row_b, send_b), (row_a, send_a))):
        copies.append(
            pltpu.make_async_copy(
                vec.at[:, pl.ds(row, SWEEPS), :], dst.at[pl.ds(0, count)], sems.at[2 * k]
            )
        )
        copies.append(
            pltpu.make_async_copy(
                log_kappa.at[pl.ds(row, SWEEPS), :], dst.at[count], sems.at[2 * k + 1]
            )
        )
    for c in copies:
        c.start()
    for c in copies:
        c.wait()


def inner_kernel(
    quad, patch, vec, halo_a, log_kappa,
    outer_left, outer_right, sub, send_right, send_left, rim, gram,
    even, odd_buf, weights, vec_slabs, halo_slabs, logs, natural, sems,
):
    odd = lax.rem(lax.axis_index(quad), 2)
    swap = lax.rem(lax.axis_index(patch), 2) == 1
    total, groups = even.shape[:2]
    height = total - SWEEPS
    count = 8 * groups
    width = even.shape[-1]
    copies = fetch_columns(vec, vec_slabs, sems.at[0])
    copies += fetch_columns(halo_a, halo_slabs, sems.at[1])
    matrix = permutation(width, False)
    logs[...] = jnp.zeros(logs.shape, f32)
    logs[pl.ds(16, height)] = permute_columns(log_kappa[...], matrix)
    for copy in copies:
        copy.wait()
    below = pl.multiple_of(8 + (1 - odd) * (height + 8), 8)
    logs[pl.ds(below, 8)] = permute_columns(field_block(halo_slabs, count), matrix)
    values = face_weights(logs[...], 1.0)
    for i in range(4):
        natural[i] = values[i]

    def natural_row(k):
        return jnp.where(odd == 1, height + 7 - k, k + 8)

    def own_row(k):
        return jnp.where(odd == 1, height - 1 - k, k)

    def load(block, carry):
        first = pl.multiple_of(8 * block, 8)
        load_rows(vec_slabs, even, first, lambda k: own_row(first + k), groups, matrix)
        return carry

    lax.fori_loop(0, height // 8, load, 0)
    load_rows(
        halo_slabs, even, height, lambda k: jnp.where(odd == 1, 7 - k, k), groups, matrix
    )
    spread_weights(natural, weights, total - 2, lambda k: natural_row(k + 1), odd)

    bufs = (even, odd_buf)
    for level in range(1, SWEEPS + 1):
        now, new = bufs[(level - 1) % 2], bufs[level % 2]
        rim[level - 1, 0] = now[level - 1]
        rim[level - 1, 1] = now[level]
        sweep(level, now, new, weights, level, total - level, 1)

    final = bufs[SWEEPS % 2]
    back = permutation(width, True)
    outs = (outer_left, outer_right, sub, send_right, send_left)

    def finish(block, carry):
        row = pl.multiple_of(8 * block, 8)
        emit(final, row + 8, count, groups, back, swap, outs, row)
        return carry

    lax.fori_loop(0, (height - SWEEPS) // 8, finish, 0)
    x = rows_as_columns(sub, 0, height - SWEEPS)
    gram[...] = gram_product(x, x)


def edge_kernel(
    quad, patch, halo_b, log_kappa, rim, gram_inner, send_right_in, send_left_in,
    outer_left, outer_right, sub, send_right, send_left,
    even, odd_buf, weights, halo_slabs, logs, natural, sems,
):
    index = lax.axis_index(quad)
    odd = lax.rem(index, 2)
    swap = lax.rem(lax.axis_index(patch), 2) == 1
    size = lax.axis_size(quad)
    alive = jnp.where(jnp.logical_or(index == 0, index == size - 1), 0.0, 1.0)
    groups = even.shape[1]
    width = even.shape[-1]
    height = log_kappa.shape[0]
    count = 8 * groups
    copies = fetch_columns(halo_b, halo_slabs, sems)
    matrix = permutation(width, False)
    logs[...] = jnp.zeros(logs.shape, f32)
    own_at = pl.multiple_of(odd * (height - 16), 8)
    place = pl.multiple_of(16 - 8 * odd, 8)
    logs[pl.ds(place, 16)] = permute_columns(log_kappa[pl.ds(own_at, 16), :], matrix)
    for copy in copies:
        copy.wait()
    halo_at = pl.multiple_of(8 + 16 * odd, 8)
    logs[pl.ds(halo_at, 8)] = permute_columns(field_block(halo_slabs, count), matrix)
    position = lax.broadcasted_iota(jnp.int32, (24, width), 0)
    outside = jnp.logical_and(position >= 16 * odd, position < 8 + 16 * odd)
    values = face_weights(logs[...], jnp.where(outside, alive, 1.0))
    for i in range(4):
        natural[i] = values[i]

    load_rows(
        halo_slabs, even, 0, lambda k: jnp.where(odd == 1, 7 - k, k), groups, matrix
    )
    spread_weights(
        natural, weights, 15, lambda k: jnp.where(odd == 1, 22 - k, k + 1), odd
    )

    bufs = (even, odd_buf)
    for level in range(1, SWEEPS + 1):
        now, new = bufs[(level - 1) % 2], bufs[level % 2]
        now[level + SWEEPS - 1] = rim[level - 1, 0]
        now[level + SWEEPS] = rim[level - 1, 1]
        sweep(level, now, new, weights, level, level + SWEEPS, 1)

    final = bufs[SWEEPS % 2]
    back = permutation(width, True)
    emit(final, SWEEPS, count, groups, back, swap, (outer_left, outer_right, sub, send_right, send_left), 0)
    x = rows_as_columns(sub, 0, SWEEPS)
    total = gram_inner[...] + gram_product(x, x)
    inner = height - SWEEPS
    for out, source in ((send_right, send_right_in), (send_left, send_left_in)):
        out[pl.ds(SWEEPS, inner)] = source[...]
        out[height] = jnp.zeros((count, LANES), f32)
        out[height, :, :count] = total


def product_kernel(
    patch, left_in, left_edge, right_in, right_edge, from_right_pair, from_left_pair, sent, out
):
    swap = lax.rem(lax.axis_index(patch), 2) == 1
    count = out.shape[0]
    inner = left_in.shape[0]
    height = inner + SWEEPS

    def products(mine, mine_edge, theirs):
        x = jnp.concatenate(
            [rows_as_columns(mine_edge, 0, SWEEPS), rows_as_columns(mine, 0, inner)], axis=1
        )
        return gram_product(x, rows_as_columns(theirs, 0, height))

    out[...] = jnp.zeros(out.shape, f32)

    def write(from_left, from_right):
        mats = (
            sent[height, :, :count],
            from_left[height, :, :count],
            from_right[height, :, :count],
            products(left_in, left_edge, from_left),
            products(right_in, right_edge, from_right),
        )
        for k, mat in enumerate(mats):
            out[:, k * count : (k + 1) * count] = mat

    @pl.when(swap)
    def _():
        write(from_right_pair, from_left_pair)

    @pl.when(jnp.logical_not(swap))
    def _():
        write(from_left_pair, from_right_pair)


def inverse_factor(mat, eye, lanes):
    count = mat.shape[0]
    sub = lax.broadcasted_iota(jnp.int32, (count, lanes), 0)
    lane = lax.broadcasted_iota(jnp.int32, (count, lanes), 1)
    work = jnp.concatenate([mat, eye, jnp.zeros((count, lanes - 2 * count), f32)], axis=1)
    for j in range(count - 1):
        pivot = work[j : j + 1, :]
        column = work[:, j : j + 1]
        ratio = jnp.where(sub > j, column / work[j : j + 1, j : j + 1], 0.0)
        work = work - ratio * pivot
    diagonal = jnp.sum(jnp.where(sub == lane, work, 0.0), axis=1, keepdims=True)
    return (work / jnp.sqrt(diagonal))[:, count : 2 * count]


def final_kernel(quad, patch, gathered, sub_in, sub_edge, basis, coupling, slabs, sems):
    odd = lax.rem(lax.axis_index(quad), 2)
    place = lax.axis_index(patch)
    last = lax.axis_size(patch) - 1
    inner, count, sub_width = sub_in.shape
    height = inner + SWEEPS
    total = gathered[0]
    for k in range(1, gathered.shape[0]):
        total = total + gathered[k]
    lanes = total.shape[1]
    mats = [total[:, k * count : (k + 1) * count] for k in range(5)]
    eye = (
        lax.broadcasted_iota(jnp.int32, (count, count), 0)
        == lax.broadcasted_iota(jnp.int32, (count, count), 1)
    ).astype(f32)
    own = inverse_factor(mats[0], eye, lanes)
    left = inverse_factor(jnp.where(place == 0, eye, mats[1]), eye, lanes)
    right = inverse_factor(jnp.where(place == last, eye, mats[2]), eye, lanes)
    coupling[0] = dot_nt(dot_nn(own, mats[3], highest), left, highest)
    coupling[1] = dot_nt(dot_nn(own, mats[4], highest), right, highest)

    high = own.astype(bf16).astype(f32)
    low = own - high
    factor = jnp.concatenate([high, high, low, low], axis=1).astype(bf16)

    def write(source, row, place_row):
        r = jnp.where(odd == 1, height - 1 - place_row, place_row)
        x = source[row]
        x_high = x.astype(bf16).astype(f32)
        x_low = x - x_high
        value = dot_nn(
            factor, jnp.concatenate([x_high, x_low, x_high, x_low], axis=0).astype(bf16)
        )
        for k in range(sub_width // LANES):
            flat = slabs.at[k].reshape(count * height, LANES)
            for g in range(count // 8):
                flat[pl.ds(8 * height * g + r, 8, stride=height), :] = value[
                    8 * g : 8 * g + 8, LANES * k : LANES * (k + 1)
                ]

    lax.fori_loop(0, SWEEPS, lambda row, c: (write(sub_edge, row, row), c)[1], 0, unroll=4)
    lax.fori_loop(
        0, inner, lambda row, c: (write(sub_in, row, row + SWEEPS), c)[1], 0, unroll=4
    )
    copies = [
        pltpu.make_async_copy(
            slabs.at[k], basis.at[:, :, pl.ds(LANES * k, LANES)], sems.at[k]
        )
        for k in range(sub_width // LANES)
    ]
    for copy in copies:
        copy.start()
    for copy in copies:
        copy.wait()


def call_prepare(vec, log_own):
    count, _, width = vec.shape
    return pl.pallas_call(
        functools.partial(prepare_kernel, "quad"),
        out_shape=(shape(count + 1, SWEEPS, width),) * 2,
        in_specs=[ANY, ANY],
        out_specs=(VMEM, VMEM),
        scratch_shapes=[pltpu.SemaphoreType.DMA((4,))],
        compiler_params=PARAMS,
        name="prepare",
    )(vec, log_own)


def call_inner(vec, halo_a, log_own):
    count, height, width = vec.shape
    band, groups, inner, total = width // 4, count // 8, height - SWEEPS, height + SWEEPS
    cost = 12 * count * width * SWEEPS * height
    return pl.pallas_call(
        functools.partial(inner_kernel, "quad", "patch"),
        out_shape=(
            shape(inner, count, band),
            shape(inner, count, band),
            shape(inner, count, 2 * band),
            shape(inner, count, band),
            shape(inner, count, band),
            shape(SWEEPS, 2, groups, 8, width),
            shape(count, count),
        ),
        scratch_shapes=[
            pltpu.VMEM((total, groups, 8, width), f32),
            pltpu.VMEM((total, groups, 8, width), f32),
            pltpu.VMEM((total - 2, 4, 8, width), f32),
            pltpu.VMEM((width // LANES, count, height, LANES), f32),
            pltpu.VMEM((width // LANES, count + 1, SWEEPS, LANES), f32),
            pltpu.VMEM((height + 32, width), f32),
            pltpu.VMEM((4, height + 16, width), f32),
            pltpu.SemaphoreType.DMA((2, width // LANES)),
        ],
        in_specs=[ANY, ANY, VMEM],
        compiler_params=PARAMS,
        cost_estimate=pl.CostEstimate(flops=cost, bytes_accessed=5 << 20, transcendentals=0),
        name="inner",
    )(vec, halo_a, log_own)


def call_edge(halo_b, log_own, rim, gram_inner, send_right, send_left):
    height, width = log_own.shape
    inner, count, band = send_right.shape
    groups = count // 8
    return pl.pallas_call(
        functools.partial(edge_kernel, "quad", "patch"),
        out_shape=(
            shape(SWEEPS, count, band),
            shape(SWEEPS, count, band),
            shape(SWEEPS, count, 2 * band),
            shape(height + 1, count, band),
            shape(height + 1, count, band),
        ),
        scratch_shapes=[
            pltpu.VMEM((2 * SWEEPS + 1, groups, 8, width), f32),
            pltpu.VMEM((2 * SWEEPS + 1, groups, 8, width), f32),
            pltpu.VMEM((2 * SWEEPS - 1, 4, 8, width), f32),
            pltpu.VMEM((width // LANES, count + 1, SWEEPS, LANES), f32),
            pltpu.VMEM((40, width), f32),
            pltpu.VMEM((4, 24, width), f32),
            pltpu.SemaphoreType.DMA((width // LANES,)),
        ],
        in_specs=[ANY] + [VMEM] * 5,
        compiler_params=PARAMS,
        name="edge",
    )(halo_b, log_own, rim, gram_inner, send_right, send_left)


def call_product(left_in, left_edge, right_in, right_edge, from_right_pair, from_left_pair, sent):
    count = left_in.shape[1]
    return pl.pallas_call(
        functools.partial(product_kernel, "patch"),
        out_shape=shape(count, LANES),
        compiler_params=PARAMS,
        name="product",
    )(left_in, left_edge, right_in, right_edge, from_right_pair, from_left_pair, sent)


def call_final(gathered, sub_in, sub_edge):
    inner, count, sub_width = sub_in.shape
    height = inner + SWEEPS
    return pl.pallas_call(
        functools.partial(final_kernel, "quad", "patch"),
        out_shape=(shape(count, height, sub_width), shape(2, count, count)),
        out_specs=(ANY, VMEM),
        scratch_shapes=[
            pltpu.VMEM((sub_width // LANES, count, height, LANES), f32),
            pltpu.SemaphoreType.DMA((sub_width // LANES,)),
        ],
        compiler_params=PARAMS,
        name="final",
    )(gathered, sub_in, sub_edge)


def pairs(size, first):
    swaps = [(i, i + 1) for i in range(first, size - 1, 2)]
    return swaps + [(j, i) for i, j in swaps]


def on_device(vectors, log_kappa):
    vec, log_own = vectors[0], log_kappa[0]
    patch_size, quad_size = lax.axis_size("patch"), lax.axis_size("quad")
    send_a, send_b = call_prepare(vec, log_own)
    halo_a = lax.ppermute(send_a, "quad", pairs(quad_size, 0))
    halo_b = lax.ppermute(send_b, "quad", pairs(quad_size, 1))
    left_in, right_in, sub_in, send_1_in, send_2_in, rim, gram_in = call_inner(
        vec, halo_a, log_own
    )
    left_edge, right_edge, sub_edge, send_1, send_2 = call_edge(
        halo_b, log_own, rim, gram_in, send_1_in, send_2_in
    )
    from_2 = lax.ppermute(send_2, "patch", pairs(patch_size, 1))
    from_1 = lax.ppermute(send_1, "patch", pairs(patch_size, 0))
    packed = call_product(left_in, left_edge, right_in, right_edge, from_1, from_2, send_1)
    gathered = lax.all_gather(packed, "quad")
    basis, coupling = call_final(gathered, sub_in, sub_edge)
    return basis[None], coupling[None]


def solution(mesh):
    placed = (P("patch", None, "quad", None), P("patch", "quad", None))
    return jax.shard_map(
        on_device,
        mesh=mesh,
        in_specs=placed,
        out_specs=(P("patch", None, "quad", None), P("patch", None, None, None)),
        check_vma=False,
    )
```

time: 193 us -> 62.9 us (0.33); the launches traced: 191 us -> 62.7 us
  waiting for transfers between devices: 60.5 us -> 7.52 us
  starting transfers between devices: 61.4 us -> 15.5 us
  blocking collectives: 37.3 us -> 7.98 us
  Pallas kernels: 0 us -> 28.7 us
  other arithmetic: 22.6 us -> 0 us
  matrix products: 3.34 us -> 0 us
  local copies, waits for them, and re-layouts: 4.47 us -> 2.24 us
    ppermute x20 -> x4, waiting for transfers between devices: 60.5 us -> 7.52 us  [the longest x1 7.42 us: on_device(): from_2 = lax.ppermute(send_2, 'patch', pairs(patch_size, 1))]
    ppermute x20 -> x4, starting transfers between devices: 61.4 us -> 15.5 us  [the longest x1 8.72 us: on_device(): halo_b = lax.ppermute(send_b, 'quad', pairs(quad_size, 1))]
    psum x2 -> x0, blocking collectives: 37.3 us -> none  [the longest x1 20.1 us: on_device(): coupling = lax.psum(jnp.stack((left_block, right_block)), 'quad')]
    pallas_call x0 -> x5, Pallas kernels: none -> 28.7 us  [the longest x1 17.5 us: call_inner(): pl.pallas_call(functools.partial(inner_kernel, 'quad', 'patch'), out_shap...]
    add x8 -> x0, other arithmetic: 16 us -> none  [the longest x6 9.46 us: on_device(): rho_next * rho_now * direction + 2.0 * rho_next / half_width * residual]
    all_gather x0 -> x1, blocking collectives: none -> 7.98 us  [on_device(): gathered = lax.all_gather(packed, 'quad')]
    another operation x5 -> x0, other arithmetic: 5.34 us -> none  [the longest x3 2.86 us: on_device(): factor = jnp.linalg.cholesky(gram)]
  transfers between devices with their start and end apart: 20 -> 4, of which waited for: 10 -> 2; matrix products, arithmetic and copies ran while one was open for 2% -> 0% of each run, Pallas kernels for 0% -> 28%
where the time goes in v2:
time: 62.9 us; the launch traced here: 62.7 us
  Pallas kernels  28.7 us (46%)
  starting transfers between devices  15.5 us (25%)
  blocking collectives  7.98 us (13%)
  waiting for transfers between devices  7.52 us (12%)
  local copies, waits for them, and re-layouts  2.24 us (4%)
  between operations  0.71 us (1%)
    pallas_call x1, Pallas kernels, call_inner(): pl.pallas_call(functools.partial(inner_kernel, 'quad', 'patch'), out_shap...  17.5 us
    ppermute x1, starting transfers between devices, on_device(): halo_b = lax.ppermute(send_b, 'quad', pairs(quad_size, 1))  8.72 us
    all_gather x1, blocking collectives, on_device(): gathered = lax.all_gather(packed, 'quad')  7.98 us
    ppermute x1, waiting for transfers between devices, on_device(): from_2 = lax.ppermute(send_2, 'patch', pairs(patch_size, 1))  7.42 us
    ppermute x1, starting transfers between devices, on_device(): from_2 = lax.ppermute(send_2, 'patch', pairs(patch_size, 1))  5.93 us
    pallas_call x1, Pallas kernels, call_final(): pl.pallas_call(functools.partial(final_kernel, 'quad', 'patch'), out_shap...  5.9 us
    pallas_call x1, Pallas kernels, call_edge(): pl.pallas_call(functools.partial(edge_kernel, 'quad', 'patch'), out_shape...  4.72 us
    unnamed x6, local copies, waits for them, and re-layouts  2.24 us
  transfers between devices with their start and end apart: 4, of which 2 were waited for; matrix products, arithmetic and copies ran while one was open for 0% of the time, Pallas kernels for 28%

profile of v2, /device:TPU:25, one launch (start us, length us, event | category | flops | bytes accessed | tf_op | source)
XLA Modules:
  0.0 62.7 jit_solution(3158141195219748738)
XLA Ops:
  0.6 0.0 copy-start
  0.6 1.4 %copy-done = f32[1,24,32,512]{3,2,1,0:T(8,128)S(1)} copy-done((f32[1,24,32,512]{3,2,1,0:T(8,128)S(1)}, f32[1,24,32,512]{3,2,1,0:T(8,128)}, u32[]{:S(2)}) %copy-start) | copy-done | bytes 1572888
  2.0 0.0 copy-start.1
  2.0 0.8 %copy-done.1 = f32[1,32,512]{2,1,0:T(8,128)S(1)} copy-done((f32[1,32,512]{2,1,0:T(8,128)S(1)}, f32[1,32,512]{2,1,0:T(8,128)}, u32[]{:S(2)}) %copy-start.1) | copy-done | bytes 65560
  2.9 0.0 copy-start.2
  2.9 0.1 prepare.1
  3.0 0.8 %collective-permute-start = (f32[25,8,512]{2,1,0:T(8,128)S(1)}, f32[25,8,512]{2,1,0:T(8,128)S(1)}, u32[]{:S(2)}, u32[]{:S(2)}) collective-permute-start(f32[25,8,512]{2,1,0:T(8,128)S(1)} %get-tuple-element.18), channel_id=1, source_target_pairs={{0,1},{2,3},{1,0},{3,2},{4,5},{6,7},{5,4},{7,6},{8,9},{10,11},{9,8... | collective-permute-start | bytes 1228808 | tf_op jit(solution)/shard_map/ppermute | solution.py:566
  3.8 8.7 %collective-permute-start.1 = (f32[25,8,512]{2,1,0:T(8,128)S(1)}, f32[25,8,512]{2,1,0:T(8,128)S(1)}, u32[]{:S(2)}, u32[]{:S(2)}) collective-permute-start(f32[25,8,512]{2,1,0:T(8,128)S(1)} %get-tuple-element.20), channel_id=1, source_target_pairs={{1,2},{2,1},{5,6},{6,5},{9,10},{10,9},{13,14},{14,13},{17,18},{18,... | collective-permute-start | bytes 1228808 | tf_op jit(solution)/shard_map/ppermute | solution.py:567
  12.5 0.0 collective-permute-done.halo_a
  12.5 17.5 %inner.1 = (f32[24,24,128]{2,1,0:T(8,128)S(1)}, f32[24,24,128]{2,1,0:T(8,128)S(1)}, f32[24,24,256]{2,1,0:T(8,128)S(1)}, f32[24,24,128]{2,1,0:T(8,128)S(1)}, f32[...) custom-call(f32[24,32,512]{2,1,0:T(8,128)S(1)} %bitcast.6, ...), custom_call_target="tpu_custom_call" | custom-call | flops 37748736 | bytes 5242880 | tf_op jit(solution)/shard_map/inner/pallas_call | solution.py:475
  30.0 0.0 collective-permute-done.1.halo_b
  30.0 0.0 copy-done.2
  30.0 4.7 %edge.1 = (f32[8,24,128]{2,1,0:T(8,128)S(1)}, f32[8,24,128]{2,1,0:T(8,128)S(1)}, f32[8,24,256]{2,1,0:T(8,128)S(1)}, f32[33,24,128]{2,1,0:T(8,128)S(1)}, f32[33,24,128]{2,1,0:T(8,128)S(1)}) custom-call(f32[25,8,512]{2,1,0:T(8,128)S(1)} %collective-permute-done.1.halo_b, f32[32,512]{1,0:T(8,128)S(1)} %bitcast.9, ...), custom_call_target="tpu_custom_call" | custom-call | tf_op jit(solution)/shard_map/edge/pallas_call | solution.py:507
  34.8 5.9 %collective-permute-start.3 = (f32[33,24,128]{2,1,0:T(8,128)S(1)}, f32[33,24,128]{2,1,0:T(8,128)S(1)}, u32[]{:S(2)}, u32[]{:S(2)}) collective-permute-start(f32[33,24,128]{2,1,0:T(8,128)S(1)} %get-tuple-element.29), channel_id=1, source_target_pairs={{4,8},{12,16},{20,24},{28,32},{36,40},{44,48},{52,56},{60,64},{68,... | collective-permute-start | bytes 1216520 | tf_op jit(solution)/shard_map/ppermute | solution.py:574
  40.7 0.1 collective-permute-start.2
  40.8 7.4 %collective-permute-done.3.from_left_pair = f32[33,24,128]{2,1,0:T(8,128)S(1)} collective-permute-done((f32[33,24,128]{2,1,0:T(8,128)S(1)}, f32[33,24,128]{2,1,0:T(8,128)S(1)}, u32[]{:S(2)}, u32[]{:S(2)}) %collective-permute-start.3) | collective-permute-done | bytes 405536 | tf_op jit(solution)/shard_map/ppermute | solution.py:574
  48.2 0.1 collective-permute-done.2.from_right_pair
  48.3 0.5 product.1
  48.8 8.0 %all-gather = f32[96,128]{1,0:T(8,128)S(1)} all-gather(f32[24,128]{1,0:T(8,128)S(1)} %product.1), channel_id=2, replica_groups=mesh['patch'=64,'quad'=4] {'quad'}, dimensions={0}, use_global_device_ids=true | all-gather | bytes 61440 | tf_op jit(solution)/shard_map/all_gather | solution.py:577
  56.8 5.9 %final.1 = (f32[24,32,256]{2,1,0:T(8,128)}, f32[2,24,24]{2,1,0:T(8,128)}) custom-call(f32[4,24,128]{2,1,0:T(8,128)S(1)} %bitcast.10, f32[24,24,256]{2,1,0:T(8,128)S(1)} %get-tuple-element.30.sub_in, f32[8,24,256]{2,1,0:T(8,128)S(1)} %get-tuple-element.31.sub_edge), custom_call_target="tpu_custom_call" | custom-call | tf_op jit(solution)/shard_map/final/pallas_call | solution.py:544
Async XLA Ops:
  0.6 1.4 %copy-start = (f32[1,24,32,512]{3,2,1,0:T(8,128)S(1)}, f32[1,24,32,512]{3,2,1,0:T(8,128)}, u32[]{:S(2)}) copy-start(f32[1,24,32,512]{3,2,1,0:T(8,128)} %param.2) | copy-start | bytes 4718596
  2.0 0.8 %copy-start.1 = (f32[1,32,512]{2,1,0:T(8,128)S(1)}, f32[1,32,512]{2,1,0:T(8,128)}, u32[]{:S(2)}) copy-start(f32[1,32,512]{2,1,0:T(8,128)} %param.3) | copy-start | bytes 196612
  2.9 27.2 %copy-start.2 = (f32[1,32,512]{2,1,0:T(8,128)S(1)}, f32[1,32,512]{2,1,0:T(8,128)}, u32[]{:S(2)}) copy-start(f32[1,32,512]{2,1,0:T(8,128)} %param.3) | copy-start | bytes 196612
  3.0 9.5 %collective-permute-start = (f32[25,8,512]{2,1,0:T(8,128)S(1)}, f32[25,8,512]{2,1,0:T(8,128)S(1)}, u32[]{:S(2)}, u32[]{:S(2)}) collective-permute-start(f32[25,8,512]{2,1,0:T(8,128)S(1)} %get-tuple-element.18), channel_id=1, source_target_pairs={{0,1},{2,3},{1,0},{3,2},{4,5},{6,7},{5,4},{7,6},{8,9},{10,11},{9,8... | collective-permute-start | bytes 1228808 | tf_op jit(solution)/shard_map/ppermute | solution.py:566
  3.8 26.2 %collective-permute-start.1 = (f32[25,8,512]{2,1,0:T(8,128)S(1)}, f32[25,8,512]{2,1,0:T(8,128)S(1)}, u32[]{:S(2)}, u32[]{:S(2)}) collective-permute-start(f32[25,8,512]{2,1,0:T(8,128)S(1)} %get-tuple-element.20), channel_id=1, source_target_pairs={{1,2},{2,1},{5,6},{6,5},{9,10},{10,9},{13,14},{14,13},{17,18},{18,... | collective-permute-start | bytes 1228808 | tf_op jit(solution)/shard_map/ppermute | solution.py:567
  34.8 13.5 %collective-permute-start.3 = (f32[33,24,128]{2,1,0:T(8,128)S(1)}, f32[33,24,128]{2,1,0:T(8,128)S(1)}, u32[]{:S(2)}, u32[]{:S(2)}) collective-permute-start(f32[33,24,128]{2,1,0:T(8,128)S(1)} %get-tuple-element.29), channel_id=1, source_target_pairs={{4,8},{12,16},{20,24},{28,32},{36,40},{44,48},{52,56},{60,64},{68,... | collective-permute-start | bytes 1216520 | tf_op jit(solution)/shard_map/ppermute | solution.py:574
  40.7 7.6 %collective-permute-start.2 = (f32[33,24,128]{2,1,0:T(8,128)S(1)}, f32[33,24,128]{2,1,0:T(8,128)S(1)}, u32[]{:S(2)}, u32[]{:S(2)}) collective-permute-start(f32[33,24,128]{2,1,0:T(8,128)S(1)} %get-tuple-element.28.sent), channel_id=1, source_target_pairs={{0,4},{8,12},{16,20},{24,28},{32,36},{40,44},{48,52},{56,60},{64,6... | collective-permute-start | bytes 1216520 | tf_op jit(solution)/shard_map/ppermute | solution.py:575

commit v3 on v2

--- a/solution.py
+++ b/solution.py
@@ -23,6 +23,8 @@
 
 BLOCKS = 4
 LANES = 128
+CHUNK = 8
+PAD = 8
 
 PARAMS = pltpu.CompilerParams(vmem_limit_bytes=40 * 1024 * 1024)
 ANY = pl.BlockSpec(memory_space=pl.ANY)
@@ -43,13 +45,6 @@
     return lax.dot_general(
         a, b, (((1,), (0,)), ((), ())), precision=precision, preferred_element_type=f32
     )
-
-
-def three_parts(x):
-    high = x.astype(bf16).astype(f32)
-    rest = x - high
-    middle = rest.astype(bf16).astype(f32)
-    return jnp.concatenate([high, middle, rest - middle], axis=0).astype(bf16)
 
 
 def two_parts(x):
@@ -74,8 +69,8 @@
 
 def permute_columns(x, matrix):
     n = x.shape[0]
-    out = dot_nn(three_parts(x), matrix)
-    return (out[:n] + out[n : 2 * n]) + out[2 * n :]
+    out = dot_nn(two_parts(x), matrix)
+    return out[:n] + out[n:]
 
 
 def blocks_of(value):
@@ -142,27 +137,49 @@
     )
 
 
+def row_loop(first, last, chunk, body):
+    whole = (last - first) // chunk
+
+    def step(k, carry):
+        for i in range(chunk):
+            body(first + chunk * k + i)
+        return carry
+
+    if whole > 1:
+        lax.fori_loop(0, whole, step, 0)
+    elif whole == 1:
+        step(0, 0)
+    for row in range(first + whole * chunk, last):
+        body(row)
+
+
 def sweep(level, now, new, weights, first, last, wfirst):
-    def body(row, carry):
+    def body(row):
         value = apply_row(now, row, weights, row - wfirst)
         if level == 1:
             new[row] = 0.5 * value
         else:
             new[row] = value - new[row]
-        return carry
-
-    lax.fori_loop(first, last, body, 0, unroll=2)
-
-
-def fetch_columns(source, slabs, sems):
+
+    row_loop(first, last, CHUNK, body)
+
+
+def fetch_columns(source, slabs, sems, rows=0):
     copies = []
     for k in range(slabs.shape[0]):
         copy = pltpu.make_async_copy(
-            source.at[:, :, pl.ds(LANES * k, LANES)], slabs.at[k], sems.at[k]
+            source.at[:, pl.ds(rows, 8), pl.ds(LANES * k, LANES)],
+            slabs.at[k, :, pl.ds(rows, 8)],
+            sems.at[k],
         )
         copy.start()
         copies.append(copy)
     return copies
+
+
+def wait_all(copies):
+    for copy in copies:
+        copy.wait()
 
 
 def rows_of_fields(slabs, rows, groups):
@@ -242,13 +259,20 @@
     height = total - SWEEPS
     count = 8 * groups
     width = even.shape[-1]
-    copies = fetch_columns(vec, vec_slabs, sems.at[0])
-    copies += fetch_columns(halo_a, halo_slabs, sems.at[1])
+
+    def own_block(b):
+        return jnp.where(odd == 1, height // 8 - 1 - b, b)
+
+    blocks = height // 8
+    halo_copies = fetch_columns(halo_a, halo_slabs, sems.at[blocks])
+    block_copies = [
+        fetch_columns(vec, vec_slabs, sems.at[b], pl.multiple_of(own_block(b) * 8, 8))
+        for b in range(blocks)
+    ]
     matrix = permutation(width, False)
     logs[...] = jnp.zeros(logs.shape, f32)
     logs[pl.ds(16, height)] = permute_columns(log_kappa[...], matrix)
-    for copy in copies:
-        copy.wait()
+    wait_all(halo_copies)
     below = pl.multiple_of(8 + (1 - odd) * (height + 8), 8)
     logs[pl.ds(below, 8)] = permute_columns(field_block(halo_slabs, count), matrix)
     values = face_weights(logs[...], 1.0)
@@ -261,15 +285,14 @@
     def own_row(k):
         return jnp.where(odd == 1, height - 1 - k, k)
 
-    def load(block, carry):
-        first = pl.multiple_of(8 * block, 8)
-        load_rows(vec_slabs, even, first, lambda k: own_row(first + k), groups, matrix)
-        return carry
-
-    lax.fori_loop(0, height // 8, load, 0)
     load_rows(
         halo_slabs, even, height, lambda k: jnp.where(odd == 1, 7 - k, k), groups, matrix
     )
+    for block in range(blocks):
+        wait_all(block_copies[block])
+        load_rows(
+            vec_slabs, even, 8 * block, lambda k: own_row(8 * block + k), groups, matrix
+        )
     spread_weights(natural, weights, total - 2, lambda k: natural_row(k + 1), odd)
 
     bufs = (even, odd_buf)
@@ -288,7 +311,7 @@
         emit(final, row + 8, count, groups, back, swap, outs, row)
         return carry
 
-    lax.fori_loop(0, (height - SWEEPS) // 8, finish, 0)
+    lax.fori_loop(0, (height - SWEEPS) // 8, finish, 0, unroll=True)
     x = rows_as_columns(sub, 0, height - SWEEPS)
     gram[...] = gram_product(x, x)
 
@@ -307,14 +330,13 @@
     width = even.shape[-1]
     height = log_kappa.shape[0]
     count = 8 * groups
-    copies = fetch_columns(halo_b, halo_slabs, sems)
+    halo_copies = fetch_columns(halo_b, halo_slabs, sems)
     matrix = permutation(width, False)
     logs[...] = jnp.zeros(logs.shape, f32)
     own_at = pl.multiple_of(odd * (height - 16), 8)
     place = pl.multiple_of(16 - 8 * odd, 8)
     logs[pl.ds(place, 16)] = permute_columns(log_kappa[pl.ds(own_at, 16), :], matrix)
-    for copy in copies:
-        copy.wait()
+    wait_all(halo_copies)
     halo_at = pl.multiple_of(8 + 16 * odd, 8)
     logs[pl.ds(halo_at, 8)] = permute_columns(field_block(halo_slabs, count), matrix)
     position = lax.broadcasted_iota(jnp.int32, (24, width), 0)
@@ -385,18 +407,30 @@
         write(from_left_pair, from_right_pair)
 
 
-def inverse_factor(mat, eye, lanes):
-    count = mat.shape[0]
+def inverse_factors(mats, eye, lanes):
+    count = eye.shape[0]
     sub = lax.broadcasted_iota(jnp.int32, (count, lanes), 0)
     lane = lax.broadcasted_iota(jnp.int32, (count, lanes), 1)
-    work = jnp.concatenate([mat, eye, jnp.zeros((count, lanes - 2 * count), f32)], axis=1)
-    for j in range(count - 1):
-        pivot = work[j : j + 1, :]
-        column = work[:, j : j + 1]
-        ratio = jnp.where(sub > j, column / work[j : j + 1, j : j + 1], 0.0)
-        work = work - ratio * pivot
-    diagonal = jnp.sum(jnp.where(sub == lane, work, 0.0), axis=1, keepdims=True)
-    return (work / jnp.sqrt(diagonal))[:, count : 2 * count]
+    zeros = jnp.zeros((count, lanes - 2 * count), f32)
+    works = [jnp.concatenate([mat, eye, zeros], axis=1) for mat in mats]
+    for j in range(0, count, 2):
+        for m, work in enumerate(works):
+            first = jnp.broadcast_to(work[:, j : j + 1], (count, lanes))
+            second = jnp.broadcast_to(work[:, j + 1 : j + 2], (count, lanes))
+            a, b, c = first[j : j + 1], second[j : j + 1], second[j + 1 : j + 2]
+            row_j = work[j : j + 1]
+            over_a = 1.0 / a
+            part = b * over_a
+            row_next = work[j + 1 : j + 2] - part * row_j
+            over_c = 1.0 / (c - part * b)
+            change = first * (row_j * over_a) + (second - first * part) * (row_next * over_c)
+            work = jnp.where(sub > j + 1, work - change, work)
+            works[m] = jnp.where(sub == j + 1, row_next, work)
+    out = []
+    for work in works:
+        diagonal = jnp.sum(jnp.where(sub == lane, work, 0.0), axis=1, keepdims=True)
+        out.append((work / jnp.sqrt(diagonal))[:, count : 2 * count])
+    return out
 
 
 def final_kernel(quad, patch, gathered, sub_in, sub_edge, basis, coupling, slabs, sems):
@@ -405,54 +439,54 @@
     last = lax.axis_size(patch) - 1
     inner, count, sub_width = sub_in.shape
     height = inner + SWEEPS
-    total = gathered[0]
-    for k in range(1, gathered.shape[0]):
-        total = total + gathered[k]
+    total = (gathered[0] + gathered[1]) + (gathered[2] + gathered[3])
     lanes = total.shape[1]
     mats = [total[:, k * count : (k + 1) * count] for k in range(5)]
     eye = (
         lax.broadcasted_iota(jnp.int32, (count, count), 0)
         == lax.broadcasted_iota(jnp.int32, (count, count), 1)
     ).astype(f32)
-    own = inverse_factor(mats[0], eye, lanes)
-    left = inverse_factor(jnp.where(place == 0, eye, mats[1]), eye, lanes)
-    right = inverse_factor(jnp.where(place == last, eye, mats[2]), eye, lanes)
-    coupling[0] = dot_nt(dot_nn(own, mats[3], highest), left, highest)
-    coupling[1] = dot_nt(dot_nn(own, mats[4], highest), right, highest)
+    grams = [
+        mats[0],
+        jnp.where(place == 0, eye, mats[1]),
+        jnp.where(place == last, eye, mats[2]),
+    ]
+    own, left, right = inverse_factors(grams, eye, lanes)
 
     high = own.astype(bf16).astype(f32)
     low = own - high
     factor = jnp.concatenate([high, high, low, low], axis=1).astype(bf16)
-
-    def write(source, row, place_row):
-        r = jnp.where(odd == 1, height - 1 - place_row, place_row)
-        x = source[row]
-        x_high = x.astype(bf16).astype(f32)
-        x_low = x - x_high
-        value = dot_nn(
-            factor, jnp.concatenate([x_high, x_low, x_high, x_low], axis=0).astype(bf16)
-        )
-        for k in range(sub_width // LANES):
-            flat = slabs.at[k].reshape(count * height, LANES)
-            for g in range(count // 8):
-                flat[pl.ds(8 * height * g + r, 8, stride=height), :] = value[
-                    8 * g : 8 * g + 8, LANES * k : LANES * (k + 1)
-                ]
-
-    lax.fori_loop(0, SWEEPS, lambda row, c: (write(sub_edge, row, row), c)[1], 0, unroll=4)
-    lax.fori_loop(
-        0, inner, lambda row, c: (write(sub_in, row, row + SWEEPS), c)[1], 0, unroll=4
-    )
-    copies = [
-        pltpu.make_async_copy(
-            slabs.at[k], basis.at[:, :, pl.ds(LANES * k, LANES)], sems.at[k]
-        )
-        for k in range(sub_width // LANES)
-    ]
-    for copy in copies:
-        copy.start()
-    for copy in copies:
-        copy.wait()
+    stride = slabs.shape[2]
+    copies = []
+    for block in range(height // 8):
+        natural = jnp.where(odd == 1, height // 8 - 1 - block, block)
+        for k in range(8):
+            row = 8 * block + k
+            x = sub_edge[row] if row < SWEEPS else sub_in[row - SWEEPS]
+            r = jnp.where(odd == 1, height - 1 - row, row)
+            x_high = x.astype(bf16).astype(f32)
+            x_low = x - x_high
+            value = dot_nn(
+                factor, jnp.concatenate([x_high, x_low, x_high, x_low], axis=0).astype(bf16)
+            )
+            for c in range(sub_width // LANES):
+                flat = slabs.at[c].reshape(count * stride, LANES)
+                for g in range(count // 8):
+                    flat[pl.ds(8 * stride * g + r, 8, stride=stride), :] = value[
+                        8 * g : 8 * g + 8, LANES * c : LANES * (c + 1)
+                    ]
+        at = pl.ds(pl.multiple_of(8 * natural, 8), 8)
+        for c in range(sub_width // LANES):
+            copy = pltpu.make_async_copy(
+                slabs.at[c, :, at],
+                basis.at[:, at, pl.ds(LANES * c, LANES)],
+                sems.at[block, c],
+            )
+            copy.start()
+            copies.append(copy)
+    coupling[0] = dot_nt(dot_nn(own, mats[3], highest), left, highest)
+    coupling[1] = dot_nt(dot_nn(own, mats[4], highest), right, highest)
+    wait_all(copies)
 
 
 def call_prepare(vec, log_own):
@@ -460,12 +494,15 @@
     return pl.pallas_call(
         functools.partial(prepare_kernel, "quad"),
         out_shape=(shape(count + 1, SWEEPS, width),) * 2,
-        in_specs=[ANY, ANY],
+        in_specs=[pl.BlockSpec(memory_space=pltpu.HBM)] * 2,
         out_specs=(VMEM, VMEM),
         scratch_shapes=[pltpu.SemaphoreType.DMA((4,))],
         compiler_params=PARAMS,
         name="prepare",
-    )(vec, log_own)
+    )(
+        pltpu.with_memory_space_constraint(vec, pltpu.HBM),
+        pltpu.with_memory_space_constraint(log_own, pltpu.HBM),
+    )
 
 
 def call_inner(vec, halo_a, log_own):
@@ -487,11 +524,11 @@
             pltpu.VMEM((total, groups, 8, width), f32),
             pltpu.VMEM((total, groups, 8, width), f32),
             pltpu.VMEM((total - 2, 4, 8, width), f32),
-            pltpu.VMEM((width // LANES, count, height, LANES), f32),
+            pltpu.VMEM((width // LANES, count, height + PAD, LANES), f32),
             pltpu.VMEM((width // LANES, count + 1, SWEEPS, LANES), f32),
             pltpu.VMEM((height + 32, width), f32),
             pltpu.VMEM((4, height + 16, width), f32),
-            pltpu.SemaphoreType.DMA((2, width // LANES)),
+            pltpu.SemaphoreType.DMA((height // 8 + 1, width // LANES)),
         ],
         in_specs=[ANY, ANY, VMEM],
         compiler_params=PARAMS,
@@ -546,8 +583,8 @@
         out_shape=(shape(count, height, sub_width), shape(2, count, count)),
         out_specs=(ANY, VMEM),
         scratch_shapes=[
-            pltpu.VMEM((sub_width // LANES, count, height, LANES), f32),
-            pltpu.SemaphoreType.DMA((sub_width // LANES,)),
+            pltpu.VMEM((sub_width // LANES, count, height + PAD, LANES), f32),
+            pltpu.SemaphoreType.DMA((height // 8, sub_width // LANES)),
         ],
         compiler_params=PARAMS,
         name="final",

time: 62.9 us -> 50.8 us (0.81)
  Pallas kernels: 28.7 us -> 16.8 us
  local copies, waits for them, and re-layouts: 2.24 us -> 0.01 us
  blocking collectives: 7.98 us -> 9.85 us
  starting transfers between devices: 15.5 us -> 16.5 us
  waiting for transfers between devices: 7.52 us -> 6.75 us
    pallas_call x1, Pallas kernels: 17.5 us -> 8.79 us  [call_inner(): pl.pallas_call(functools.partial(inner_kernel, 'quad', 'patch'), out_shap...]
    pallas_call x1, Pallas kernels: 5.9 us -> 3.38 us  [call_final(): pl.pallas_call(functools.partial(final_kernel, 'quad', 'patch'), out_shap...]
    unnamed x6 -> x4, local copies, waits for them, and re-layouts: 2.24 us -> 0.01 us
    pallas_call x1, Pallas kernels: 4.72 us -> 2.81 us  [call_edge(): pl.pallas_call(functools.partial(edge_kernel, 'quad', 'patch'), out_shape...]
    all_gather x1, blocking collectives: 7.98 us -> 9.85 us  [on_device(): gathered = lax.all_gather(packed, 'quad')]
    pallas_call x1, Pallas kernels: 0.15 us -> 1.3 us  [call_prepare(): pl.pallas_call(functools.partial(prepare_kernel, 'quad'), out_shape=(shap...]
    ppermute x1, starting transfers between devices: 5.93 us -> 6.91 us  [on_device(): from_2 = lax.ppermute(send_2, 'patch', pairs(patch_size, 1))]
    ppermute x1, waiting for transfers between devices: 7.42 us -> 6.44 us  [on_device(): from_2 = lax.ppermute(send_2, 'patch', pairs(patch_size, 1))]
  transfers between devices with their start and end apart: 4 -> 4, of which waited for: 2 -> 2; matrix products, arithmetic and copies ran while one was open for 0% -> 0% of each run, Pallas kernels for 28% -> 17%
where the time goes in v3:
time: 50.8 us; the launch traced here: 50.6 us
  Pallas kernels  16.8 us (33%)
  starting transfers between devices  16.5 us (32%)
  blocking collectives  9.85 us (19%)
  waiting for transfers between devices  6.75 us (13%)
  between operations  0.73 us (1%)
    all_gather x1, blocking collectives, on_device(): gathered = lax.all_gather(packed, 'quad')  9.85 us
    pallas_call x1, Pallas kernels, call_inner(): pl.pallas_call(functools.partial(inner_kernel, 'quad', 'patch'), out_shap...  8.79 us
    ppermute x1, starting transfers between devices, on_device(): halo_b = lax.ppermute(send_b, 'quad', pairs(quad_size, 1))  8.72 us
    ppermute x1, starting transfers between devices, on_device(): from_2 = lax.ppermute(send_2, 'patch', pairs(patch_size, 1))  6.91 us
    ppermute x1, waiting for transfers between devices, on_device(): from_2 = lax.ppermute(send_2, 'patch', pairs(patch_size, 1))  6.44 us
    pallas_call x1, Pallas kernels, call_final(): pl.pallas_call(functools.partial(final_kernel, 'quad', 'patch'), out_shap...  3.38 us
    pallas_call x1, Pallas kernels, call_edge(): pl.pallas_call(functools.partial(edge_kernel, 'quad', 'patch'), out_shape...  2.81 us
    pallas_call x1, Pallas kernels, call_prepare(): pl.pallas_call(functools.partial(prepare_kernel, 'quad'), out_shape=(shap...  1.3 us
  transfers between devices with their start and end apart: 4, of which 2 were waited for; matrix products, arithmetic and copies ran while one was open for 0% of the time, Pallas kernels for 17%

profile of v3, /device:TPU:25, one launch (start us, length us, event | category | flops | bytes accessed | tf_op | source)
XLA Modules:
  0.0 50.6 jit_solution(7405753463593819377)
XLA Ops:
  0.6 0.0 copy-start.1
  0.6 0.0 copy-start
  0.6 1.3 %prepare.1 = (f32[25,8,512]{2,1,0:T(8,128)S(1)}, f32[25,8,512]{2,1,0:T(8,128)S(1)}) custom-call(f32[24,32,512]{2,1,0:T(8,128)} %bitcast.5, f32[32,512]{1,0:T(8,128)} %bitcast.7), custom_call_target="tpu_custom_call" | custom-call | tf_op jit(solution)/shard_map/prepare/pallas_call | solution.py:494
  2.0 0.8 %collective-permute-start = (f32[25,8,512]{2,1,0:T(8,128)S(1)}, f32[25,8,512]{2,1,0:T(8,128)S(1)}, u32[]{:S(2)}, u32[]{:S(2)}) collective-permute-start(f32[25,8,512]{2,1,0:T(8,128)S(1)} %get-tuple-element.18), channel_id=1, source_target_pairs={{0,1},{2,3},{1,0},{3,2},{4,5},{6,7},{5,4},{7,6},{8,9},{10,11},{9,8... | collective-permute-start | bytes 1228808 | tf_op jit(solution)/shard_map/ppermute | solution.py:603
  2.7 8.7 %collective-permute-start.1 = (f32[25,8,512]{2,1,0:T(8,128)S(1)}, f32[25,8,512]{2,1,0:T(8,128)S(1)}, u32[]{:S(2)}, u32[]{:S(2)}) collective-permute-start(f32[25,8,512]{2,1,0:T(8,128)S(1)} %get-tuple-element.20), channel_id=1, source_target_pairs={{1,2},{2,1},{5,6},{6,5},{9,10},{10,9},{13,14},{14,13},{17,18},{18,... | collective-permute-start | bytes 1228808 | tf_op jit(solution)/shard_map/ppermute | solution.py:604
  11.4 0.0 collective-permute-done.halo_a
  11.5 0.0 copy-done.1
  11.5 0.0 copy-done
  11.5 8.8 %inner.1 = (f32[24,24,128]{2,1,0:T(8,128)S(1)}, f32[24,24,128]{2,1,0:T(8,128)S(1)}, f32[24,24,256]{2,1,0:T(8,128)S(1)}, f32[24,24,128]{2,1,0:T(8,128)S(1)}, f32[...) custom-call(f32[24,32,512]{2,1,0:T(8,128)S(1)} %bitcast.6, ...), custom_call_target="tpu_custom_call" | custom-call | flops 37748736 | bytes 5242880 | tf_op jit(solution)/shard_map/inner/pallas_call | solution.py:512
  20.3 0.0 collective-permute-done.1.halo_b
  20.3 2.8 %edge.1 = (f32[8,24,128]{2,1,0:T(8,128)S(1)}, f32[8,24,128]{2,1,0:T(8,128)S(1)}, f32[8,24,256]{2,1,0:T(8,128)S(1)}, f32[33,24,128]{2,1,0:T(8,128)S(1)}, f32[33,24,128]{2,1,0:T(8,128)S(1)}) custom-call(f32[25,8,512]{2,1,0:T(8,128)S(1)} %collective-permute-done.1.halo_b, f32[32,512]{1,0:T(8,128)S(1)} %bitcast.9, ...), custom_call_target="tpu_custom_call" | custom-call | tf_op jit(solution)/shard_map/edge/pallas_call | solution.py:544
  23.1 6.9 %collective-permute-start.3 = (f32[33,24,128]{2,1,0:T(8,128)S(1)}, f32[33,24,128]{2,1,0:T(8,128)S(1)}, u32[]{:S(2)}, u32[]{:S(2)}) collective-permute-start(f32[33,24,128]{2,1,0:T(8,128)S(1)} %get-tuple-element.29), channel_id=1, source_target_pairs={{4,8},{12,16},{20,24},{28,32},{36,40},{44,48},{52,56},{60,64},{68,... | collective-permute-start | bytes 1216520 | tf_op jit(solution)/shard_map/ppermute | solution.py:611
  30.0 0.1 collective-permute-start.2
  30.1 6.4 %collective-permute-done.3.from_left_pair = f32[33,24,128]{2,1,0:T(8,128)S(1)} collective-permute-done((f32[33,24,128]{2,1,0:T(8,128)S(1)}, f32[33,24,128]{2,1,0:T(8,128)S(1)}, u32[]{:S(2)}, u32[]{:S(2)}) %collective-permute-start.3) | collective-permute-done | bytes 405536 | tf_op jit(solution)/shard_map/ppermute | solution.py:611
  36.6 0.3 collective-permute-done.2.from_right_pair
  36.9 0.5 product.1
  37.4 9.9 %all-gather = f32[96,128]{1,0:T(8,128)S(1)} all-gather(f32[24,128]{1,0:T(8,128)S(1)} %product.1), channel_id=2, replica_groups=mesh['patch'=64,'quad'=4] {'quad'}, dimensions={0}, use_global_device_ids=true | all-gather | bytes 61440 | tf_op jit(solution)/shard_map/all_gather | solution.py:614
  47.2 3.4 %final.1 = (f32[24,32,256]{2,1,0:T(8,128)}, f32[2,24,24]{2,1,0:T(8,128)}) custom-call(f32[4,24,128]{2,1,0:T(8,128)S(1)} %bitcast.10, f32[24,24,256]{2,1,0:T(8,128)S(1)} %get-tuple-element.30.sub_in, f32[8,24,256]{2,1,0:T(8,128)S(1)} %get-tuple-element.31.sub_edge), custom_call_target="tpu_custom_call" | custom-call | tf_op jit(solution)/shard_map/final/pallas_call | solution.py:581
Async XLA Ops:
  0.6 10.8 %copy-start.1 = (f32[1,32,512]{2,1,0:T(8,128)S(1)}, f32[1,32,512]{2,1,0:T(8,128)}, u32[]{:S(2)}) copy-start(f32[1,32,512]{2,1,0:T(8,128)} %param.3) | copy-start | bytes 196612
  0.6 10.8 %copy-start = (f32[1,24,32,512]{3,2,1,0:T(8,128)S(1)}, f32[1,24,32,512]{3,2,1,0:T(8,128)}, u32[]{:S(2)}) copy-start(f32[1,24,32,512]{3,2,1,0:T(8,128)} %param.2) | copy-start | bytes 4718596
  2.0 9.5 %collective-permute-start = (f32[25,8,512]{2,1,0:T(8,128)S(1)}, f32[25,8,512]{2,1,0:T(8,128)S(1)}, u32[]{:S(2)}, u32[]{:S(2)}) collective-permute-start(f32[25,8,512]{2,1,0:T(8,128)S(1)} %get-tuple-element.18), channel_id=1, source_target_pairs={{0,1},{2,3},{1,0},{3,2},{4,5},{6,7},{5,4},{7,6},{8,9},{10,11},{9,8... | collective-permute-start | bytes 1228808 | tf_op jit(solution)/shard_map/ppermute | solution.py:603
  2.7 17.6 %collective-permute-start.1 = (f32[25,8,512]{2,1,0:T(8,128)S(1)}, f32[25,8,512]{2,1,0:T(8,128)S(1)}, u32[]{:S(2)}, u32[]{:S(2)}) collective-permute-start(f32[25,8,512]{2,1,0:T(8,128)S(1)} %get-tuple-element.20), channel_id=1, source_target_pairs={{1,2},{2,1},{5,6},{6,5},{9,10},{10,9},{13,14},{14,13},{17,18},{18,... | collective-permute-start | bytes 1228808 | tf_op jit(solution)/shard_map/ppermute | solution.py:604
  23.1 13.5 %collective-permute-start.3 = (f32[33,24,128]{2,1,0:T(8,128)S(1)}, f32[33,24,128]{2,1,0:T(8,128)S(1)}, u32[]{:S(2)}, u32[]{:S(2)}) collective-permute-start(f32[33,24,128]{2,1,0:T(8,128)S(1)} %get-tuple-element.29), channel_id=1, source_target_pairs={{4,8},{12,16},{20,24},{28,32},{36,40},{44,48},{52,56},{60,64},{68,... | collective-permute-start | bytes 1216520 | tf_op jit(solution)/shard_map/ppermute | solution.py:611
  30.0 6.8 %collective-permute-start.2 = (f32[33,24,128]{2,1,0:T(8,128)S(1)}, f32[33,24,128]{2,1,0:T(8,128)S(1)}, u32[]{:S(2)}, u32[]{:S(2)}) collective-permute-start(f32[33,24,128]{2,1,0:T(8,128)S(1)} %get-tuple-element.28.sent), channel_id=1, source_target_pairs={{0,4},{8,12},{16,20},{24,28},{32,36},{40,44},{48,52},{56,60},{64,6... | collective-permute-start | bytes 1216520 | tf_op jit(solution)/shard_map/ppermute | solution.py:612

commit v4 on v3

--- a/solution.py
+++ b/solution.py
@@ -433,13 +433,17 @@
     return out
 
 
-def final_kernel(quad, patch, gathered, sub_in, sub_edge, basis, coupling, slabs, sems):
+def final_kernel(
+    quad, patch, outer_total, passed, sub_in, sub_edge, basis, coupling, slabs, sems
+):
     odd = lax.rem(lax.axis_index(quad), 2)
     place = lax.axis_index(patch)
     last = lax.axis_size(patch) - 1
     inner, count, sub_width = sub_in.shape
     height = inner + SWEEPS
-    total = (gathered[0] + gathered[1]) + (gathered[2] + gathered[3])
+    index = lax.axis_index(quad)
+    outer = jnp.logical_or(index == 0, index == lax.axis_size(quad) - 1)
+    total = jnp.where(outer, outer_total[...], passed[...])
     lanes = total.shape[1]
     mats = [total[:, k * count : (k + 1) * count] for k in range(5)]
     eye = (
@@ -575,7 +579,7 @@
     )(left_in, left_edge, right_in, right_edge, from_right_pair, from_left_pair, sent)
 
 
-def call_final(gathered, sub_in, sub_edge):
+def call_final(outer_total, passed, sub_in, sub_edge):
     inner, count, sub_width = sub_in.shape
     height = inner + SWEEPS
     return pl.pallas_call(
@@ -588,7 +592,7 @@
         ],
         compiler_params=PARAMS,
         name="final",
-    )(gathered, sub_in, sub_edge)
+    )(outer_total, passed, sub_in, sub_edge)
 
 
 def pairs(size, first):
@@ -611,8 +615,12 @@
     from_2 = lax.ppermute(send_2, "patch", pairs(patch_size, 1))
     from_1 = lax.ppermute(send_1, "patch", pairs(patch_size, 0))
     packed = call_product(left_in, left_edge, right_in, right_edge, from_1, from_2, send_1)
-    gathered = lax.all_gather(packed, "quad")
-    basis, coupling = call_final(gathered, sub_in, sub_edge)
+    far = lax.ppermute(packed, "quad", [(1, 3), (2, 0)])
+    ends = lax.ppermute(packed, "quad", [(0, 3), (3, 0)])
+    near = lax.ppermute(packed, "quad", [(1, 0), (2, 3)])
+    outer_total = (packed + near) + (far + ends)
+    passed = lax.ppermute(outer_total, "quad", [(0, 1), (3, 2)])
+    basis, coupling = call_final(outer_total, passed, sub_in, sub_edge)
     return basis[None], coupling[None]
 
 

time: 50.8 us -> 53.9 us (1.061)
  blocking collectives: 9.85 us -> 0 us
  starting transfers between devices: 16.5 us -> 24.2 us
  waiting for transfers between devices: 6.75 us -> 11.9 us
    all_gather x1 -> x0, blocking collectives: 9.85 us -> none  [on_device(): gathered = lax.all_gather(packed, 'quad')]
    ppermute x0 -> x4, starting transfers between devices: none -> 7.75 us  [the longest x1 4.53 us: on_device(): far = lax.ppermute(packed, 'quad', [(1, 3), (2, 0)])]
    ppermute x0 -> x4, waiting for transfers between devices: none -> 5.15 us  [the longest x1 4.35 us: on_device(): passed = lax.ppermute(outer_total, 'quad', [(0, 1), (3, 2)])]
  transfers between devices with their start and end apart: 4 -> 8, of which waited for: 2 -> 4; matrix products, arithmetic and copies ran while one was open for 0% -> 0% of each run, Pallas kernels for 17% -> 16%
where the time goes in v4:
time: 53.9 us; the launch traced here: 53.7 us
  starting transfers between devices  24.2 us (45%)
  Pallas kernels  16.8 us (31%)
  waiting for transfers between devices  11.9 us (22%)
  between operations  0.78 us (1%)
    pallas_call x1, Pallas kernels, call_inner(): pl.pallas_call(functools.partial(inner_kernel, 'quad', 'patch'), out_shap...  8.79 us
    ppermute x1, starting transfers between devices, on_device(): halo_b = lax.ppermute(send_b, 'quad', pairs(quad_size, 1))  8.72 us
    ppermute x1, starting transfers between devices, on_device(): from_2 = lax.ppermute(send_2, 'patch', pairs(patch_size, 1))  6.91 us
    ppermute x1, waiting for transfers between devices, on_device(): from_2 = lax.ppermute(send_2, 'patch', pairs(patch_size, 1))  6.44 us
    ppermute x1, starting transfers between devices, on_device(): far = lax.ppermute(packed, 'quad', [(1, 3), (2, 0)])  4.53 us
    ppermute x1, waiting for transfers between devices, on_device(): passed = lax.ppermute(outer_total, 'quad', [(0, 1), (3, 2)])  4.35 us
    pallas_call x1, Pallas kernels, call_final(): pl.pallas_call(functools.partial(final_kernel, 'quad', 'patch'), out_shap...  3.38 us
    pallas_call x1, Pallas kernels, call_edge(): pl.pallas_call(functools.partial(edge_kernel, 'quad', 'patch'), out_shape...  2.81 us
  transfers between devices with their start and end apart: 8, of which 4 were waited for; matrix products, arithmetic and copies ran while one was open for 0% of the time, Pallas kernels for 16%

profile of v4, /device:TPU:25, one launch (start us, length us, event | category | flops | bytes accessed | tf_op | source)
XLA Modules:
  0.0 53.7 jit_solution(7332781723781636860)
XLA Ops:
  0.6 0.0 copy-start.1
  0.6 0.0 copy-start
  0.6 1.3 %prepare.1 = (f32[25,8,512]{2,1,0:T(8,128)S(1)}, f32[25,8,512]{2,1,0:T(8,128)S(1)}) custom-call(f32[24,32,512]{2,1,0:T(8,128)} %bitcast.4, f32[32,512]{1,0:T(8,128)} %bitcast.6), custom_call_target="tpu_custom_call" | custom-call | tf_op jit(solution)/shard_map/prepare/pallas_call | solution.py:498
  2.0 0.8 %collective-permute-start = (f32[25,8,512]{2,1,0:T(8,128)S(1)}, f32[25,8,512]{2,1,0:T(8,128)S(1)}, u32[]{:S(2)}, u32[]{:S(2)}) collective-permute-start(f32[25,8,512]{2,1,0:T(8,128)S(1)} %get-tuple-element.18), channel_id=1, source_target_pairs={{0,1},{2,3},{1,0},{3,2},{4,5},{6,7},{5,4},{7,6},{8,9},{10,11},{9,8... | collective-permute-start | bytes 1228808 | tf_op jit(solution)/shard_map/ppermute | solution.py:607
  2.7 8.7 %collective-permute-start.1 = (f32[25,8,512]{2,1,0:T(8,128)S(1)}, f32[25,8,512]{2,1,0:T(8,128)S(1)}, u32[]{:S(2)}, u32[]{:S(2)}) collective-permute-start(f32[25,8,512]{2,1,0:T(8,128)S(1)} %get-tuple-element.20), channel_id=1, source_target_pairs={{1,2},{2,1},{5,6},{6,5},{9,10},{10,9},{13,14},{14,13},{17,18},{18,... | collective-permute-start | bytes 1228808 | tf_op jit(solution)/shard_map/ppermute | solution.py:608
  11.4 0.0 collective-permute-done.halo_a
  11.5 0.0 copy-done.1
  11.5 0.0 copy-done
  11.5 8.8 %inner.1 = (f32[24,24,128]{2,1,0:T(8,128)S(1)}, f32[24,24,128]{2,1,0:T(8,128)S(1)}, f32[24,24,256]{2,1,0:T(8,128)S(1)}, f32[24,24,128]{2,1,0:T(8,128)S(1)}, f32[...) custom-call(f32[24,32,512]{2,1,0:T(8,128)S(1)} %bitcast.5, ...), custom_call_target="tpu_custom_call" | custom-call | flops 37748736 | bytes 5242880 | tf_op jit(solution)/shard_map/inner/pallas_call | solution.py:516
  20.3 0.0 collective-permute-done.1.halo_b
  20.3 2.8 %edge.1 = (f32[8,24,128]{2,1,0:T(8,128)S(1)}, f32[8,24,128]{2,1,0:T(8,128)S(1)}, f32[8,24,256]{2,1,0:T(8,128)S(1)}, f32[33,24,128]{2,1,0:T(8,128)S(1)}, f32[33,24,128]{2,1,0:T(8,128)S(1)}) custom-call(f32[25,8,512]{2,1,0:T(8,128)S(1)} %collective-permute-done.1.halo_b, f32[32,512]{1,0:T(8,128)S(1)} %bitcast.8, ...), custom_call_target="tpu_custom_call" | custom-call | tf_op jit(solution)/shard_map/edge/pallas_call | solution.py:548
  23.1 6.9 %collective-permute-start.3 = (f32[33,24,128]{2,1,0:T(8,128)S(1)}, f32[33,24,128]{2,1,0:T(8,128)S(1)}, u32[]{:S(2)}, u32[]{:S(2)}) collective-permute-start(f32[33,24,128]{2,1,0:T(8,128)S(1)} %get-tuple-element.29), channel_id=1, source_target_pairs={{4,8},{12,16},{20,24},{28,32},{36,40},{44,48},{52,56},{60,64},{68,... | collective-permute-start | bytes 1216520 | tf_op jit(solution)/shard_map/ppermute | solution.py:615
  30.0 0.1 collective-permute-start.2
  30.1 6.4 %collective-permute-done.3.from_left_pair = f32[33,24,128]{2,1,0:T(8,128)S(1)} collective-permute-done((f32[33,24,128]{2,1,0:T(8,128)S(1)}, f32[33,24,128]{2,1,0:T(8,128)S(1)}, u32[]{:S(2)}, u32[]{:S(2)}) %collective-permute-start.3) | collective-permute-done | bytes 405536 | tf_op jit(solution)/shard_map/ppermute | solution.py:615
  36.6 0.3 collective-permute-done.2.from_right_pair
  36.9 0.5 product.1
  37.4 0.7 %collective-permute-start.6 = (f32[24,128]{1,0:T(8,128)S(1)}, f32[24,128]{1,0:T(8,128)S(1)}, u32[]{:S(2)}, u32[]{:S(2)}) collective-permute-start(f32[24,128]{1,0:T(8,128)S(1)} %product.1), channel_id=1, source_target_pairs={{0,3},{3,0},{4,7},{7,4},{8,11},{11,8},{12,15},{15,12},{16,19},{19,... | collective-permute-start | bytes 36872 | tf_op jit(solution)/shard_map/ppermute | solution.py:619
  38.0 4.5 %collective-permute-start.5 = (f32[24,128]{1,0:T(8,128)S(1)}, f32[24,128]{1,0:T(8,128)S(1)}, u32[]{:S(2)}, u32[]{:S(2)}) collective-permute-start(f32[24,128]{1,0:T(8,128)S(1)} %product.1), channel_id=1, source_target_pairs={{1,3},{2,0},{5,7},{6,4},{9,11},{10,8},{13,15},{14,12},{17,19},{18,... | collective-permute-start | bytes 36872 | tf_op jit(solution)/shard_map/ppermute | solution.py:618
  42.6 1.3 %collective-permute-start.4 = (f32[24,128]{1,0:T(8,128)S(1)}, f32[24,128]{1,0:T(8,128)S(1)}, u32[]{:S(2)}, u32[]{:S(2)}) collective-permute-start(f32[24,128]{1,0:T(8,128)S(1)} %product.1), channel_id=1, source_target_pairs={{1,0},{2,3},{5,4},{6,7},{9,8},{10,11},{13,12},{14,15},{17,16},{18,... | collective-permute-start | bytes 36872 | tf_op jit(solution)/shard_map/ppermute | solution.py:620
  43.9 0.0 collective-permute-done.6
  43.9 0.0 collective-permute-done.5
  43.9 0.8 %collective-permute-done.4 = f32[24,128]{1,0:T(8,128)S(1)} collective-permute-done((f32[24,128]{1,0:T(8,128)S(1)}, f32[24,128]{1,0:T(8,128)S(1)}, u32[]{:S(2)}, u32[]{:S(2)}) %collective-permute-start.4) | collective-permute-done | bytes 12320 | tf_op jit(solution)/shard_map/ppermute | solution.py:620
  44.7 1.3 %collective-permute-start.7 = (f32[24,128]{1,0:T(8,128)S(1)}, f32[24,128]{1,0:T(8,128)S(1)}, u32[]{:S(2)}, u32[]{:S(2)}) collective-permute-start(f32[24,128]{1,0:T(8,128)S(1)} %add_add_fusion.outer_total), channel_id=1, source_target_pairs={{0,1},{3,2},{4,5},{7,6},{8,9},{11,10},{12,13},{15,14},{16,17},{19,... | collective-permute-start | bytes 36872 | tf_op jit(solution)/shard_map/ppermute | solution.py:622
  46.0 4.4 %collective-permute-done.7.passed = f32[24,128]{1,0:T(8,128)S(1)} collective-permute-done((f32[24,128]{1,0:T(8,128)S(1)}, f32[24,128]{1,0:T(8,128)S(1)}, u32[]{:S(2)}, u32[]{:S(2)}) %collective-permute-start.7) | collective-permute-done | bytes 12320 | tf_op jit(solution)/shard_map/ppermute | solution.py:622
  50.3 3.4 %final.1 = (f32[24,32,256]{2,1,0:T(8,128)}, f32[2,24,24]{2,1,0:T(8,128)}) custom-call(f32[24,128]{1,0:T(8,128)S(1)} %add_add_fusion.outer_total, f32[24,128]{1,0:T(8,128)S(1)} %collective-permute-done.7.passed, f32[24,24,256]{2,1,0:T(8,128)S(1)} %get-tuple-element.30.sub_in, f32[8,24,256]{2,1,0:T(8,128)S(1)} %get-tuple-element.31.sub_edge), custom_call_target="tpu_custom_call" | custom-call | tf_op jit(solution)/shard_map/final/pallas_call | solution.py:585
  (1 shorter events, 0.0 us)
Async XLA Ops:
  0.6 10.8 %copy-start.1 = (f32[1,32,512]{2,1,0:T(8,128)S(1)}, f32[1,32,512]{2,1,0:T(8,128)}, u32[]{:S(2)}) copy-start(f32[1,32,512]{2,1,0:T(8,128)} %param.3) | copy-start | bytes 196612
  0.6 10.8 %copy-start = (f32[1,24,32,512]{3,2,1,0:T(8,128)S(1)}, f32[1,24,32,512]{3,2,1,0:T(8,128)}, u32[]{:S(2)}) copy-start(f32[1,24,32,512]{3,2,1,0:T(8,128)} %param.2) | copy-start | bytes 4718596
  2.0 9.5 %collective-permute-start = (f32[25,8,512]{2,1,0:T(8,128)S(1)}, f32[25,8,512]{2,1,0:T(8,128)S(1)}, u32[]{:S(2)}, u32[]{:S(2)}) collective-permute-start(f32[25,8,512]{2,1,0:T(8,128)S(1)} %get-tuple-element.18), channel_id=1, source_target_pairs={{0,1},{2,3},{1,0},{3,2},{4,5},{6,7},{5,4},{7,6},{8,9},{10,11},{9,8... | collective-permute-start | bytes 1228808 | tf_op jit(solution)/shard_map/ppermute | solution.py:607
  2.7 17.6 %collective-permute-start.1 = (f32[25,8,512]{2,1,0:T(8,128)S(1)}, f32[25,8,512]{2,1,0:T(8,128)S(1)}, u32[]{:S(2)}, u32[]{:S(2)}) collective-permute-start(f32[25,8,512]{2,1,0:T(8,128)S(1)} %get-tuple-element.20), channel_id=1, source_target_pairs={{1,2},{2,1},{5,6},{6,5},{9,10},{10,9},{13,14},{14,13},{17,18},{18,... | collective-permute-start | bytes 1228808 | tf_op jit(solution)/shard_map/ppermute | solution.py:608
  23.1 13.5 %collective-permute-start.3 = (f32[33,24,128]{2,1,0:T(8,128)S(1)}, f32[33,24,128]{2,1,0:T(8,128)S(1)}, u32[]{:S(2)}, u32[]{:S(2)}) collective-permute-start(f32[33,24,128]{2,1,0:T(8,128)S(1)} %get-tuple-element.29), channel_id=1, source_target_pairs={{4,8},{12,16},{20,24},{28,32},{36,40},{44,48},{52,56},{60,64},{68,... | collective-permute-start | bytes 1216520 | tf_op jit(solution)/shard_map/ppermute | solution.py:615
  30.0 6.8 %collective-permute-start.2 = (f32[33,24,128]{2,1,0:T(8,128)S(1)}, f32[33,24,128]{2,1,0:T(8,128)S(1)}, u32[]{:S(2)}, u32[]{:S(2)}) collective-permute-start(f32[33,24,128]{2,1,0:T(8,128)S(1)} %get-tuple-element.28.sent), channel_id=1, source_target_pairs={{0,4},{8,12},{16,20},{24,28},{32,36},{40,44},{48,52},{56,60},{64,6... | collective-permute-start | bytes 1216520 | tf_op jit(solution)/shard_map/ppermute | solution.py:616
  37.4 6.5 %collective-permute-start.6 = (f32[24,128]{1,0:T(8,128)S(1)}, f32[24,128]{1,0:T(8,128)S(1)}, u32[]{:S(2)}, u32[]{:S(2)}) collective-permute-start(f32[24,128]{1,0:T(8,128)S(1)} %product.1), channel_id=1, source_target_pairs={{0,3},{3,0},{4,7},{7,4},{8,11},{11,8},{12,15},{15,12},{16,19},{19,... | collective-permute-start | bytes 36872 | tf_op jit(solution)/shard_map/ppermute | solution.py:619
  38.0 5.8 %collective-permute-start.5 = (f32[24,128]{1,0:T(8,128)S(1)}, f32[24,128]{1,0:T(8,128)S(1)}, u32[]{:S(2)}, u32[]{:S(2)}) collective-permute-start(f32[24,128]{1,0:T(8,128)S(1)} %product.1), channel_id=1, source_target_pairs={{1,3},{2,0},{5,7},{6,4},{9,11},{10,8},{13,15},{14,12},{17,19},{18,... | collective-permute-start | bytes 36872 | tf_op jit(solution)/shard_map/ppermute | solution.py:618
  42.6 2.1 %collective-permute-start.4 = (f32[24,128]{1,0:T(8,128)S(1)}, f32[24,128]{1,0:T(8,128)S(1)}, u32[]{:S(2)}, u32[]{:S(2)}) collective-permute-start(f32[24,128]{1,0:T(8,128)S(1)} %product.1), channel_id=1, source_target_pairs={{1,0},{2,3},{5,4},{6,7},{9,8},{10,11},{13,12},{14,15},{17,16},{18,... | collective-permute-start | bytes 36872 | tf_op jit(solution)/shard_map/ppermute | solution.py:620
  44.7 5.6 %collective-permute-start.7 = (f32[24,128]{1,0:T(8,128)S(1)}, f32[24,128]{1,0:T(8,128)S(1)}, u32[]{:S(2)}, u32[]{:S(2)}) collective-permute-start(f32[24,128]{1,0:T(8,128)S(1)} %add_add_fusion.outer_total), channel_id=1, source_target_pairs={{0,1},{3,2},{4,5},{7,6},{8,9},{11,10},{12,13},{15,14},{16,17},{19,... | collective-permute-start | bytes 36872 | tf_op jit(solution)/shard_map/ppermute | solution.py:622

commit v5 on v3

--- a/solution.py
+++ b/solution.py
@@ -207,14 +207,14 @@
 
 
 def emit(final, first, count, groups, matrix, swap, outs, out_first):
-    outer_left, outer_right, sub, send_right_pair, send_left_pair = outs
+    outer, sub, send_right_pair, send_left_pair = outs
     width = final.shape[-1]
     x = final[pl.ds(first, 8)].reshape(8 * count, width)
     x = permute_columns(x, matrix).reshape(8, count, width)
     b = blocks_of(x)
     at = pl.ds(out_first, 8)
-    outer_left[at] = b[0]
-    outer_right[at] = b[3]
+    outer[0, at] = b[0]
+    outer[1, at] = b[3]
     sub[at] = jnp.concatenate(b[1:3], axis=2)
     send_right_pair[at] = jnp.where(swap, b[1], b[2])
     send_left_pair[at] = jnp.where(swap, b[2], b[1])
@@ -250,7 +250,7 @@
 
 def inner_kernel(
     quad, patch, vec, halo_a, log_kappa,
-    outer_left, outer_right, sub, send_right, send_left, rim, gram,
+    outer, sub, send_right, send_left, rim, gram,
     even, odd_buf, weights, vec_slabs, halo_slabs, logs, natural, sems,
 ):
     odd = lax.rem(lax.axis_index(quad), 2)
@@ -304,7 +304,7 @@
 
     final = bufs[SWEEPS % 2]
     back = permutation(width, True)
-    outs = (outer_left, outer_right, sub, send_right, send_left)
+    outs = (outer, sub, send_right, send_left)
 
     def finish(block, carry):
         row = pl.multiple_of(8 * block, 8)
@@ -317,8 +317,8 @@
 
 
 def edge_kernel(
-    quad, patch, halo_b, log_kappa, rim, gram_inner, send_right_in, send_left_in,
-    outer_left, outer_right, sub, send_right, send_left,
+    quad, patch, halo_b, log_kappa, rim, gram_inner, outer_in, send_right_in, send_left_in,
+    outer, sub, send_right, send_left,
     even, odd_buf, weights, halo_slabs, logs, natural, sems,
 ):
     index = lax.axis_index(quad)
@@ -361,50 +361,61 @@
 
     final = bufs[SWEEPS % 2]
     back = permutation(width, True)
-    emit(final, SWEEPS, count, groups, back, swap, (outer_left, outer_right, sub, send_right, send_left), 0)
+    emit(final, SWEEPS, count, groups, back, swap, (outer, sub, send_right, send_left), 0)
     x = rows_as_columns(sub, 0, SWEEPS)
     total = gram_inner[...] + gram_product(x, x)
     inner = height - SWEEPS
-    for out, source in ((send_right, send_right_in), (send_left, send_left_in)):
+    for out, source in (
+        (send_right, send_right_in),
+        (send_left, send_left_in),
+        (outer.at[0], outer_in.at[0]),
+        (outer.at[1], outer_in.at[1]),
+    ):
         out[pl.ds(SWEEPS, inner)] = source[...]
         out[height] = jnp.zeros((count, LANES), f32)
         out[height, :, :count] = total
 
 
+def at_end(quad):
+    index = lax.axis_index(quad)
+    return jnp.logical_or(index == 0, index == lax.axis_size(quad) - 1)
+
+
 def product_kernel(
-    patch, left_in, left_edge, right_in, right_edge, from_right_pair, from_left_pair, sent, out
+    quad, patch, left_pair, left_pair_mate, right_pair, right_pair_mate, chip_mate, mine, out
 ):
+    end = at_end(quad)
     swap = lax.rem(lax.axis_index(patch), 2) == 1
     count = out.shape[0]
-    inner = left_in.shape[0]
-    height = inner + SWEEPS
-
-    def products(mine, mine_edge, theirs):
-        x = jnp.concatenate(
-            [rows_as_columns(mine_edge, 0, SWEEPS), rows_as_columns(mine, 0, inner)], axis=1
+    height = mine.shape[1] - 1
+    out[...] = jnp.zeros(out.shape, f32)
+
+    def both(a, b):
+        return jnp.concatenate(
+            [rows_as_columns(a, 0, height), rows_as_columns(b, 0, height)], axis=1
         )
-        return gram_product(x, rows_as_columns(theirs, 0, height))
-
-    out[...] = jnp.zeros(out.shape, f32)
-
-    def write(from_left, from_right):
+
+    def gram(a, b):
+        return a[height, :, :count] + b[height, :, :count]
+
+    def write(left, left_mate, right, right_mate):
         mats = (
-            sent[height, :, :count],
-            from_left[height, :, :count],
-            from_right[height, :, :count],
-            products(left_in, left_edge, from_left),
-            products(right_in, right_edge, from_right),
+            gram(mine.at[0], chip_mate.at[0]),
+            gram(left, left_mate),
+            gram(right, right_mate),
+            gram_product(both(mine.at[0], chip_mate.at[0]), both(left, left_mate)),
+            gram_product(both(mine.at[1], chip_mate.at[1]), both(right, right_mate)),
         )
         for k, mat in enumerate(mats):
             out[:, k * count : (k + 1) * count] = mat
 
-    @pl.when(swap)
+    @pl.when(jnp.logical_and(end, swap))
     def _():
-        write(from_right_pair, from_left_pair)
-
-    @pl.when(jnp.logical_not(swap))
+        write(right_pair, right_pair_mate, left_pair, left_pair_mate)
+
+    @pl.when(jnp.logical_and(end, jnp.logical_not(swap)))
     def _():
-        write(from_left_pair, from_right_pair)
+        write(left_pair, left_pair_mate, right_pair, right_pair_mate)
 
 
 def inverse_factors(mats, eye, lanes):
@@ -433,13 +444,15 @@
     return out
 
 
-def final_kernel(quad, patch, gathered, sub_in, sub_edge, basis, coupling, slabs, sems):
+def final_kernel(
+    quad, patch, near, far, passed, sub_in, sub_edge, basis, coupling, slabs, sems
+):
     odd = lax.rem(lax.axis_index(quad), 2)
     place = lax.axis_index(patch)
     last = lax.axis_size(patch) - 1
     inner, count, sub_width = sub_in.shape
     height = inner + SWEEPS
-    total = (gathered[0] + gathered[1]) + (gathered[2] + gathered[3])
+    total = jnp.where(at_end(quad), passed[...], near[...] + far[...])
     lanes = total.shape[1]
     mats = [total[:, k * count : (k + 1) * count] for k in range(5)]
     eye = (
@@ -512,8 +525,7 @@
     return pl.pallas_call(
         functools.partial(inner_kernel, "quad", "patch"),
         out_shape=(
-            shape(inner, count, band),
-            shape(inner, count, band),
+            shape(2, inner, count, band),
             shape(inner, count, 2 * band),
             shape(inner, count, band),
             shape(inner, count, band),
@@ -537,15 +549,14 @@
     )(vec, halo_a, log_own)
 
 
-def call_edge(halo_b, log_own, rim, gram_inner, send_right, send_left):
+def call_edge(halo_b, log_own, rim, gram_inner, outer, send_right, send_left):
     height, width = log_own.shape
     inner, count, band = send_right.shape
     groups = count // 8
     return pl.pallas_call(
         functools.partial(edge_kernel, "quad", "patch"),
         out_shape=(
-            shape(SWEEPS, count, band),
-            shape(SWEEPS, count, band),
+            shape(2, height + 1, count, band),
             shape(SWEEPS, count, 2 * band),
             shape(height + 1, count, band),
             shape(height + 1, count, band),
@@ -559,23 +570,23 @@
             pltpu.VMEM((4, 24, width), f32),
             pltpu.SemaphoreType.DMA((width // LANES,)),
         ],
-        in_specs=[ANY] + [VMEM] * 5,
+        in_specs=[ANY] + [VMEM] * 6,
         compiler_params=PARAMS,
         name="edge",
-    )(halo_b, log_own, rim, gram_inner, send_right, send_left)
-
-
-def call_product(left_in, left_edge, right_in, right_edge, from_right_pair, from_left_pair, sent):
-    count = left_in.shape[1]
+    )(halo_b, log_own, rim, gram_inner, outer, send_right, send_left)
+
+
+def call_product(*blocks):
+    count = blocks[0].shape[1]
     return pl.pallas_call(
-        functools.partial(product_kernel, "patch"),
+        functools.partial(product_kernel, "quad", "patch"),
         out_shape=shape(count, LANES),
         compiler_params=PARAMS,
         name="product",
-    )(left_in, left_edge, right_in, right_edge, from_right_pair, from_left_pair, sent)
-
-
-def call_final(gathered, sub_in, sub_edge):
+    )(*blocks)
+
+
+def call_final(near, far, passed, sub_in, sub_edge):
     inner, count, sub_width = sub_in.shape
     height = inner + SWEEPS
     return pl.pallas_call(
@@ -588,7 +599,7 @@
         ],
         compiler_params=PARAMS,
         name="final",
-    )(gathered, sub_in, sub_edge)
+    )(near, far, passed, sub_in, sub_edge)
 
 
 def pairs(size, first):
@@ -598,21 +609,38 @@
 
 def on_device(vectors, log_kappa):
     vec, log_own = vectors[0], log_kappa[0]
-    patch_size, quad_size = lax.axis_size("patch"), lax.axis_size("quad")
+    patches, quads = lax.axis_size("patch"), lax.axis_size("quad")
     send_a, send_b = call_prepare(vec, log_own)
-    halo_a = lax.ppermute(send_a, "quad", pairs(quad_size, 0))
-    halo_b = lax.ppermute(send_b, "quad", pairs(quad_size, 1))
-    left_in, right_in, sub_in, send_1_in, send_2_in, rim, gram_in = call_inner(
-        vec, halo_a, log_own
-    )
-    left_edge, right_edge, sub_edge, send_1, send_2 = call_edge(
-        halo_b, log_own, rim, gram_in, send_1_in, send_2_in
-    )
-    from_2 = lax.ppermute(send_2, "patch", pairs(patch_size, 1))
-    from_1 = lax.ppermute(send_1, "patch", pairs(patch_size, 0))
-    packed = call_product(left_in, left_edge, right_in, right_edge, from_1, from_2, send_1)
-    gathered = lax.all_gather(packed, "quad")
-    basis, coupling = call_final(gathered, sub_in, sub_edge)
+    halo_a = lax.ppermute(send_a, "quad", pairs(quads, 0))
+    halo_b = lax.ppermute(send_b, "quad", pairs(quads, 1))
+    outer_in, sub_in, send_1_in, send_2_in, rim, gram_in = call_inner(vec, halo_a, log_own)
+    outer, sub_edge, send_1, send_2 = call_edge(
+        halo_b, log_own, rim, gram_in, outer_in, send_1_in, send_2_in
+    )
+
+    ends, mates = [(0, 0), (3, 3)], [(1, 0), (2, 3)]
+
+    def across(block, first, routes):
+        return lax.ppermute(
+            block,
+            ("patch", "quad"),
+            [
+                (quads * i + a, quads * j + b)
+                for i, j in pairs(patches, first)
+                for a, b in routes
+            ],
+        )
+
+    mate_2 = across(send_2, 1, mates)
+    mate_1 = across(send_1, 0, mates)
+    chip_mate = lax.ppermute(outer, "quad", mates)
+    end_2 = across(send_2, 1, ends)
+    end_1 = across(send_1, 0, ends)
+    packed = call_product(end_2, mate_2, end_1, mate_1, chip_mate, outer)
+    far = lax.ppermute(packed, "quad", [(0, 2), (3, 1)])
+    near = lax.ppermute(packed, "quad", [(0, 1), (3, 2)])
+    passed = lax.ppermute(near + far, "quad", mates)
+    basis, coupling = call_final(near, far, passed, sub_in, sub_edge)
     return basis[None], coupling[None]
 
 

time: 50.8 us -> 53.6 us (1.055)
  waiting for transfers between devices: 6.75 us -> 17.4 us
  blocking collectives: 9.85 us -> 0 us
  starting transfers between devices: 16.5 us -> 18.8 us
    ppermute x4 -> x10, waiting for transfers between devices: 6.75 us -> 17.4 us  [the longest x1 11.2 us: on_device(): far = lax.ppermute(packed, 'quad', [(0, 2), (3, 1)])]
    all_gather x1 -> x0, blocking collectives: 9.85 us -> none  [on_device(): gathered = lax.all_gather(packed, 'quad')]
    ppermute x4 -> x10, starting transfers between devices: 16.5 us -> 18.8 us  [the longest x1 8.72 us: on_device(): halo_b = lax.ppermute(send_b, 'quad', pairs(quads, 1))]
  transfers between devices with their start and end apart: 4 -> 10, of which waited for: 2 -> 4; matrix products, arithmetic and copies ran while one was open for 0% -> 0% of each run, Pallas kernels for 17% -> 16%
where the time goes in v5:
time: 53.6 us; the launch traced here: 53.4 us
  starting transfers between devices  18.8 us (35%)
  waiting for transfers between devices  17.4 us (32%)
  Pallas kernels  16.4 us (31%)
  between operations  0.78 us (1%)
    ppermute x1, waiting for transfers between devices, on_device(): far = lax.ppermute(packed, 'quad', [(0, 2), (3, 1)])  11.2 us
    pallas_call x1, Pallas kernels, call_inner(): pl.pallas_call(functools.partial(inner_kernel, 'quad', 'patch'), out_shap...  8.79 us
    ppermute x1, starting transfers between devices, on_device(): halo_b = lax.ppermute(send_b, 'quad', pairs(quads, 1))  8.72 us
    ppermute x4, waiting for transfers between devices, across(): lax.ppermute(block, ('patch', 'quad'), [(quads * i + a, quads * j + b) fo...  5.31 us
    ppermute x4, starting transfers between devices, across(): lax.ppermute(block, ('patch', 'quad'), [(quads * i + a, quads * j + b) fo...  4.14 us
    pallas_call x1, Pallas kernels, call_final(): pl.pallas_call(functools.partial(final_kernel, 'quad', 'patch'), out_shap...  3.38 us
    pallas_call x1, Pallas kernels, call_edge(): pl.pallas_call(functools.partial(edge_kernel, 'quad', 'patch'), out_shape...  2.88 us
    ppermute x1, starting transfers between devices, on_device(): chip_mate = lax.ppermute(outer, 'quad', mates)  1.34 us
  transfers between devices with their start and end apart: 10, of which 4 were waited for; matrix products, arithmetic and copies ran while one was open for 0% of the time, Pallas kernels for 16%

profile of v5, /device:TPU:25, one launch (start us, length us, event | category | flops | bytes accessed | tf_op | source)
XLA Modules:
  0.0 53.4 jit_solution(10231515979073462595)
XLA Ops:
  0.6 0.0 copy-start.1
  0.6 0.0 copy-start
  0.6 1.3 %prepare.1 = (f32[25,8,512]{2,1,0:T(8,128)S(1)}, f32[25,8,512]{2,1,0:T(8,128)S(1)}) custom-call(f32[24,32,512]{2,1,0:T(8,128)} %bitcast.4, f32[32,512]{1,0:T(8,128)} %bitcast.6), custom_call_target="tpu_custom_call" | custom-call | tf_op jit(solution)/shard_map/prepare/pallas_call | solution.py:507
  2.0 0.8 %collective-permute-start.1 = (f32[25,8,512]{2,1,0:T(8,128)S(1)}, f32[25,8,512]{2,1,0:T(8,128)S(1)}, u32[]{:S(2)}, u32[]{:S(2)}) collective-permute-start(f32[25,8,512]{2,1,0:T(8,128)S(1)} %get-tuple-element.17), channel_id=1, source_target_pairs={{0,1},{2,3},{1,0},{3,2},{4,5},{6,7},{5,4},{7,6},{8,9},{10,11},{9,8... | collective-permute-start | bytes 1228808 | tf_op jit(solution)/shard_map/ppermute | solution.py:614
  2.7 8.7 %collective-permute-start = (f32[25,8,512]{2,1,0:T(8,128)S(1)}, f32[25,8,512]{2,1,0:T(8,128)S(1)}, u32[]{:S(2)}, u32[]{:S(2)}) collective-permute-start(f32[25,8,512]{2,1,0:T(8,128)S(1)} %get-tuple-element.16), channel_id=1, source_target_pairs={{1,2},{2,1},{5,6},{6,5},{9,10},{10,9},{13,14},{14,13},{17,18},{18,... | collective-permute-start | bytes 1228808 | tf_op jit(solution)/shard_map/ppermute | solution.py:615
  11.4 0.0 collective-permute-done.1.halo_a
  11.5 0.0 copy-done.1
  11.5 0.0 copy-done
  11.5 8.8 %inner.1 = (f32[2,24,24,128]{3,2,1,0:T(8,128)S(1)}, f32[24,24,256]{2,1,0:T(8,128)S(1)}, f32[24,24,128]{2,1,0:T(8,128)S(1)}, f32[24,24,128]{2,1,0:T(8,128)S(1)}, ...) custom-call(f32[24,32,512]{2,1,0:T(8,128)S(1)} %bitcast.5, f32[25,8,512]{2,1,0:T(8,128)S(1)} %collective-permute-done.1.halo_a, ...), custom_call_target="tpu_custom_call" | custom-call | flops 37748736 | bytes 5242880 | tf_op jit(solution)/shard_map/inner/pallas_call | solution.py:525
  20.3 0.0 collective-permute-done.halo_b
  20.3 2.9 %edge.1 = (f32[2,33,24,128]{3,2,1,0:T(8,128)S(1)}, f32[8,24,256]{2,1,0:T(8,128)S(1)}, f32[33,24,128]{2,1,0:T(8,128)S(1)}, f32[33,24,128]{2,1,0:T(8,128)S(1)}) custom-call(f32[25,8,512]{2,1,0:T(8,128)S(1)} %collective-permute-done.halo_b, f32[32,512]{1,0:T(8,128)S(1)} %bitcast.8, f32[8,2,3,8,512]{4,3,2,1,0:T(8,128)S(1)} %get-tuple-element.18.rim, ...), custom_call_target="tpu_custom_call" | custom-call | tf_op jit(solution)/shard_map/edge/pallas_call | solution.py:556
  23.2 1.3 %collective-permute-start.6 = (f32[2,33,24,128]{3,2,1,0:T(8,128)S(1)}, f32[2,33,24,128]{3,2,1,0:T(8,128)S(1)}, u32[]{:S(2)}, u32[]{:S(2)}) collective-permute-start(f32[2,33,24,128]{3,2,1,0:T(8,128)S(1)} %get-tuple-element.25.mine), channel_id=1, source_target_pairs={{1,0},{2,3},{5,4},{6,7},{9,8},{10,11},{13,12},{14,15},{17,16},{18,... | collective-permute-start | bytes 2433032 | tf_op jit(solution)/shard_map/ppermute | solution.py:636
  24.5 1.5 %collective-permute-start.3 = (f32[33,24,128]{2,1,0:T(8,128)S(1)}, f32[33,24,128]{2,1,0:T(8,128)S(1)}, u32[]{:S(2)}, u32[]{:S(2)}) collective-permute-start(f32[33,24,128]{2,1,0:T(8,128)S(1)} %get-tuple-element.23), channel_id=1, source_target_pairs={{5,8},{6,11},{13,16},{14,19},{21,24},{22,27},{29,32},{30,35},{37,4... | collective-permute-start | bytes 1216520 | tf_op jit(solution)/shard_map/ppermute | solution.py:624
  26.0 0.7 %collective-permute-start.2 = (f32[33,24,128]{2,1,0:T(8,128)S(1)}, f32[33,24,128]{2,1,0:T(8,128)S(1)}, u32[]{:S(2)}, u32[]{:S(2)}) collective-permute-start(f32[33,24,128]{2,1,0:T(8,128)S(1)} %get-tuple-element.23), channel_id=1, source_target_pairs={{4,8},{7,11},{12,16},{15,19},{20,24},{23,27},{28,32},{31,35},{36,4... | collective-permute-start | bytes 1216520 | tf_op jit(solution)/shard_map/ppermute | solution.py:624
  26.7 1.3 %collective-permute-start.5 = (f32[33,24,128]{2,1,0:T(8,128)S(1)}, f32[33,24,128]{2,1,0:T(8,128)S(1)}, u32[]{:S(2)}, u32[]{:S(2)}) collective-permute-start(f32[33,24,128]{2,1,0:T(8,128)S(1)} %get-tuple-element.24), channel_id=1, source_target_pairs={{1,4},{2,7},{9,12},{10,15},{17,20},{18,23},{25,28},{26,31},{33,36}... | collective-permute-start | bytes 1216520 | tf_op jit(solution)/shard_map/ppermute | solution.py:624
  28.0 0.7 %collective-permute-start.4 = (f32[33,24,128]{2,1,0:T(8,128)S(1)}, f32[33,24,128]{2,1,0:T(8,128)S(1)}, u32[]{:S(2)}, u32[]{:S(2)}) collective-permute-start(f32[33,24,128]{2,1,0:T(8,128)S(1)} %get-tuple-element.24), channel_id=1, source_target_pairs={{0,4},{3,7},{8,12},{11,15},{16,20},{19,23},{24,28},{27,31},{32,36}... | collective-permute-start | bytes 1216520 | tf_op jit(solution)/shard_map/ppermute | solution.py:624
  28.7 4.5 %collective-permute-done.3.left_pair_mate = f32[33,24,128]{2,1,0:T(8,128)S(1)} collective-permute-done((f32[33,24,128]{2,1,0:T(8,128)S(1)}, f32[33,24,128]{2,1,0:T(8,128)S(1)}, u32[]{:S(2)}, u32[]{:S(2)}) %collective-permute-start.3) | collective-permute-done | bytes 405536 | tf_op jit(solution)/shard_map/ppermute | solution.py:624
  33.2 0.0 collective-permute-done.2.left_pair
  33.2 0.8 %collective-permute-done.5.right_pair_mate = f32[33,24,128]{2,1,0:T(8,128)S(1)} collective-permute-done((f32[33,24,128]{2,1,0:T(8,128)S(1)}, f32[33,24,128]{2,1,0:T(8,128)S(1)}, u32[]{:S(2)}, u32[]{:S(2)}) %collective-permute-start.5) | collective-permute-done | bytes 405536 | tf_op jit(solution)/shard_map/ppermute | solution.py:624
  34.0 0.0 collective-permute-done.4.right_pair
  34.0 0.0 collective-permute-done.6.chip_mate
  34.0 1.3 %collective-permute-start.8 = (f32[24,128]{1,0:T(8,128)S(1)}, f32[24,128]{1,0:T(8,128)S(1)}, u32[]{:S(2)}, u32[]{:S(2)}) collective-permute-start(f32[24,128]{1,0:T(8,128)S(1)} %product.1), channel_id=1, source_target_pairs={{0,2},{3,1},{4,6},{7,5},{8,10},{11,9},{12,14},{15,13},{16,18},{19,... | collective-permute-start | bytes 36872 | tf_op jit(solution)/shard_map/ppermute | solution.py:640
  35.3 1.3 %collective-permute-start.7 = (f32[24,128]{1,0:T(8,128)S(1)}, f32[24,128]{1,0:T(8,128)S(1)}, u32[]{:S(2)}, u32[]{:S(2)}) collective-permute-start(f32[24,128]{1,0:T(8,128)S(1)} %product.1), channel_id=1, source_target_pairs={{0,1},{3,2},{4,5},{7,6},{8,9},{11,10},{12,13},{15,14},{16,17},{19,... | collective-permute-start | bytes 36872 | tf_op jit(solution)/shard_map/ppermute | solution.py:641
  36.6 11.2 %collective-permute-done.8.far = f32[24,128]{1,0:T(8,128)S(1)} collective-permute-done((f32[24,128]{1,0:T(8,128)S(1)}, f32[24,128]{1,0:T(8,128)S(1)}, u32[]{:S(2)}, u32[]{:S(2)}) %collective-permute-start.8) | collective-permute-done | bytes 12320 | tf_op jit(solution)/shard_map/ppermute | solution.py:640
  47.9 0.0 collective-permute-done.7.near
  47.9 1.3 %collective-permute-start.9 = (f32[24,128]{1,0:T(8,128)S(1)}, f32[24,128]{1,0:T(8,128)S(1)}, u32[]{:S(2)}, u32[]{:S(2)}) collective-permute-start(f32[24,128]{1,0:T(8,128)S(1)} %add.3), channel_id=1, source_target_pairs={{1,0},{2,3},{5,4},{6,7},{9,8},{10,11},{13,12},{14,15},{17,16},{18,... | collective-permute-start | bytes 36872 | tf_op jit(solution)/shard_map/ppermute | solution.py:642
  49.2 0.8 %collective-permute-done.9.passed = f32[24,128]{1,0:T(8,128)S(1)} collective-permute-done((f32[24,128]{1,0:T(8,128)S(1)}, f32[24,128]{1,0:T(8,128)S(1)}, u32[]{:S(2)}, u32[]{:S(2)}) %collective-permute-start.9) | collective-permute-done | bytes 12320 | tf_op jit(solution)/shard_map/ppermute | solution.py:642
  50.0 3.4 %final.1 = (f32[24,32,256]{2,1,0:T(8,128)}, f32[2,24,24]{2,1,0:T(8,128)}) custom-call(f32[24,128]{1,0:T(8,128)S(1)} %collective-permute-done.7.near, f32[24,128]{1,0:T(8,128)S(1)} %collective-permute-done.8.far, f32[24,128]{1,0:T(8,128)S(1)} %collective-permute-done.9.passed, f32[24,24,256]{2,1,0:T(8,128)S(1)} %get-tuple-element.26.sub_in, ...), custom_call_target="tpu_custom_call" | custom-call | tf_op jit(solution)/shard_map/final/pallas_call | solution.py:592
  (2 shorter events, 0.0 us)
Async XLA Ops:
  0.6 10.8 %copy-start.1 = (f32[1,32,512]{2,1,0:T(8,128)S(1)}, f32[1,32,512]{2,1,0:T(8,128)}, u32[]{:S(2)}) copy-start(f32[1,32,512]{2,1,0:T(8,128)} %param.3) | copy-start | bytes 196612
  0.6 10.8 %copy-start = (f32[1,24,32,512]{3,2,1,0:T(8,128)S(1)}, f32[1,24,32,512]{3,2,1,0:T(8,128)}, u32[]{:S(2)}) copy-start(f32[1,24,32,512]{3,2,1,0:T(8,128)} %param.2) | copy-start | bytes 4718596
  2.0 9.5 %collective-permute-start.1 = (f32[25,8,512]{2,1,0:T(8,128)S(1)}, f32[25,8,512]{2,1,0:T(8,128)S(1)}, u32[]{:S(2)}, u32[]{:S(2)}) collective-permute-start(f32[25,8,512]{2,1,0:T(8,128)S(1)} %get-tuple-element.17), channel_id=1, source_target_pairs={{0,1},{2,3},{1,0},{3,2},{4,5},{6,7},{5,4},{7,6},{8,9},{10,11},{9,8... | collective-permute-start | bytes 1228808 | tf_op jit(solution)/shard_map/ppermute | solution.py:614
  2.7 17.6 %collective-permute-start = (f32[25,8,512]{2,1,0:T(8,128)S(1)}, f32[25,8,512]{2,1,0:T(8,128)S(1)}, u32[]{:S(2)}, u32[]{:S(2)}) collective-permute-start(f32[25,8,512]{2,1,0:T(8,128)S(1)} %get-tuple-element.16), channel_id=1, source_target_pairs={{1,2},{2,1},{5,6},{6,5},{9,10},{10,9},{13,14},{14,13},{17,18},{18,... | collective-permute-start | bytes 1228808 | tf_op jit(solution)/shard_map/ppermute | solution.py:615
  23.2 10.8 %collective-permute-start.6 = (f32[2,33,24,128]{3,2,1,0:T(8,128)S(1)}, f32[2,33,24,128]{3,2,1,0:T(8,128)S(1)}, u32[]{:S(2)}, u32[]{:S(2)}) collective-permute-start(f32[2,33,24,128]{3,2,1,0:T(8,128)S(1)} %get-tuple-element.25.mine), channel_id=1, source_target_pairs={{1,0},{2,3},{5,4},{6,7},{9,8},{10,11},{13,12},{14,15},{17,16},{18,... | collective-permute-start | bytes 2433032 | tf_op jit(solution)/shard_map/ppermute | solution.py:636
  24.5 8.7 %collective-permute-start.3 = (f32[33,24,128]{2,1,0:T(8,128)S(1)}, f32[33,24,128]{2,1,0:T(8,128)S(1)}, u32[]{:S(2)}, u32[]{:S(2)}) collective-permute-start(f32[33,24,128]{2,1,0:T(8,128)S(1)} %get-tuple-element.23), channel_id=1, source_target_pairs={{5,8},{6,11},{13,16},{14,19},{21,24},{22,27},{29,32},{30,35},{37,4... | collective-permute-start | bytes 1216520 | tf_op jit(solution)/shard_map/ppermute | solution.py:624
  26.0 7.2 %collective-permute-start.2 = (f32[33,24,128]{2,1,0:T(8,128)S(1)}, f32[33,24,128]{2,1,0:T(8,128)S(1)}, u32[]{:S(2)}, u32[]{:S(2)}) collective-permute-start(f32[33,24,128]{2,1,0:T(8,128)S(1)} %get-tuple-element.23), channel_id=1, source_target_pairs={{4,8},{7,11},{12,16},{15,19},{20,24},{23,27},{28,32},{31,35},{36,4... | collective-permute-start | bytes 1216520 | tf_op jit(solution)/shard_map/ppermute | solution.py:624
  26.7 7.3 %collective-permute-start.5 = (f32[33,24,128]{2,1,0:T(8,128)S(1)}, f32[33,24,128]{2,1,0:T(8,128)S(1)}, u32[]{:S(2)}, u32[]{:S(2)}) collective-permute-start(f32[33,24,128]{2,1,0:T(8,128)S(1)} %get-tuple-element.24), channel_id=1, source_target_pairs={{1,4},{2,7},{9,12},{10,15},{17,20},{18,23},{25,28},{26,31},{33,36}... | collective-permute-start | bytes 1216520 | tf_op jit(solution)/shard_map/ppermute | solution.py:624
  28.0 6.0 %collective-permute-start.4 = (f32[33,24,128]{2,1,0:T(8,128)S(1)}, f32[33,24,128]{2,1,0:T(8,128)S(1)}, u32[]{:S(2)}, u32[]{:S(2)}) collective-permute-start(f32[33,24,128]{2,1,0:T(8,128)S(1)} %get-tuple-element.24), channel_id=1, source_target_pairs={{0,4},{3,7},{8,12},{11,15},{16,20},{19,23},{24,28},{27,31},{32,36}... | collective-permute-start | bytes 1216520 | tf_op jit(solution)/shard_map/ppermute | solution.py:624
  34.0 13.8 %collective-permute-start.8 = (f32[24,128]{1,0:T(8,128)S(1)}, f32[24,128]{1,0:T(8,128)S(1)}, u32[]{:S(2)}, u32[]{:S(2)}) collective-permute-start(f32[24,128]{1,0:T(8,128)S(1)} %product.1), channel_id=1, source_target_pairs={{0,2},{3,1},{4,6},{7,5},{8,10},{11,9},{12,14},{15,13},{16,18},{19,... | collective-permute-start | bytes 36872 | tf_op jit(solution)/shard_map/ppermute | solution.py:640
  35.3 12.5 %collective-permute-start.7 = (f32[24,128]{1,0:T(8,128)S(1)}, f32[24,128]{1,0:T(8,128)S(1)}, u32[]{:S(2)}, u32[]{:S(2)}) collective-permute-start(f32[24,128]{1,0:T(8,128)S(1)} %product.1), channel_id=1, source_target_pairs={{0,1},{3,2},{4,5},{7,6},{8,9},{11,10},{12,13},{15,14},{16,17},{19,... | collective-permute-start | bytes 36872 | tf_op jit(solution)/shard_map/ppermute | solution.py:641
  47.9 2.1 %collective-permute-start.9 = (f32[24,128]{1,0:T(8,128)S(1)}, f32[24,128]{1,0:T(8,128)S(1)}, u32[]{:S(2)}, u32[]{:S(2)}) collective-permute-start(f32[24,128]{1,0:T(8,128)S(1)} %add.3), channel_id=1, source_target_pairs={{1,0},{2,3},{5,4},{6,7},{9,8},{10,11},{13,12},{14,15},{17,16},{18,... | collective-permute-start | bytes 36872 | tf_op jit(solution)/shard_map/ppermute | solution.py:642

commit v6 on v3

--- a/solution.py
+++ b/solution.py
@@ -25,6 +25,7 @@
 LANES = 128
 CHUNK = 8
 PAD = 8
+STEP = 8
 
 PARAMS = pltpu.CompilerParams(vmem_limit_bytes=40 * 1024 * 1024)
 ANY = pl.BlockSpec(memory_space=pl.ANY)
@@ -164,46 +165,18 @@
     row_loop(first, last, CHUNK, body)
 
 
-def fetch_columns(source, slabs, sems, rows=0):
-    copies = []
-    for k in range(slabs.shape[0]):
-        copy = pltpu.make_async_copy(
-            source.at[:, pl.ds(rows, 8), pl.ds(LANES * k, LANES)],
-            slabs.at[k, :, pl.ds(rows, 8)],
-            sems.at[k],
-        )
-        copy.start()
-        copies.append(copy)
-    return copies
-
-
-def wait_all(copies):
-    for copy in copies:
-        copy.wait()
-
-
-def rows_of_fields(slabs, rows, groups):
-    height = slabs.shape[2]
-    pieces = []
-    for r in rows:
-        for g in range(groups):
-            parts = []
-            for k in range(slabs.shape[0]):
-                flat = slabs.at[k].reshape(slabs.shape[1] * height, LANES)
-                parts.append(flat[pl.ds(8 * height * g + r, 8, stride=height), :])
-            pieces.append(jnp.concatenate(parts, axis=1))
-    return jnp.concatenate(pieces, axis=0)
-
-
-def field_block(slabs, field):
-    return jnp.concatenate([slabs[k, field] for k in range(slabs.shape[0])], axis=1)
-
-
-def load_rows(slabs, target, first, natural_row, groups, matrix):
-    rows = [natural_row(k) for k in range(8)]
-    x = permute_columns(rows_of_fields(slabs, rows, groups), matrix)
-    width = x.shape[1]
-    target[pl.ds(first, 8)] = x.reshape(8, groups, 8, width)
+def load_rows(fields, mixed, target, first, odd, matrix):
+    count, rows, width = fields.shape
+    x = permute_columns(fields.reshape(count * rows, width), matrix)
+    for k, block in enumerate(blocks_of(x)):
+        mixed[k] = block
+    for i in range(rows):
+        r = jnp.where(odd == 1, rows - 1 - i, i)
+        for g in range(count // 8):
+            parts = [
+                mixed[k, pl.ds(8 * rows * g + r, 8, stride=rows), :] for k in range(BLOCKS)
+            ]
+            target[first + i, g] = jnp.concatenate(parts, axis=1)
 
 
 def emit(final, first, count, groups, matrix, swap, outs, out_first):
@@ -250,8 +223,8 @@
 
 def inner_kernel(
     quad, patch, vec, halo_a, log_kappa,
-    outer_left, outer_right, sub, send_right, send_left, rim, gram,
-    even, odd_buf, weights, vec_slabs, halo_slabs, logs, natural, sems,
+    outer_left, outer_right, sub, send_right, send_left, rim, gram, own_weights, forth, back,
+    even, odd_buf, weights, mixed, logs, natural,
 ):
     odd = lax.rem(lax.axis_index(quad), 2)
     swap = lax.rem(lax.axis_index(patch), 2) == 1
@@ -260,21 +233,12 @@
     count = 8 * groups
     width = even.shape[-1]
 
-    def own_block(b):
-        return jnp.where(odd == 1, height // 8 - 1 - b, b)
-
-    blocks = height // 8
-    halo_copies = fetch_columns(halo_a, halo_slabs, sems.at[blocks])
-    block_copies = [
-        fetch_columns(vec, vec_slabs, sems.at[b], pl.multiple_of(own_block(b) * 8, 8))
-        for b in range(blocks)
-    ]
     matrix = permutation(width, False)
+    forth[...] = matrix
     logs[...] = jnp.zeros(logs.shape, f32)
     logs[pl.ds(16, height)] = permute_columns(log_kappa[...], matrix)
-    wait_all(halo_copies)
     below = pl.multiple_of(8 + (1 - odd) * (height + 8), 8)
-    logs[pl.ds(below, 8)] = permute_columns(field_block(halo_slabs, count), matrix)
+    logs[pl.ds(below, 8)] = permute_columns(halo_a[count], matrix)
     values = face_weights(logs[...], 1.0)
     for i in range(4):
         natural[i] = values[i]
@@ -282,18 +246,14 @@
     def natural_row(k):
         return jnp.where(odd == 1, height + 7 - k, k + 8)
 
-    def own_row(k):
-        return jnp.where(odd == 1, height - 1 - k, k)
-
-    load_rows(
-        halo_slabs, even, height, lambda k: jnp.where(odd == 1, 7 - k, k), groups, matrix
-    )
-    for block in range(blocks):
-        wait_all(block_copies[block])
+    load_rows(halo_a[pl.ds(0, count)], mixed.at[0], even, height, odd, matrix)
+    for block in range(height // 8):
+        own = pl.multiple_of(8 * jnp.where(odd == 1, height // 8 - 1 - block, block), 8)
         load_rows(
-            vec_slabs, even, 8 * block, lambda k: own_row(8 * block + k), groups, matrix
+            vec[:, pl.ds(own, 8), :], mixed.at[block + 1], even, 8 * block, odd, matrix
         )
     spread_weights(natural, weights, total - 2, lambda k: natural_row(k + 1), odd)
+    own_weights[...] = weights[pl.ds(0, SWEEPS - 1)]
 
     bufs = (even, odd_buf)
     for level in range(1, SWEEPS + 1):
@@ -303,12 +263,13 @@
         sweep(level, now, new, weights, level, total - level, 1)
 
     final = bufs[SWEEPS % 2]
-    back = permutation(width, True)
+    unmix = permutation(width, True)
+    back[...] = unmix
     outs = (outer_left, outer_right, sub, send_right, send_left)
 
     def finish(block, carry):
         row = pl.multiple_of(8 * block, 8)
-        emit(final, row + 8, count, groups, back, swap, outs, row)
+        emit(final, row + 8, count, groups, unmix, swap, outs, row)
         return carry
 
     lax.fori_loop(0, (height - SWEEPS) // 8, finish, 0, unroll=True)
@@ -317,9 +278,9 @@
 
 
 def edge_kernel(
-    quad, patch, halo_b, log_kappa, rim, gram_inner, send_right_in, send_left_in,
-    outer_left, outer_right, sub, send_right, send_left,
-    even, odd_buf, weights, halo_slabs, logs, natural, sems,
+    quad, patch, halo_b, log_kappa, rim, gram_inner, own_weights, forth, back,
+    send_right_in, send_left_in, outer_left, outer_right, sub, send_right, send_left,
+    even, odd_buf, weights, mixed, logs, natural,
 ):
     index = lax.axis_index(quad)
     odd = lax.rem(index, 2)
@@ -330,27 +291,24 @@
     width = even.shape[-1]
     height = log_kappa.shape[0]
     count = 8 * groups
-    halo_copies = fetch_columns(halo_b, halo_slabs, sems)
-    matrix = permutation(width, False)
+    matrix = forth[...]
     logs[...] = jnp.zeros(logs.shape, f32)
     own_at = pl.multiple_of(odd * (height - 16), 8)
     place = pl.multiple_of(16 - 8 * odd, 8)
     logs[pl.ds(place, 16)] = permute_columns(log_kappa[pl.ds(own_at, 16), :], matrix)
-    wait_all(halo_copies)
     halo_at = pl.multiple_of(8 + 16 * odd, 8)
-    logs[pl.ds(halo_at, 8)] = permute_columns(field_block(halo_slabs, count), matrix)
+    logs[pl.ds(halo_at, 8)] = permute_columns(halo_b[count], matrix)
     position = lax.broadcasted_iota(jnp.int32, (24, width), 0)
     outside = jnp.logical_and(position >= 16 * odd, position < 8 + 16 * odd)
     values = face_weights(logs[...], jnp.where(outside, alive, 1.0))
     for i in range(4):
         natural[i] = values[i]
 
-    load_rows(
-        halo_slabs, even, 0, lambda k: jnp.where(odd == 1, 7 - k, k), groups, matrix
-    )
+    load_rows(halo_b[pl.ds(0, count)], mixed, even, 0, odd, matrix)
     spread_weights(
-        natural, weights, 15, lambda k: jnp.where(odd == 1, 22 - k, k + 1), odd
-    )
+        natural, weights, SWEEPS, lambda k: jnp.where(odd == 1, 22 - k, k + 1), odd
+    )
+    weights[pl.ds(SWEEPS, SWEEPS - 1)] = own_weights[...]
 
     bufs = (even, odd_buf)
     for level in range(1, SWEEPS + 1):
@@ -360,8 +318,7 @@
         sweep(level, now, new, weights, level, level + SWEEPS, 1)
 
     final = bufs[SWEEPS % 2]
-    back = permutation(width, True)
-    emit(final, SWEEPS, count, groups, back, swap, (outer_left, outer_right, sub, send_right, send_left), 0)
+    emit(final, SWEEPS, count, groups, back[...], swap, (outer_left, outer_right, sub, send_right, send_left), 0)
     x = rows_as_columns(sub, 0, SWEEPS)
     total = gram_inner[...] + gram_product(x, x)
     inner = height - SWEEPS
@@ -413,19 +370,22 @@
     lane = lax.broadcasted_iota(jnp.int32, (count, lanes), 1)
     zeros = jnp.zeros((count, lanes - 2 * count), f32)
     works = [jnp.concatenate([mat, eye, zeros], axis=1) for mat in mats]
-    for j in range(0, count, 2):
+    for j in range(0, count, STEP):
         for m, work in enumerate(works):
-            first = jnp.broadcast_to(work[:, j : j + 1], (count, lanes))
-            second = jnp.broadcast_to(work[:, j + 1 : j + 2], (count, lanes))
-            a, b, c = first[j : j + 1], second[j : j + 1], second[j + 1 : j + 2]
-            row_j = work[j : j + 1]
-            over_a = 1.0 / a
-            part = b * over_a
-            row_next = work[j + 1 : j + 2] - part * row_j
-            over_c = 1.0 / (c - part * b)
-            change = first * (row_j * over_a) + (second - first * part) * (row_next * over_c)
-            work = jnp.where(sub > j + 1, work - change, work)
-            works[m] = jnp.where(sub == j + 1, row_next, work)
+            cols = [jnp.broadcast_to(work[:, k : k + 1], (count, lanes)) for k in range(j, j + STEP)]
+            rows = [work[k : k + 1] for k in range(j, j + STEP)]
+            change = jnp.zeros_like(work)
+            for i in range(STEP):
+                over = 1.0 / cols[i][j + i : j + i + 1]
+                scaled = rows[i] * over
+                for k in range(i + 1, STEP):
+                    rows[k] = rows[k] - cols[i][j + k : j + k + 1] * scaled
+                    cols[k] = cols[k] - cols[i] * (cols[k][j + i : j + i + 1] * over)
+                change = change + cols[i] * scaled
+            work = jnp.where(sub >= j + STEP, work - change, work)
+            for i in range(1, STEP):
+                work = jnp.where(sub == j + i, rows[i], work)
+            works[m] = work
     out = []
     for work in works:
         diagonal = jnp.sum(jnp.where(sub == lane, work, 0.0), axis=1, keepdims=True)
@@ -486,7 +446,8 @@
             copies.append(copy)
     coupling[0] = dot_nt(dot_nn(own, mats[3], highest), left, highest)
     coupling[1] = dot_nt(dot_nn(own, mats[4], highest), right, highest)
-    wait_all(copies)
+    for copy in copies:
+        copy.wait()
 
 
 def call_prepare(vec, log_own):
@@ -519,25 +480,25 @@
             shape(inner, count, band),
             shape(SWEEPS, 2, groups, 8, width),
             shape(count, count),
+            shape(SWEEPS - 1, 4, 8, width),
+            jax.ShapeDtypeStruct((width, width), bf16),
+            jax.ShapeDtypeStruct((width, width), bf16),
         ),
         scratch_shapes=[
             pltpu.VMEM((total, groups, 8, width), f32),
             pltpu.VMEM((total, groups, 8, width), f32),
             pltpu.VMEM((total - 2, 4, 8, width), f32),
-            pltpu.VMEM((width // LANES, count, height + PAD, LANES), f32),
-            pltpu.VMEM((width // LANES, count + 1, SWEEPS, LANES), f32),
+            pltpu.VMEM((height // 8 + 1, BLOCKS, 8 * count, LANES), f32),
             pltpu.VMEM((height + 32, width), f32),
             pltpu.VMEM((4, height + 16, width), f32),
-            pltpu.SemaphoreType.DMA((height // 8 + 1, width // LANES)),
         ],
-        in_specs=[ANY, ANY, VMEM],
         compiler_params=PARAMS,
         cost_estimate=pl.CostEstimate(flops=cost, bytes_accessed=5 << 20, transcendentals=0),
         name="inner",
     )(vec, halo_a, log_own)
 
 
-def call_edge(halo_b, log_own, rim, gram_inner, send_right, send_left):
+def call_edge(halo_b, log_own, rim, gram_inner, own_weights, forth, back, send_right, send_left):
     height, width = log_own.shape
     inner, count, band = send_right.shape
     groups = count // 8
@@ -554,15 +515,13 @@
             pltpu.VMEM((2 * SWEEPS + 1, groups, 8, width), f32),
             pltpu.VMEM((2 * SWEEPS + 1, groups, 8, width), f32),
             pltpu.VMEM((2 * SWEEPS - 1, 4, 8, width), f32),
-            pltpu.VMEM((width // LANES, count + 1, SWEEPS, LANES), f32),
+            pltpu.VMEM((BLOCKS, 8 * count, LANES), f32),
             pltpu.VMEM((40, width), f32),
             pltpu.VMEM((4, 24, width), f32),
-            pltpu.SemaphoreType.DMA((width // LANES,)),
         ],
-        in_specs=[ANY] + [VMEM] * 5,
         compiler_params=PARAMS,
         name="edge",
-    )(halo_b, log_own, rim, gram_inner, send_right, send_left)
+    )(halo_b, log_own, rim, gram_inner, own_weights, forth, back, send_right, send_left)
 
 
 def call_product(left_in, left_edge, right_in, right_edge, from_right_pair, from_left_pair, sent):
@@ -602,11 +561,9 @@
     send_a, send_b = call_prepare(vec, log_own)
     halo_a = lax.ppermute(send_a, "quad", pairs(quad_size, 0))
     halo_b = lax.ppermute(send_b, "quad", pairs(quad_size, 1))
-    left_in, right_in, sub_in, send_1_in, send_2_in, rim, gram_in = call_inner(
-        vec, halo_a, log_own
-    )
+    left_in, right_in, sub_in, send_1_in, send_2_in, *for_edge = call_inner(vec, halo_a, log_own)
     left_edge, right_edge, sub_edge, send_1, send_2 = call_edge(
-        halo_b, log_own, rim, gram_in, send_1_in, send_2_in
+        halo_b, log_own, *for_edge, send_1_in, send_2_in
     )
     from_2 = lax.ppermute(send_2, "patch", pairs(patch_size, 1))
     from_1 = lax.ppermute(send_1, "patch", pairs(patch_size, 0))

time: 50.8 us -> 49.7 us (0.978)
  Pallas kernels: 16.8 us -> 15.1 us
  starting transfers between devices: 16.5 us -> 17.1 us
    pallas_call x1, Pallas kernels: 3.38 us -> 2.67 us  [call_final(): pl.pallas_call(functools.partial(final_kernel, 'quad', 'patch'), out_shap...]
    ppermute x1, waiting for transfers between devices: 0.3 us -> 0.93 us  [on_device(): from_1 = lax.ppermute(send_1, 'patch', pairs(patch_size, 0))]
    ppermute x1, waiting for transfers between devices: 6.44 us -> 5.81 us  [on_device(): from_2 = lax.ppermute(send_2, 'patch', pairs(patch_size, 1))]
    pallas_call x1, Pallas kernels: 8.79 us -> 8.17 us  [call_inner(): pl.pallas_call(functools.partial(inner_kernel, 'quad', 'patch'), out_shap...]
    ppermute x1, starting transfers between devices: 6.91 us -> 7.53 us  [on_device(): from_2 = lax.ppermute(send_2, 'patch', pairs(patch_size, 1))]
  transfers between devices with their start and end apart: 4 -> 4, of which waited for: 2 -> 2; matrix products, arithmetic and copies ran while one was open for 0% -> 0% of each run, Pallas kernels for 17% -> 16%
where the time goes in v6:
time: 49.7 us; the launch traced here: 49.6 us
  starting transfers between devices  17.1 us (34%)
  Pallas kernels  15.1 us (30%)
  blocking collectives  9.85 us (20%)
  waiting for transfers between devices  6.75 us (14%)
  between operations  0.7 us (1%)
    all_gather x1, blocking collectives, on_device(): gathered = lax.all_gather(packed, 'quad')  9.85 us
    ppermute x1, starting transfers between devices, on_device(): halo_b = lax.ppermute(send_b, 'quad', pairs(quad_size, 1))  8.72 us
    pallas_call x1, Pallas kernels, call_inner(): pl.pallas_call(functools.partial(inner_kernel, 'quad', 'patch'), out_shap...  8.17 us
    ppermute x1, starting transfers between devices, on_device(): from_2 = lax.ppermute(send_2, 'patch', pairs(patch_size, 1))  7.53 us
    ppermute x1, waiting for transfers between devices, on_device(): from_2 = lax.ppermute(send_2, 'patch', pairs(patch_size, 1))  5.81 us
    pallas_call x1, Pallas kernels, call_final(): pl.pallas_call(functools.partial(final_kernel, 'quad', 'patch'), out_shap...  2.67 us
    pallas_call x1, Pallas kernels, call_edge(): pl.pallas_call(functools.partial(edge_kernel, 'quad', 'patch'), out_shape...  2.51 us
    pallas_call x1, Pallas kernels, call_prepare(): pl.pallas_call(functools.partial(prepare_kernel, 'quad'), out_shape=(shap...  1.3 us
  transfers between devices with their start and end apart: 4, of which 2 were waited for; matrix products, arithmetic and copies ran while one was open for 0% of the time, Pallas kernels for 16%

profile of v6, /device:TPU:25, one launch (start us, length us, event | category | flops | bytes accessed | tf_op | source)
XLA Modules:
  0.0 49.6 jit_solution(16514922098653105037)
XLA Ops:
  0.6 0.0 copy-start.1
  0.6 0.0 copy-start
  0.6 1.3 %prepare.1 = (f32[25,8,512]{2,1,0:T(8,128)S(1)}, f32[25,8,512]{2,1,0:T(8,128)S(1)}) custom-call(f32[24,32,512]{2,1,0:T(8,128)} %bitcast.5, f32[32,512]{1,0:T(8,128)} %bitcast.7), custom_call_target="tpu_custom_call" | custom-call | tf_op jit(solution)/shard_map/prepare/pallas_call | solution.py:455
  2.0 0.8 %collective-permute-start = (f32[25,8,512]{2,1,0:T(8,128)S(1)}, f32[25,8,512]{2,1,0:T(8,128)S(1)}, u32[]{:S(2)}, u32[]{:S(2)}) collective-permute-start(f32[25,8,512]{2,1,0:T(8,128)S(1)} %get-tuple-element.21), channel_id=1, source_target_pairs={{0,1},{2,3},{1,0},{3,2},{4,5},{6,7},{5,4},{7,6},{8,9},{10,11},{9,8... | collective-permute-start | bytes 1228808 | tf_op jit(solution)/shard_map/ppermute | solution.py:562
  2.7 8.7 %collective-permute-start.1 = (f32[25,8,512]{2,1,0:T(8,128)S(1)}, f32[25,8,512]{2,1,0:T(8,128)S(1)}, u32[]{:S(2)}, u32[]{:S(2)}) collective-permute-start(f32[25,8,512]{2,1,0:T(8,128)S(1)} %get-tuple-element.23), channel_id=1, source_target_pairs={{1,2},{2,1},{5,6},{6,5},{9,10},{10,9},{13,14},{14,13},{17,18},{18,... | collective-permute-start | bytes 1228808 | tf_op jit(solution)/shard_map/ppermute | solution.py:563
  11.4 0.0 collective-permute-done.halo_a
  11.5 0.0 copy-done.1
  11.5 0.0 copy-done
  11.5 8.2 %inner.1 = (f32[24,24,128]{2,1,0:T(8,128)S(1)}, f32[24,24,128]{2,1,0:T(8,128)S(1)}, f32[24,24,256]{2,1,0:T(8,128)S(1)}, f32[24,24,128]{2,1,0:T(8,128)S(1)}, f32[...) custom-call(f32[24,32,512]{2,1,0:T(8,128)S(1)} %bitcast.6, ...), custom_call_target="tpu_custom_call" | custom-call | flops 37748736 | bytes 5242880 | tf_op jit(solution)/shard_map/inner/pallas_call | solution.py:473
  19.6 0.0 collective-permute-done.1.halo_b
  19.6 2.5 %edge.1 = (f32[8,24,128]{2,1,0:T(8,128)S(1)}, f32[8,24,128]{2,1,0:T(8,128)S(1)}, f32[8,24,256]{2,1,0:T(8,128)S(1)}, f32[33,24,128]{2,1,0:T(8,128)S(1)}, f32[33,24,128]{2,1,0:T(8,128)S(1)}) custom-call(f32[25,8,512]{2,1,0:T(8,128)S(1)} %collective-permute-done.1.halo_b, f32[32,512]{1,0:T(8,128)S(1)} %bitcast.9, ...), custom_call_target="tpu_custom_call" | custom-call | tf_op jit(solution)/shard_map/edge/pallas_call | solution.py:505
  22.2 7.5 %collective-permute-start.3 = (f32[33,24,128]{2,1,0:T(8,128)S(1)}, f32[33,24,128]{2,1,0:T(8,128)S(1)}, u32[]{:S(2)}, u32[]{:S(2)}) collective-permute-start(f32[33,24,128]{2,1,0:T(8,128)S(1)} %get-tuple-element.35), channel_id=1, source_target_pairs={{4,8},{12,16},{20,24},{28,32},{36,40},{44,48},{52,56},{60,64},{68,... | collective-permute-start | bytes 1216520 | tf_op jit(solution)/shard_map/ppermute | solution.py:568
  29.7 0.1 collective-permute-start.2
  29.8 5.8 %collective-permute-done.3.from_left_pair = f32[33,24,128]{2,1,0:T(8,128)S(1)} collective-permute-done((f32[33,24,128]{2,1,0:T(8,128)S(1)}, f32[33,24,128]{2,1,0:T(8,128)S(1)}, u32[]{:S(2)}, u32[]{:S(2)}) %collective-permute-start.3) | collective-permute-done | bytes 405536 | tf_op jit(solution)/shard_map/ppermute | solution.py:568
  35.6 0.9 %collective-permute-done.2.from_right_pair = f32[33,24,128]{2,1,0:T(8,128)S(1)} collective-permute-done((f32[33,24,128]{2,1,0:T(8,128)S(1)}, f32[33,24,128]{2,1,0:T(8,128)S(1)}, u32[]{:S(2)}, u32[]{:S(2)}) %collective-permute-start.2) | collective-permute-done | bytes 405536 | tf_op jit(solution)/shard_map/ppermute | solution.py:569
  36.5 0.5 %product.1 = f32[24,128]{1,0:T(8,128)S(1)} custom-call(f32[24,24,128]{2,1,0:T(8,128)S(1)} %get-tuple-element.22.left_in, f32[8,24,128]{2,1,0:T(8,128)S(1)} %get-tuple-element.31.left_edge, f32[24,24,128]{2,1,0:T(8,128)S(1)} %get-tuple-element.32.right_in, f32[8,24,128]{2,1,0:T(8,128)S(1)} %get-tuple-element.33.right_edge, ...), custom_call_target="tpu_custom_call" | custom-call | tf_op jit(solution)/shard_map/product/pallas_call | solution.py:529
  37.0 9.9 %all-gather = f32[96,128]{1,0:T(8,128)S(1)} all-gather(f32[24,128]{1,0:T(8,128)S(1)} %product.1), channel_id=2, replica_groups=mesh['patch'=64,'quad'=4] {'quad'}, dimensions={0}, use_global_device_ids=true | all-gather | bytes 61440 | tf_op jit(solution)/shard_map/all_gather | solution.py:571
  46.9 2.7 %final.1 = (f32[24,32,256]{2,1,0:T(8,128)}, f32[2,24,24]{2,1,0:T(8,128)}) custom-call(f32[4,24,128]{2,1,0:T(8,128)S(1)} %bitcast.10, f32[24,24,256]{2,1,0:T(8,128)S(1)} %get-tuple-element.36.sub_in, f32[8,24,256]{2,1,0:T(8,128)S(1)} %get-tuple-element.37.sub_edge), custom_call_target="tpu_custom_call" | custom-call | tf_op jit(solution)/shard_map/final/pallas_call | solution.py:540
Async XLA Ops:
  0.6 10.8 %copy-start.1 = (f32[1,32,512]{2,1,0:T(8,128)S(1)}, f32[1,32,512]{2,1,0:T(8,128)}, u32[]{:S(2)}) copy-start(f32[1,32,512]{2,1,0:T(8,128)} %param.3) | copy-start | bytes 196612
  0.6 10.8 %copy-start = (f32[1,24,32,512]{3,2,1,0:T(8,128)S(1)}, f32[1,24,32,512]{3,2,1,0:T(8,128)}, u32[]{:S(2)}) copy-start(f32[1,24,32,512]{3,2,1,0:T(8,128)} %param.2) | copy-start | bytes 4718596
  2.0 9.5 %collective-permute-start = (f32[25,8,512]{2,1,0:T(8,128)S(1)}, f32[25,8,512]{2,1,0:T(8,128)S(1)}, u32[]{:S(2)}, u32[]{:S(2)}) collective-permute-start(f32[25,8,512]{2,1,0:T(8,128)S(1)} %get-tuple-element.21), channel_id=1, source_target_pairs={{0,1},{2,3},{1,0},{3,2},{4,5},{6,7},{5,4},{7,6},{8,9},{10,11},{9,8... | collective-permute-start | bytes 1228808 | tf_op jit(solution)/shard_map/ppermute | solution.py:562
  2.7 16.9 %collective-permute-start.1 = (f32[25,8,512]{2,1,0:T(8,128)S(1)}, f32[25,8,512]{2,1,0:T(8,128)S(1)}, u32[]{:S(2)}, u32[]{:S(2)}) collective-permute-start(f32[25,8,512]{2,1,0:T(8,128)S(1)} %get-tuple-element.23), channel_id=1, source_target_pairs={{1,2},{2,1},{5,6},{6,5},{9,10},{10,9},{13,14},{14,13},{17,18},{18,... | collective-permute-start | bytes 1228808 | tf_op jit(solution)/shard_map/ppermute | solution.py:563
  22.2 13.5 %collective-permute-start.3 = (f32[33,24,128]{2,1,0:T(8,128)S(1)}, f32[33,24,128]{2,1,0:T(8,128)S(1)}, u32[]{:S(2)}, u32[]{:S(2)}) collective-permute-start(f32[33,24,128]{2,1,0:T(8,128)S(1)} %get-tuple-element.35), channel_id=1, source_target_pairs={{4,8},{12,16},{20,24},{28,32},{36,40},{44,48},{52,56},{60,64},{68,... | collective-permute-start | bytes 1216520 | tf_op jit(solution)/shard_map/ppermute | solution.py:568
  29.7 6.8 %collective-permute-start.2 = (f32[33,24,128]{2,1,0:T(8,128)S(1)}, f32[33,24,128]{2,1,0:T(8,128)S(1)}, u32[]{:S(2)}, u32[]{:S(2)}) collective-permute-start(f32[33,24,128]{2,1,0:T(8,128)S(1)} %get-tuple-element.34.sent), channel_id=1, source_target_pairs={{0,4},{8,12},{16,20},{24,28},{32,36},{40,44},{48,52},{56,60},{64,6... | collective-permute-start | bytes 1216520 | tf_op jit(solution)/shard_map/ppermute | solution.py:569

commit v7 on v6

--- a/solution.py
+++ b/solution.py
@@ -286,7 +286,8 @@
     odd = lax.rem(index, 2)
     swap = lax.rem(lax.axis_index(patch), 2) == 1
     size = lax.axis_size(quad)
-    alive = jnp.where(jnp.logical_or(index == 0, index == size - 1), 0.0, 1.0)
+    inside = jnp.logical_and(index > 0, index < size - 1)
+    alive = jnp.where(inside, 1.0, 0.0)
     groups = even.shape[1]
     width = even.shape[-1]
     height = log_kappa.shape[0]
@@ -297,14 +298,15 @@
     place = pl.multiple_of(16 - 8 * odd, 8)
     logs[pl.ds(place, 16)] = permute_columns(log_kappa[pl.ds(own_at, 16), :], matrix)
     halo_at = pl.multiple_of(8 + 16 * odd, 8)
-    logs[pl.ds(halo_at, 8)] = permute_columns(halo_b[count], matrix)
+    logs[pl.ds(halo_at, 8)] = permute_columns(jnp.where(inside, halo_b[count], 0.0), matrix)
     position = lax.broadcasted_iota(jnp.int32, (24, width), 0)
     outside = jnp.logical_and(position >= 16 * odd, position < 8 + 16 * odd)
     values = face_weights(logs[...], jnp.where(outside, alive, 1.0))
     for i in range(4):
         natural[i] = values[i]
 
-    load_rows(halo_b[pl.ds(0, count)], mixed, even, 0, odd, matrix)
+    fields = jnp.where(inside, halo_b[pl.ds(0, count)], 0.0)
+    load_rows(fields, mixed, even, 0, odd, matrix)
     spread_weights(
         natural, weights, SWEEPS, lambda k: jnp.where(odd == 1, 22 - k, k + 1), odd
     )
@@ -393,13 +395,13 @@
     return out
 
 
-def final_kernel(quad, patch, gathered, sub_in, sub_edge, basis, coupling, slabs, sems):
+def final_kernel(quad, patch, chip, other, sub_in, sub_edge, basis, coupling, slabs, sems):
     odd = lax.rem(lax.axis_index(quad), 2)
     place = lax.axis_index(patch)
     last = lax.axis_size(patch) - 1
     inner, count, sub_width = sub_in.shape
     height = inner + SWEEPS
-    total = (gathered[0] + gathered[1]) + (gathered[2] + gathered[3])
+    total = chip[...] + other[...]
     lanes = total.shape[1]
     mats = [total[:, k * count : (k + 1) * count] for k in range(5)]
     eye = (
@@ -412,6 +414,8 @@
         jnp.where(place == last, eye, mats[2]),
     ]
     own, left, right = inverse_factors(grams, eye, lanes)
+    from_left = jnp.where(place == 0, 0.0, mats[3])
+    from_right = jnp.where(place == last, 0.0, mats[4])
 
     high = own.astype(bf16).astype(f32)
     low = own - high
@@ -444,8 +448,8 @@
             )
             copy.start()
             copies.append(copy)
-    coupling[0] = dot_nt(dot_nn(own, mats[3], highest), left, highest)
-    coupling[1] = dot_nt(dot_nn(own, mats[4], highest), right, highest)
+    coupling[0] = dot_nt(dot_nn(own, from_left, highest), left, highest)
+    coupling[1] = dot_nt(dot_nn(own, from_right, highest), right, highest)
     for copy in copies:
         copy.wait()
 
@@ -534,7 +538,7 @@
     )(left_in, left_edge, right_in, right_edge, from_right_pair, from_left_pair, sent)
 
 
-def call_final(gathered, sub_in, sub_edge):
+def call_final(chip, other, sub_in, sub_edge):
     inner, count, sub_width = sub_in.shape
     height = inner + SWEEPS
     return pl.pallas_call(
@@ -547,29 +551,41 @@
         ],
         compiler_params=PARAMS,
         name="final",
-    )(gathered, sub_in, sub_edge)
-
-
-def pairs(size, first):
-    swaps = [(i, i + 1) for i in range(first, size - 1, 2)]
-    return swaps + [(j, i) for i, j in swaps]
+    )(chip, other, sub_in, sub_edge)
+
+
+def swaps(size, first):
+    route = [(i, i + 1) for i in range(first, size - 1, 2)]
+    return route + [(j, i) for i, j in route]
 
 
 def on_device(vectors, log_kappa):
     vec, log_own = vectors[0], log_kappa[0]
-    patch_size, quad_size = lax.axis_size("patch"), lax.axis_size("quad")
+    patches, quads = lax.axis_size("patch"), lax.axis_size("quad")
     send_a, send_b = call_prepare(vec, log_own)
-    halo_a = lax.ppermute(send_a, "quad", pairs(quad_size, 0))
-    halo_b = lax.ppermute(send_b, "quad", pairs(quad_size, 1))
+    halo_a = lax.ppermute(send_a, "quad", swaps(quads, 0))
+    middle = [(quads * p + i, quads * p + j) for p in range(patches) for i, j in swaps(quads, 1)]
+    idle = [
+        (quads * i + q, quads * j + q) for i, j in swaps(patches, 0) for q in (0, quads - 1)
+    ]
+    halo_b = lax.ppermute(send_b, ("patch", "quad"), middle + idle)
     left_in, right_in, sub_in, send_1_in, send_2_in, *for_edge = call_inner(vec, halo_a, log_own)
     left_edge, right_edge, sub_edge, send_1, send_2 = call_edge(
         halo_b, log_own, *for_edge, send_1_in, send_2_in
     )
-    from_2 = lax.ppermute(send_2, "patch", pairs(patch_size, 1))
-    from_1 = lax.ppermute(send_1, "patch", pairs(patch_size, 0))
+    partners = [
+        (quads * i + q, quads * j + q) for i, j in swaps(patches, 1) for q in range(quads)
+    ]
+    idle = [
+        (quads * p + i, quads * p + j) for p in (0, patches - 1) for i, j in swaps(quads, 0)
+    ]
+    from_2 = lax.ppermute(send_2, ("patch", "quad"), partners + idle)
+    from_1 = lax.ppermute(send_1, "patch", swaps(patches, 0))
     packed = call_product(left_in, left_edge, right_in, right_edge, from_1, from_2, send_1)
-    gathered = lax.all_gather(packed, "quad")
-    basis, coupling = call_final(gathered, sub_in, sub_edge)
+    chip = packed + lax.ppermute(packed, "quad", swaps(quads, 0))
+    half = quads // 2
+    other = lax.ppermute(chip, "quad", [(i, (i + half) % quads) for i in range(quads)])
+    basis, coupling = call_final(chip, other, sub_in, sub_edge)
     return basis[None], coupling[None]
 
 

time: 49.7 us -> 45.3 us (0.911); the launches traced: 49.6 us -> 44.6 us
  blocking collectives: 9.85 us -> 0 us
  waiting for transfers between devices: 6.75 us -> 10.3 us
  starting transfers between devices: 17.1 us -> 18.4 us
    all_gather x1 -> x0, blocking collectives: 9.85 us -> none  [on_device(): gathered = lax.all_gather(packed, 'quad')]
    ppermute x4 -> x6, waiting for transfers between devices: 6.75 us -> 10.3 us  [the longest x1 6.05 us: on_device(): from_2 = lax.ppermute(send_2, ('patch', 'quad'), partners + idle)]
    ppermute x4 -> x6, starting transfers between devices: 17.1 us -> 18.4 us  [the longest x1 6.89 us: on_device(): halo_b = lax.ppermute(send_b, ('patch', 'quad'), middle + idle)]
  transfers between devices with their start and end apart: 4 -> 6, of which waited for: 2 -> 4; matrix products, arithmetic and copies ran while one was open for 0% -> 0% of each run, Pallas kernels for 16% -> 18%
where the time goes in v7:
time: 45.3 us; the launch traced here: 44.6 us
  starting transfers between devices  18.4 us (41%)
  Pallas kernels  15.2 us (34%)
  waiting for transfers between devices  10.3 us (23%)
  between operations  0.67 us (1%)
    pallas_call x1, Pallas kernels, call_inner(): pl.pallas_call(functools.partial(inner_kernel, 'quad', 'patch'), out_shap...  8.17 us
    ppermute x1, starting transfers between devices, on_device(): halo_b = lax.ppermute(send_b, ('patch', 'quad'), middle + idle)  6.89 us
    ppermute x1, waiting for transfers between devices, on_device(): from_2 = lax.ppermute(send_2, ('patch', 'quad'), partners + idle)  6.05 us
    ppermute x1, starting transfers between devices, on_device(): from_2 = lax.ppermute(send_2, ('patch', 'quad'), partners + idle)  5.55 us
    ppermute x1, starting transfers between devices, on_device(): lax.ppermute(chip, 'quad', [(i, (i + half) % quads) for i in range(quads)])  5.18 us
    pallas_call x1, Pallas kernels, call_final(): pl.pallas_call(functools.partial(final_kernel, 'quad', 'patch'), out_shap...  2.67 us
    pallas_call x1, Pallas kernels, call_edge(): pl.pallas_call(functools.partial(edge_kernel, 'quad', 'patch'), out_shape...  2.51 us
    ppermute x1, waiting for transfers between devices, on_device(): from_1 = lax.ppermute(send_1, 'patch', swaps(patches, 0))  1.85 us
  transfers between devices with their start and end apart: 6, of which 4 were waited for; matrix products, arithmetic and copies ran while one was open for 0% of the time, Pallas kernels for 18%

profile of v7, /device:TPU:25, one launch (start us, length us, event | category | flops | bytes accessed | tf_op | source)
XLA Modules:
  0.0 44.6 jit_solution(17566990758727617968)
XLA Ops:
  0.6 0.0 copy-start.1
  0.6 0.0 copy-start
  0.6 1.3 %prepare.1 = (f32[25,8,512]{2,1,0:T(8,128)S(1)}, f32[25,8,512]{2,1,0:T(8,128)S(1)}) custom-call(f32[24,32,512]{2,1,0:T(8,128)} %bitcast.4, f32[32,512]{1,0:T(8,128)} %bitcast.6), custom_call_target="tpu_custom_call" | custom-call | tf_op jit(solution)/shard_map/prepare/pallas_call | solution.py:459
  2.0 0.8 %collective-permute-start = (f32[25,8,512]{2,1,0:T(8,128)S(1)}, f32[25,8,512]{2,1,0:T(8,128)S(1)}, u32[]{:S(2)}, u32[]{:S(2)}) collective-permute-start(f32[25,8,512]{2,1,0:T(8,128)S(1)} %get-tuple-element.21), channel_id=1, source_target_pairs={{0,1},{2,3},{1,0},{3,2},{4,5},{6,7},{5,4},{7,6},{8,9},{10,11},{9,8... | collective-permute-start | bytes 1228808 | tf_op jit(solution)/shard_map/ppermute | solution.py:566
  2.7 6.9 %collective-permute-start.1 = (f32[25,8,512]{2,1,0:T(8,128)S(1)}, f32[25,8,512]{2,1,0:T(8,128)S(1)}, u32[]{:S(2)}, u32[]{:S(2)}) collective-permute-start(f32[25,8,512]{2,1,0:T(8,128)S(1)} %get-tuple-element.23), channel_id=1, source_target_pairs={{1,2},{2,1},{5,6},{6,5},{9,10},{10,9},{13,14},{14,13},{17,18},{18,... | collective-permute-start | bytes 1228808 | tf_op jit(solution)/shard_map/ppermute | solution.py:571
  9.6 0.0 collective-permute-done.halo_a
  9.6 0.0 copy-done.1
  9.6 0.0 copy-done
  9.6 8.2 %inner.1 = (f32[24,24,128]{2,1,0:T(8,128)S(1)}, f32[24,24,128]{2,1,0:T(8,128)S(1)}, f32[24,24,256]{2,1,0:T(8,128)S(1)}, f32[24,24,128]{2,1,0:T(8,128)S(1)}, f32[...) custom-call(f32[24,32,512]{2,1,0:T(8,128)S(1)} %bitcast.5, ...), custom_call_target="tpu_custom_call" | custom-call | flops 37748736 | bytes 5242880 | tf_op jit(solution)/shard_map/inner/pallas_call | solution.py:477
  17.8 0.0 collective-permute-done.1.halo_b
  17.8 2.5 %edge.1 = (f32[8,24,128]{2,1,0:T(8,128)S(1)}, f32[8,24,128]{2,1,0:T(8,128)S(1)}, f32[8,24,256]{2,1,0:T(8,128)S(1)}, f32[33,24,128]{2,1,0:T(8,128)S(1)}, f32[33,24,128]{2,1,0:T(8,128)S(1)}) custom-call(f32[25,8,512]{2,1,0:T(8,128)S(1)} %collective-permute-done.1.halo_b, f32[32,512]{1,0:T(8,128)S(1)} %bitcast.8, ...), custom_call_target="tpu_custom_call" | custom-call | tf_op jit(solution)/shard_map/edge/pallas_call | solution.py:509
  20.3 5.5 %collective-permute-start.3 = (f32[33,24,128]{2,1,0:T(8,128)S(1)}, f32[33,24,128]{2,1,0:T(8,128)S(1)}, u32[]{:S(2)}, u32[]{:S(2)}) collective-permute-start(f32[33,24,128]{2,1,0:T(8,128)S(1)} %get-tuple-element.35), channel_id=1, source_target_pairs={{4,8},{5,9},{6,10},{7,11},{12,16},{13,17},{14,18},{15,19},{20,24},... | collective-permute-start | bytes 1216520 | tf_op jit(solution)/shard_map/ppermute | solution.py:582
  25.9 0.0 collective-permute-start.2
  25.9 6.0 %collective-permute-done.3.from_left_pair = f32[33,24,128]{2,1,0:T(8,128)S(1)} collective-permute-done((f32[33,24,128]{2,1,0:T(8,128)S(1)}, f32[33,24,128]{2,1,0:T(8,128)S(1)}, u32[]{:S(2)}, u32[]{:S(2)}) %collective-permute-start.3) | collective-permute-done | bytes 405536 | tf_op jit(solution)/shard_map/ppermute | solution.py:582
  31.9 1.8 %collective-permute-done.2.from_right_pair = f32[33,24,128]{2,1,0:T(8,128)S(1)} collective-permute-done((f32[33,24,128]{2,1,0:T(8,128)S(1)}, f32[33,24,128]{2,1,0:T(8,128)S(1)}, u32[]{:S(2)}, u32[]{:S(2)}) %collective-permute-start.2) | collective-permute-done | bytes 405536 | tf_op jit(solution)/shard_map/ppermute | solution.py:583
  33.8 0.5 %product.1 = f32[24,128]{1,0:T(8,128)S(1)} custom-call(f32[24,24,128]{2,1,0:T(8,128)S(1)} %get-tuple-element.22.left_in, f32[8,24,128]{2,1,0:T(8,128)S(1)} %get-tuple-element.31.left_edge, f32[24,24,128]{2,1,0:T(8,128)S(1)} %get-tuple-element.32.right_in, f32[8,24,128]{2,1,0:T(8,128)S(1)} %get-tuple-element.33.right_edge, ...), custom_call_target="tpu_custom_call" | custom-call | tf_op jit(solution)/shard_map/product/pallas_call | solution.py:533
  34.3 0.0 collective-permute-start.4
  34.3 1.2 %collective-permute-done.4 = f32[24,128]{1,0:T(8,128)S(1)} collective-permute-done((f32[24,128]{1,0:T(8,128)S(1)}, f32[24,128]{1,0:T(8,128)S(1)}, u32[]{:S(2)}, u32[]{:S(2)}) %collective-permute-start.4) | collective-permute-done | bytes 12320 | tf_op jit(solution)/shard_map/ppermute | solution.py:585
  35.5 5.2 %collective-permute-start.5 = (f32[24,128]{1,0:T(8,128)S(1)}, f32[24,128]{1,0:T(8,128)S(1)}, u32[]{:S(2)}, u32[]{:S(2)}) collective-permute-start(f32[24,128]{1,0:T(8,128)S(1)} %add.3.chip), channel_id=1, source_target_pairs={{0,2},{1,3},{2,0},{3,1},{4,6},{5,7},{6,4},{7,5},{8,10},{9,11},{10,... | collective-permute-start | bytes 36872 | tf_op jit(solution)/shard_map/ppermute | solution.py:587
  40.7 1.3 %collective-permute-done.5.other = f32[24,128]{1,0:T(8,128)S(1)} collective-permute-done((f32[24,128]{1,0:T(8,128)S(1)}, f32[24,128]{1,0:T(8,128)S(1)}, u32[]{:S(2)}, u32[]{:S(2)}) %collective-permute-start.5) | collective-permute-done | bytes 12320 | tf_op jit(solution)/shard_map/ppermute | solution.py:587
  41.9 2.7 %final.1 = (f32[24,32,256]{2,1,0:T(8,128)}, f32[2,24,24]{2,1,0:T(8,128)}) custom-call(f32[24,128]{1,0:T(8,128)S(1)} %add.3.chip, f32[24,128]{1,0:T(8,128)S(1)} %collective-permute-done.5.other, f32[24,24,256]{2,1,0:T(8,128)S(1)} %get-tuple-element.36.sub_in, f32[8,24,256]{2,1,0:T(8,128)S(1)} %get-tuple-element.37.sub_edge), custom_call_target="tpu_custom_call" | custom-call | tf_op jit(solution)/shard_map/final/pallas_call | solution.py:544
  (1 shorter events, 0.0 us)
Async XLA Ops:
  0.6 9.0 %copy-start.1 = (f32[1,32,512]{2,1,0:T(8,128)S(1)}, f32[1,32,512]{2,1,0:T(8,128)}, u32[]{:S(2)}) copy-start(f32[1,32,512]{2,1,0:T(8,128)} %param.3) | copy-start | bytes 196612
  0.6 9.0 %copy-start = (f32[1,24,32,512]{3,2,1,0:T(8,128)S(1)}, f32[1,24,32,512]{3,2,1,0:T(8,128)}, u32[]{:S(2)}) copy-start(f32[1,24,32,512]{3,2,1,0:T(8,128)} %param.2) | copy-start | bytes 4718596
  2.0 7.7 %collective-permute-start = (f32[25,8,512]{2,1,0:T(8,128)S(1)}, f32[25,8,512]{2,1,0:T(8,128)S(1)}, u32[]{:S(2)}, u32[]{:S(2)}) collective-permute-start(f32[25,8,512]{2,1,0:T(8,128)S(1)} %get-tuple-element.21), channel_id=1, source_target_pairs={{0,1},{2,3},{1,0},{3,2},{4,5},{6,7},{5,4},{7,6},{8,9},{10,11},{9,8... | collective-permute-start | bytes 1228808 | tf_op jit(solution)/shard_map/ppermute | solution.py:566
  2.7 15.1 %collective-permute-start.1 = (f32[25,8,512]{2,1,0:T(8,128)S(1)}, f32[25,8,512]{2,1,0:T(8,128)S(1)}, u32[]{:S(2)}, u32[]{:S(2)}) collective-permute-start(f32[25,8,512]{2,1,0:T(8,128)S(1)} %get-tuple-element.23), channel_id=1, source_target_pairs={{1,2},{2,1},{5,6},{6,5},{9,10},{10,9},{13,14},{14,13},{17,18},{18,... | collective-permute-start | bytes 1228808 | tf_op jit(solution)/shard_map/ppermute | solution.py:571
  20.3 11.6 %collective-permute-start.3 = (f32[33,24,128]{2,1,0:T(8,128)S(1)}, f32[33,24,128]{2,1,0:T(8,128)S(1)}, u32[]{:S(2)}, u32[]{:S(2)}) collective-permute-start(f32[33,24,128]{2,1,0:T(8,128)S(1)} %get-tuple-element.35), channel_id=1, source_target_pairs={{4,8},{5,9},{6,10},{7,11},{12,16},{13,17},{14,18},{15,19},{20,24},... | collective-permute-start | bytes 1216520 | tf_op jit(solution)/shard_map/ppermute | solution.py:582
  25.9 7.9 %collective-permute-start.2 = (f32[33,24,128]{2,1,0:T(8,128)S(1)}, f32[33,24,128]{2,1,0:T(8,128)S(1)}, u32[]{:S(2)}, u32[]{:S(2)}) collective-permute-start(f32[33,24,128]{2,1,0:T(8,128)S(1)} %get-tuple-element.34.sent), channel_id=1, source_target_pairs={{0,4},{8,12},{16,20},{24,28},{32,36},{40,44},{48,52},{56,60},{64,6... | collective-permute-start | bytes 1216520 | tf_op jit(solution)/shard_map/ppermute | solution.py:583
  34.3 1.2 %collective-permute-start.4 = (f32[24,128]{1,0:T(8,128)S(1)}, f32[24,128]{1,0:T(8,128)S(1)}, u32[]{:S(2)}, u32[]{:S(2)}) collective-permute-start(f32[24,128]{1,0:T(8,128)S(1)} %product.1), channel_id=1, source_target_pairs={{0,1},{2,3},{1,0},{3,2},{4,5},{6,7},{5,4},{7,6},{8,9},{10,11},{9,8... | collective-permute-start | bytes 36872 | tf_op jit(solution)/shard_map/ppermute | solution.py:585
  35.5 6.5 %collective-permute-start.5 = (f32[24,128]{1,0:T(8,128)S(1)}, f32[24,128]{1,0:T(8,128)S(1)}, u32[]{:S(2)}, u32[]{:S(2)}) collective-permute-start(f32[24,128]{1,0:T(8,128)S(1)} %add.3.chip), channel_id=1, source_target_pairs={{0,2},{1,3},{2,0},{3,1},{4,6},{5,7},{6,4},{7,5},{8,10},{9,11},{10,... | collective-permute-start | bytes 36872 | tf_op jit(solution)/shard_map/ppermute | solution.py:587

commit v8 on v7

--- a/solution.py
+++ b/solution.py
@@ -59,13 +59,24 @@
     return (full[:n, :m] + full[n:, :m]) + (full[:n, m:] + full[n:, m:])
 
 
+def interleaved(column):
+    return (column & (BLOCKS - 1)) * LANES + lax.shift_right_logical(column, 2)
+
+
 def permutation(width, inverse):
-    row = lax.broadcasted_iota(jnp.int32, (width, width), 0)
-    col = lax.broadcasted_iota(jnp.int32, (width, width), 1)
-    if inverse:
-        row, col = col, row
-    target = (row % BLOCKS) * LANES + row // BLOCKS
-    return jnp.where(target == col, 1.0, 0.0).astype(bf16)
+    shape = (width, LANES)
+    row = lax.broadcasted_iota(jnp.int32, shape, 0)
+    lane = lax.broadcasted_iota(jnp.int32, shape, 1)
+    wanted = row if inverse else interleaved(row)
+    blocks = []
+    for k in range(width // LANES):
+        if inverse:
+            one = lax.broadcasted_iota(jnp.int32, (8, LANES), 1) + k * LANES
+            place = jnp.concatenate([interleaved(one)] * (width // 8), axis=0)
+        else:
+            place = lane + k * LANES
+        blocks.append(jnp.where(wanted == place, 1.0, 0.0))
+    return jnp.concatenate(blocks, axis=1).astype(bf16)
 
 
 def permute_columns(x, matrix):
@@ -125,7 +136,7 @@
             weights[k, i] = jnp.broadcast_to(natural[source, pl.ds(r, 1), :], (8, width))
         return carry
 
-    lax.fori_loop(0, count, body, 0, unroll=2)
+    lax.fori_loop(0, count, body, 0, unroll=8 if count % 8 == 0 else 19)
 
 
 def apply_row(now, row, weights, wrow):

time: 45.3 us -> 45.1 us (level)
  no operation moved by 1% of the time
where the time goes in v8:
time: 45.1 us; the launch traced here: 44.4 us
  starting transfers between devices  18.6 us (41%)
  Pallas kernels  14.9 us (33%)
  waiting for transfers between devices  10.2 us (23%)
  between operations  0.67 us (1%)
    pallas_call x1, Pallas kernels, call_inner(): pl.pallas_call(functools.partial(inner_kernel, 'quad', 'patch'), out_shap...  8.08 us
    ppermute x1, starting transfers between devices, on_device(): halo_b = lax.ppermute(send_b, ('patch', 'quad'), middle + idle)  6.89 us
    ppermute x1, waiting for transfers between devices, on_device(): from_2 = lax.ppermute(send_2, ('patch', 'quad'), partners + idle)  5.97 us
    ppermute x1, starting transfers between devices, on_device(): from_2 = lax.ppermute(send_2, ('patch', 'quad'), partners + idle)  5.64 us
    ppermute x1, starting transfers between devices, on_device(): lax.ppermute(chip, 'quad', [(i, (i + half) % quads) for i in range(quads)])  5.27 us
    pallas_call x1, Pallas kernels, call_final(): pl.pallas_call(functools.partial(final_kernel, 'quad', 'patch'), out_shap...  2.67 us
    pallas_call x1, Pallas kernels, call_edge(): pl.pallas_call(functools.partial(edge_kernel, 'quad', 'patch'), out_shape...  2.34 us
    ppermute x1, waiting for transfers between devices, on_device(): from_1 = lax.ppermute(send_1, 'patch', swaps(patches, 0))  1.84 us
  transfers between devices with their start and end apart: 6, of which 4 were waited for; matrix products, arithmetic and copies ran while one was open for 0% of the time, Pallas kernels for 18%

profile of v8, /device:TPU:25, one launch (start us, length us, event | category | flops | bytes accessed | tf_op | source)
XLA Modules:
  0.0 44.4 jit_solution(11697421380030228770)
XLA Ops:
  0.6 0.0 copy-start.1
  0.6 0.0 copy-start
  0.6 1.3 %prepare.1 = (f32[25,8,512]{2,1,0:T(8,128)S(1)}, f32[25,8,512]{2,1,0:T(8,128)S(1)}) custom-call(f32[24,32,512]{2,1,0:T(8,128)} %bitcast.4, f32[32,512]{1,0:T(8,128)} %bitcast.6), custom_call_target="tpu_custom_call" | custom-call | tf_op jit(solution)/shard_map/prepare/pallas_call | solution.py:470
  2.0 0.8 %collective-permute-start = (f32[25,8,512]{2,1,0:T(8,128)S(1)}, f32[25,8,512]{2,1,0:T(8,128)S(1)}, u32[]{:S(2)}, u32[]{:S(2)}) collective-permute-start(f32[25,8,512]{2,1,0:T(8,128)S(1)} %get-tuple-element.21), channel_id=1, source_target_pairs={{0,1},{2,3},{1,0},{3,2},{4,5},{6,7},{5,4},{7,6},{8,9},{10,11},{9,8... | collective-permute-start | bytes 1228808 | tf_op jit(solution)/shard_map/ppermute | solution.py:577
  2.7 6.9 %collective-permute-start.1 = (f32[25,8,512]{2,1,0:T(8,128)S(1)}, f32[25,8,512]{2,1,0:T(8,128)S(1)}, u32[]{:S(2)}, u32[]{:S(2)}) collective-permute-start(f32[25,8,512]{2,1,0:T(8,128)S(1)} %get-tuple-element.23), channel_id=1, source_target_pairs={{1,2},{2,1},{5,6},{6,5},{9,10},{10,9},{13,14},{14,13},{17,18},{18,... | collective-permute-start | bytes 1228808 | tf_op jit(solution)/shard_map/ppermute | solution.py:582
  9.6 0.0 collective-permute-done.halo_a
  9.6 0.0 copy-done.1
  9.6 0.0 copy-done
  9.6 8.1 %inner.1 = (f32[24,24,128]{2,1,0:T(8,128)S(1)}, f32[24,24,128]{2,1,0:T(8,128)S(1)}, f32[24,24,256]{2,1,0:T(8,128)S(1)}, f32[24,24,128]{2,1,0:T(8,128)S(1)}, f32[...) custom-call(f32[24,32,512]{2,1,0:T(8,128)S(1)} %bitcast.5, ...), custom_call_target="tpu_custom_call" | custom-call | flops 37748736 | bytes 5242880 | tf_op jit(solution)/shard_map/inner/pallas_call | solution.py:488
  17.7 0.0 collective-permute-done.1.halo_b
  17.7 2.3 %edge.1 = (f32[8,24,128]{2,1,0:T(8,128)S(1)}, f32[8,24,128]{2,1,0:T(8,128)S(1)}, f32[8,24,256]{2,1,0:T(8,128)S(1)}, f32[33,24,128]{2,1,0:T(8,128)S(1)}, f32[33,24,128]{2,1,0:T(8,128)S(1)}) custom-call(f32[25,8,512]{2,1,0:T(8,128)S(1)} %collective-permute-done.1.halo_b, f32[32,512]{1,0:T(8,128)S(1)} %bitcast.8, ...), custom_call_target="tpu_custom_call" | custom-call | tf_op jit(solution)/shard_map/edge/pallas_call | solution.py:520
  20.1 5.6 %collective-permute-start.3 = (f32[33,24,128]{2,1,0:T(8,128)S(1)}, f32[33,24,128]{2,1,0:T(8,128)S(1)}, u32[]{:S(2)}, u32[]{:S(2)}) collective-permute-start(f32[33,24,128]{2,1,0:T(8,128)S(1)} %get-tuple-element.35), channel_id=1, source_target_pairs={{4,8},{5,9},{6,10},{7,11},{12,16},{13,17},{14,18},{15,19},{20,24},... | collective-permute-start | bytes 1216520 | tf_op jit(solution)/shard_map/ppermute | solution.py:593
  25.7 0.0 collective-permute-start.2
  25.7 6.0 %collective-permute-done.3.from_left_pair = f32[33,24,128]{2,1,0:T(8,128)S(1)} collective-permute-done((f32[33,24,128]{2,1,0:T(8,128)S(1)}, f32[33,24,128]{2,1,0:T(8,128)S(1)}, u32[]{:S(2)}, u32[]{:S(2)}) %collective-permute-start.3) | collective-permute-done | bytes 405536 | tf_op jit(solution)/shard_map/ppermute | solution.py:593
  31.7 1.8 %collective-permute-done.2.from_right_pair = f32[33,24,128]{2,1,0:T(8,128)S(1)} collective-permute-done((f32[33,24,128]{2,1,0:T(8,128)S(1)}, f32[33,24,128]{2,1,0:T(8,128)S(1)}, u32[]{:S(2)}, u32[]{:S(2)}) %collective-permute-start.2) | collective-permute-done | bytes 405536 | tf_op jit(solution)/shard_map/ppermute | solution.py:594
  33.5 0.5 %product.1 = f32[24,128]{1,0:T(8,128)S(1)} custom-call(f32[24,24,128]{2,1,0:T(8,128)S(1)} %get-tuple-element.22.left_in, f32[8,24,128]{2,1,0:T(8,128)S(1)} %get-tuple-element.31.left_edge, f32[24,24,128]{2,1,0:T(8,128)S(1)} %get-tuple-element.32.right_in, f32[8,24,128]{2,1,0:T(8,128)S(1)} %get-tuple-element.33.right_edge, ...), custom_call_target="tpu_custom_call" | custom-call | tf_op jit(solution)/shard_map/product/pallas_call | solution.py:544
  34.0 0.0 collective-permute-start.4
  34.1 1.2 %collective-permute-done.4 = f32[24,128]{1,0:T(8,128)S(1)} collective-permute-done((f32[24,128]{1,0:T(8,128)S(1)}, f32[24,128]{1,0:T(8,128)S(1)}, u32[]{:S(2)}, u32[]{:S(2)}) %collective-permute-start.4) | collective-permute-done | bytes 12320 | tf_op jit(solution)/shard_map/ppermute | solution.py:596
  35.2 5.3 %collective-permute-start.5 = (f32[24,128]{1,0:T(8,128)S(1)}, f32[24,128]{1,0:T(8,128)S(1)}, u32[]{:S(2)}, u32[]{:S(2)}) collective-permute-start(f32[24,128]{1,0:T(8,128)S(1)} %add.3.chip), channel_id=1, source_target_pairs={{0,2},{1,3},{2,0},{3,1},{4,6},{5,7},{6,4},{7,5},{8,10},{9,11},{10,... | collective-permute-start | bytes 36872 | tf_op jit(solution)/shard_map/ppermute | solution.py:598
  40.5 1.2 %collective-permute-done.5.other = f32[24,128]{1,0:T(8,128)S(1)} collective-permute-done((f32[24,128]{1,0:T(8,128)S(1)}, f32[24,128]{1,0:T(8,128)S(1)}, u32[]{:S(2)}, u32[]{:S(2)}) %collective-permute-start.5) | collective-permute-done | bytes 12320 | tf_op jit(solution)/shard_map/ppermute | solution.py:598
  41.7 2.7 %final.1 = (f32[24,32,256]{2,1,0:T(8,128)}, f32[2,24,24]{2,1,0:T(8,128)}) custom-call(f32[24,128]{1,0:T(8,128)S(1)} %add.3.chip, f32[24,128]{1,0:T(8,128)S(1)} %collective-permute-done.5.other, f32[24,24,256]{2,1,0:T(8,128)S(1)} %get-tuple-element.36.sub_in, f32[8,24,256]{2,1,0:T(8,128)S(1)} %get-tuple-element.37.sub_edge), custom_call_target="tpu_custom_call" | custom-call | tf_op jit(solution)/shard_map/final/pallas_call | solution.py:555
  (1 shorter events, 0.0 us)
Async XLA Ops:
  0.6 9.0 %copy-start.1 = (f32[1,32,512]{2,1,0:T(8,128)S(1)}, f32[1,32,512]{2,1,0:T(8,128)}, u32[]{:S(2)}) copy-start(f32[1,32,512]{2,1,0:T(8,128)} %param.3) | copy-start | bytes 196612
  0.6 9.0 %copy-start = (f32[1,24,32,512]{3,2,1,0:T(8,128)S(1)}, f32[1,24,32,512]{3,2,1,0:T(8,128)}, u32[]{:S(2)}) copy-start(f32[1,24,32,512]{3,2,1,0:T(8,128)} %param.2) | copy-start | bytes 4718596
  2.0 7.7 %collective-permute-start = (f32[25,8,512]{2,1,0:T(8,128)S(1)}, f32[25,8,512]{2,1,0:T(8,128)S(1)}, u32[]{:S(2)}, u32[]{:S(2)}) collective-permute-start(f32[25,8,512]{2,1,0:T(8,128)S(1)} %get-tuple-element.21), channel_id=1, source_target_pairs={{0,1},{2,3},{1,0},{3,2},{4,5},{6,7},{5,4},{7,6},{8,9},{10,11},{9,8... | collective-permute-start | bytes 1228808 | tf_op jit(solution)/shard_map/ppermute | solution.py:577
  2.7 15.0 %collective-permute-start.1 = (f32[25,8,512]{2,1,0:T(8,128)S(1)}, f32[25,8,512]{2,1,0:T(8,128)S(1)}, u32[]{:S(2)}, u32[]{:S(2)}) collective-permute-start(f32[25,8,512]{2,1,0:T(8,128)S(1)} %get-tuple-element.23), channel_id=1, source_target_pairs={{1,2},{2,1},{5,6},{6,5},{9,10},{10,9},{13,14},{14,13},{17,18},{18,... | collective-permute-start | bytes 1228808 | tf_op jit(solution)/shard_map/ppermute | solution.py:582
  20.1 11.6 %collective-permute-start.3 = (f32[33,24,128]{2,1,0:T(8,128)S(1)}, f32[33,24,128]{2,1,0:T(8,128)S(1)}, u32[]{:S(2)}, u32[]{:S(2)}) collective-permute-start(f32[33,24,128]{2,1,0:T(8,128)S(1)} %get-tuple-element.35), channel_id=1, source_target_pairs={{4,8},{5,9},{6,10},{7,11},{12,16},{13,17},{14,18},{15,19},{20,24},... | collective-permute-start | bytes 1216520 | tf_op jit(solution)/shard_map/ppermute | solution.py:593
  25.7 7.8 %collective-permute-start.2 = (f32[33,24,128]{2,1,0:T(8,128)S(1)}, f32[33,24,128]{2,1,0:T(8,128)S(1)}, u32[]{:S(2)}, u32[]{:S(2)}) collective-permute-start(f32[33,24,128]{2,1,0:T(8,128)S(1)} %get-tuple-element.34.sent), channel_id=1, source_target_pairs={{0,4},{8,12},{16,20},{24,28},{32,36},{40,44},{48,52},{56,60},{64,6... | collective-permute-start | bytes 1216520 | tf_op jit(solution)/shard_map/ppermute | solution.py:594
  34.0 1.2 %collective-permute-start.4 = (f32[24,128]{1,0:T(8,128)S(1)}, f32[24,128]{1,0:T(8,128)S(1)}, u32[]{:S(2)}, u32[]{:S(2)}) collective-permute-start(f32[24,128]{1,0:T(8,128)S(1)} %product.1), channel_id=1, source_target_pairs={{0,1},{2,3},{1,0},{3,2},{4,5},{6,7},{5,4},{7,6},{8,9},{10,11},{9,8... | collective-permute-start | bytes 36872 | tf_op jit(solution)/shard_map/ppermute | solution.py:596
  35.2 6.5 %collective-permute-start.5 = (f32[24,128]{1,0:T(8,128)S(1)}, f32[24,128]{1,0:T(8,128)S(1)}, u32[]{:S(2)}, u32[]{:S(2)}) collective-permute-start(f32[24,128]{1,0:T(8,128)S(1)} %add.3.chip), channel_id=1, source_target_pairs={{0,2},{1,3},{2,0},{3,1},{4,6},{5,7},{6,4},{7,5},{8,10},{9,11},{10,... | collective-permute-start | bytes 36872 | tf_op jit(solution)/shard_map/ppermute | solution.py:598

commit v9 on v8

--- a/solution.py
+++ b/solution.py
@@ -359,10 +359,10 @@
 
     def write(from_left, from_right):
         mats = (
+            products(left_in, left_edge, from_left),
             sent[height, :, :count],
             from_left[height, :, :count],
             from_right[height, :, :count],
-            products(left_in, left_edge, from_left),
             products(right_in, right_edge, from_right),
         )
         for k, mat in enumerate(mats):
@@ -377,19 +377,19 @@
         write(from_left_pair, from_right_pair)
 
 
-def inverse_factors(mats, eye, lanes):
-    count = eye.shape[0]
-    sub = lax.broadcasted_iota(jnp.int32, (count, lanes), 0)
-    lane = lax.broadcasted_iota(jnp.int32, (count, lanes), 1)
-    zeros = jnp.zeros((count, lanes - 2 * count), f32)
-    works = [jnp.concatenate([mat, eye, zeros], axis=1) for mat in mats]
+def inverse_factors(works, offsets, count):
+    sub = lax.broadcasted_iota(jnp.int32, works[0].shape, 0)
+    scales = [jnp.zeros_like(work) for work in works]
     for j in range(0, count, STEP):
         for m, work in enumerate(works):
-            cols = [jnp.broadcast_to(work[:, k : k + 1], (count, lanes)) for k in range(j, j + STEP)]
+            at = [offsets[m] + k for k in range(j, j + STEP)]
+            cols = [jnp.broadcast_to(work[:, k : k + 1], work.shape) for k in at]
             rows = [work[k : k + 1] for k in range(j, j + STEP)]
             change = jnp.zeros_like(work)
             for i in range(STEP):
-                over = 1.0 / cols[i][j + i : j + i + 1]
+                pivot = cols[i][j + i : j + i + 1]
+                scales[m] = jnp.where(sub == j + i, 1.0 / jnp.sqrt(pivot), scales[m])
+                over = 1.0 / pivot
                 scaled = rows[i] * over
                 for k in range(i + 1, STEP):
                     rows[k] = rows[k] - cols[i][j + k : j + k + 1] * scaled
@@ -399,11 +399,7 @@
             for i in range(1, STEP):
                 work = jnp.where(sub == j + i, rows[i], work)
             works[m] = work
-    out = []
-    for work in works:
-        diagonal = jnp.sum(jnp.where(sub == lane, work, 0.0), axis=1, keepdims=True)
-        out.append((work / jnp.sqrt(diagonal))[:, count : 2 * count])
-    return out
+    return [(work * scale)[:, :count] for work, scale in zip(works, scales)]
 
 
 def final_kernel(quad, patch, chip, other, sub_in, sub_edge, basis, coupling, slabs, sems):
@@ -413,20 +409,17 @@
     inner, count, sub_width = sub_in.shape
     height = inner + SWEEPS
     total = chip[...] + other[...]
-    lanes = total.shape[1]
-    mats = [total[:, k * count : (k + 1) * count] for k in range(5)]
-    eye = (
-        lax.broadcasted_iota(jnp.int32, (count, count), 0)
-        == lax.broadcasted_iota(jnp.int32, (count, count), 1)
-    ).astype(f32)
-    grams = [
-        mats[0],
-        jnp.where(place == 0, eye, mats[1]),
-        jnp.where(place == last, eye, mats[2]),
-    ]
-    own, left, right = inverse_factors(grams, eye, lanes)
-    from_left = jnp.where(place == 0, 0.0, mats[3])
-    from_right = jnp.where(place == last, 0.0, mats[4])
+    sub = lax.broadcasted_iota(jnp.int32, total.shape, 0)
+    lane = lax.broadcasted_iota(jnp.int32, total.shape, 1)
+    works = []
+    for k, missing in ((1, None), (2, place == 0), (3, place == last)):
+        column = lane - k * count
+        work = total if missing is None else jnp.where(missing, (sub == column).astype(f32), total)
+        work = jnp.where(jnp.logical_and(column >= 0, column < count), work, 0.0)
+        works.append(jnp.where(lane < count, (sub == lane).astype(f32), work))
+    own, left, right = inverse_factors(works, (count, 2 * count, 3 * count), count)
+    from_left = jnp.where(place == 0, 0.0, total[:, :count])
+    from_right = jnp.where(place == last, 0.0, total[:, 4 * count : 5 * count])
 
     high = own.astype(bf16).astype(f32)
     low = own - high

time: 45.1 us -> 44.8 us (level)
  no operation moved by 1% of the time
where the time goes in v9:
time: 44.8 us; the launch traced here: 44 us
  starting transfers between devices  18.6 us (42%)
  Pallas kernels  14.6 us (33%)
  waiting for transfers between devices  10.2 us (23%)
  between operations  0.67 us (1%)
    pallas_call x1, Pallas kernels, call_inner(): pl.pallas_call(functools.partial(inner_kernel, 'quad', 'patch'), out_shap...  8.08 us
    ppermute x1, starting transfers between devices, on_device(): halo_b = lax.ppermute(send_b, ('patch', 'quad'), middle + idle)  6.89 us
    ppermute x1, waiting for transfers between devices, on_device(): from_2 = lax.ppermute(send_2, ('patch', 'quad'), partners + idle)  5.97 us
    ppermute x1, starting transfers between devices, on_device(): from_2 = lax.ppermute(send_2, ('patch', 'quad'), partners + idle)  5.64 us
    ppermute x1, starting transfers between devices, on_device(): lax.ppermute(chip, 'quad', [(i, (i + half) % quads) for i in range(quads)])  5.27 us
    pallas_call x1, Pallas kernels, call_edge(): pl.pallas_call(functools.partial(edge_kernel, 'quad', 'patch'), out_shape...  2.34 us
    pallas_call x1, Pallas kernels, call_final(): pl.pallas_call(functools.partial(final_kernel, 'quad', 'patch'), out_shap...  2.33 us
    ppermute x1, waiting for transfers between devices, on_device(): from_1 = lax.ppermute(send_1, 'patch', swaps(patches, 0))  1.84 us
  transfers between devices with their start and end apart: 6, of which 4 were waited for; matrix products, arithmetic and copies ran while one was open for 0% of the time, Pallas kernels for 18%

profile of v9, /device:TPU:25, one launch (start us, length us, event | category | flops | bytes accessed | tf_op | source)
XLA Modules:
  0.0 44.0 jit_solution(18064057727944598434)
XLA Ops:
  0.6 0.0 copy-start.1
  0.6 0.0 copy-start
  0.6 1.3 %prepare.1 = (f32[25,8,512]{2,1,0:T(8,128)S(1)}, f32[25,8,512]{2,1,0:T(8,128)S(1)}) custom-call(f32[24,32,512]{2,1,0:T(8,128)} %bitcast.4, f32[32,512]{1,0:T(8,128)} %bitcast.6), custom_call_target="tpu_custom_call" | custom-call | tf_op jit(solution)/shard_map/prepare/pallas_call | solution.py:463
  2.0 0.8 %collective-permute-start = (f32[25,8,512]{2,1,0:T(8,128)S(1)}, f32[25,8,512]{2,1,0:T(8,128)S(1)}, u32[]{:S(2)}, u32[]{:S(2)}) collective-permute-start(f32[25,8,512]{2,1,0:T(8,128)S(1)} %get-tuple-element.21), channel_id=1, source_target_pairs={{0,1},{2,3},{1,0},{3,2},{4,5},{6,7},{5,4},{7,6},{8,9},{10,11},{9,8... | collective-permute-start | bytes 1228808 | tf_op jit(solution)/shard_map/ppermute | solution.py:570
  2.7 6.9 %collective-permute-start.1 = (f32[25,8,512]{2,1,0:T(8,128)S(1)}, f32[25,8,512]{2,1,0:T(8,128)S(1)}, u32[]{:S(2)}, u32[]{:S(2)}) collective-permute-start(f32[25,8,512]{2,1,0:T(8,128)S(1)} %get-tuple-element.23), channel_id=1, source_target_pairs={{1,2},{2,1},{5,6},{6,5},{9,10},{10,9},{13,14},{14,13},{17,18},{18,... | collective-permute-start | bytes 1228808 | tf_op jit(solution)/shard_map/ppermute | solution.py:575
  9.6 0.0 collective-permute-done.halo_a
  9.6 0.0 copy-done.1
  9.6 0.0 copy-done
  9.6 8.1 %inner.1 = (f32[24,24,128]{2,1,0:T(8,128)S(1)}, f32[24,24,128]{2,1,0:T(8,128)S(1)}, f32[24,24,256]{2,1,0:T(8,128)S(1)}, f32[24,24,128]{2,1,0:T(8,128)S(1)}, f32[...) custom-call(f32[24,32,512]{2,1,0:T(8,128)S(1)} %bitcast.5, ...), custom_call_target="tpu_custom_call" | custom-call | flops 37748736 | bytes 5242880 | tf_op jit(solution)/shard_map/inner/pallas_call | solution.py:481
  17.7 0.0 collective-permute-done.1.halo_b
  17.7 2.3 %edge.1 = (f32[8,24,128]{2,1,0:T(8,128)S(1)}, f32[8,24,128]{2,1,0:T(8,128)S(1)}, f32[8,24,256]{2,1,0:T(8,128)S(1)}, f32[33,24,128]{2,1,0:T(8,128)S(1)}, f32[33,24,128]{2,1,0:T(8,128)S(1)}) custom-call(f32[25,8,512]{2,1,0:T(8,128)S(1)} %collective-permute-done.1.halo_b, f32[32,512]{1,0:T(8,128)S(1)} %bitcast.8, ...), custom_call_target="tpu_custom_call" | custom-call | tf_op jit(solution)/shard_map/edge/pallas_call | solution.py:513
  20.1 5.6 %collective-permute-start.3 = (f32[33,24,128]{2,1,0:T(8,128)S(1)}, f32[33,24,128]{2,1,0:T(8,128)S(1)}, u32[]{:S(2)}, u32[]{:S(2)}) collective-permute-start(f32[33,24,128]{2,1,0:T(8,128)S(1)} %get-tuple-element.35), channel_id=1, source_target_pairs={{4,8},{5,9},{6,10},{7,11},{12,16},{13,17},{14,18},{15,19},{20,24},... | collective-permute-start | bytes 1216520 | tf_op jit(solution)/shard_map/ppermute | solution.py:586
  25.7 0.0 collective-permute-start.2
  25.7 6.0 %collective-permute-done.3.from_left_pair = f32[33,24,128]{2,1,0:T(8,128)S(1)} collective-permute-done((f32[33,24,128]{2,1,0:T(8,128)S(1)}, f32[33,24,128]{2,1,0:T(8,128)S(1)}, u32[]{:S(2)}, u32[]{:S(2)}) %collective-permute-start.3) | collective-permute-done | bytes 405536 | tf_op jit(solution)/shard_map/ppermute | solution.py:586
  31.7 1.8 %collective-permute-done.2.from_right_pair = f32[33,24,128]{2,1,0:T(8,128)S(1)} collective-permute-done((f32[33,24,128]{2,1,0:T(8,128)S(1)}, f32[33,24,128]{2,1,0:T(8,128)S(1)}, u32[]{:S(2)}, u32[]{:S(2)}) %collective-permute-start.2) | collective-permute-done | bytes 405536 | tf_op jit(solution)/shard_map/ppermute | solution.py:587
  33.5 0.5 %product.1 = f32[24,128]{1,0:T(8,128)S(1)} custom-call(f32[24,24,128]{2,1,0:T(8,128)S(1)} %get-tuple-element.22.left_in, f32[8,24,128]{2,1,0:T(8,128)S(1)} %get-tuple-element.31.left_edge, f32[24,24,128]{2,1,0:T(8,128)S(1)} %get-tuple-element.32.right_in, f32[8,24,128]{2,1,0:T(8,128)S(1)} %get-tuple-element.33.right_edge, ...), custom_call_target="tpu_custom_call" | custom-call | tf_op jit(solution)/shard_map/product/pallas_call | solution.py:537
  34.0 0.1 collective-permute-start.4
  34.1 1.2 %collective-permute-done.4 = f32[24,128]{1,0:T(8,128)S(1)} collective-permute-done((f32[24,128]{1,0:T(8,128)S(1)}, f32[24,128]{1,0:T(8,128)S(1)}, u32[]{:S(2)}, u32[]{:S(2)}) %collective-permute-start.4) | collective-permute-done | bytes 12320 | tf_op jit(solution)/shard_map/ppermute | solution.py:589
  35.2 5.3 %collective-permute-start.5 = (f32[24,128]{1,0:T(8,128)S(1)}, f32[24,128]{1,0:T(8,128)S(1)}, u32[]{:S(2)}, u32[]{:S(2)}) collective-permute-start(f32[24,128]{1,0:T(8,128)S(1)} %add.3.chip), channel_id=1, source_target_pairs={{0,2},{1,3},{2,0},{3,1},{4,6},{5,7},{6,4},{7,5},{8,10},{9,11},{10,... | collective-permute-start | bytes 36872 | tf_op jit(solution)/shard_map/ppermute | solution.py:591
  40.5 1.2 %collective-permute-done.5.other = f32[24,128]{1,0:T(8,128)S(1)} collective-permute-done((f32[24,128]{1,0:T(8,128)S(1)}, f32[24,128]{1,0:T(8,128)S(1)}, u32[]{:S(2)}, u32[]{:S(2)}) %collective-permute-start.5) | collective-permute-done | bytes 12320 | tf_op jit(solution)/shard_map/ppermute | solution.py:591
  41.7 2.3 %final.1 = (f32[24,32,256]{2,1,0:T(8,128)}, f32[2,24,24]{2,1,0:T(8,128)}) custom-call(f32[24,128]{1,0:T(8,128)S(1)} %add.3.chip, f32[24,128]{1,0:T(8,128)S(1)} %collective-permute-done.5.other, f32[24,24,256]{2,1,0:T(8,128)S(1)} %get-tuple-element.36.sub_in, f32[8,24,256]{2,1,0:T(8,128)S(1)} %get-tuple-element.37.sub_edge), custom_call_target="tpu_custom_call" | custom-call | tf_op jit(solution)/shard_map/final/pallas_call | solution.py:548
  (1 shorter events, 0.0 us)
Async XLA Ops:
  0.6 9.0 %copy-start.1 = (f32[1,32,512]{2,1,0:T(8,128)S(1)}, f32[1,32,512]{2,1,0:T(8,128)}, u32[]{:S(2)}) copy-start(f32[1,32,512]{2,1,0:T(8,128)} %param.3) | copy-start | bytes 196612
  0.6 9.0 %copy-start = (f32[1,24,32,512]{3,2,1,0:T(8,128)S(1)}, f32[1,24,32,512]{3,2,1,0:T(8,128)}, u32[]{:S(2)}) copy-start(f32[1,24,32,512]{3,2,1,0:T(8,128)} %param.2) | copy-start | bytes 4718596
  2.0 7.7 %collective-permute-start = (f32[25,8,512]{2,1,0:T(8,128)S(1)}, f32[25,8,512]{2,1,0:T(8,128)S(1)}, u32[]{:S(2)}, u32[]{:S(2)}) collective-permute-start(f32[25,8,512]{2,1,0:T(8,128)S(1)} %get-tuple-element.21), channel_id=1, source_target_pairs={{0,1},{2,3},{1,0},{3,2},{4,5},{6,7},{5,4},{7,6},{8,9},{10,11},{9,8... | collective-permute-start | bytes 1228808 | tf_op jit(solution)/shard_map/ppermute | solution.py:570
  2.7 15.0 %collective-permute-start.1 = (f32[25,8,512]{2,1,0:T(8,128)S(1)}, f32[25,8,512]{2,1,0:T(8,128)S(1)}, u32[]{:S(2)}, u32[]{:S(2)}) collective-permute-start(f32[25,8,512]{2,1,0:T(8,128)S(1)} %get-tuple-element.23), channel_id=1, source_target_pairs={{1,2},{2,1},{5,6},{6,5},{9,10},{10,9},{13,14},{14,13},{17,18},{18,... | collective-permute-start | bytes 1228808 | tf_op jit(solution)/shard_map/ppermute | solution.py:575
  20.1 11.6 %collective-permute-start.3 = (f32[33,24,128]{2,1,0:T(8,128)S(1)}, f32[33,24,128]{2,1,0:T(8,128)S(1)}, u32[]{:S(2)}, u32[]{:S(2)}) collective-permute-start(f32[33,24,128]{2,1,0:T(8,128)S(1)} %get-tuple-element.35), channel_id=1, source_target_pairs={{4,8},{5,9},{6,10},{7,11},{12,16},{13,17},{14,18},{15,19},{20,24},... | collective-permute-start | bytes 1216520 | tf_op jit(solution)/shard_map/ppermute | solution.py:586
  25.7 7.8 %collective-permute-start.2 = (f32[33,24,128]{2,1,0:T(8,128)S(1)}, f32[33,24,128]{2,1,0:T(8,128)S(1)}, u32[]{:S(2)}, u32[]{:S(2)}) collective-permute-start(f32[33,24,128]{2,1,0:T(8,128)S(1)} %get-tuple-element.34.sent), channel_id=1, source_target_pairs={{0,4},{8,12},{16,20},{24,28},{32,36},{40,44},{48,52},{56,60},{64,6... | collective-permute-start | bytes 1216520 | tf_op jit(solution)/shard_map/ppermute | solution.py:587
  34.0 1.2 %collective-permute-start.4 = (f32[24,128]{1,0:T(8,128)S(1)}, f32[24,128]{1,0:T(8,128)S(1)}, u32[]{:S(2)}, u32[]{:S(2)}) collective-permute-start(f32[24,128]{1,0:T(8,128)S(1)} %product.1), channel_id=1, source_target_pairs={{0,1},{2,3},{1,0},{3,2},{4,5},{6,7},{5,4},{7,6},{8,9},{10,11},{9,8... | collective-permute-start | bytes 36872 | tf_op jit(solution)/shard_map/ppermute | solution.py:589
  35.2 6.5 %collective-permute-start.5 = (f32[24,128]{1,0:T(8,128)S(1)}, f32[24,128]{1,0:T(8,128)S(1)}, u32[]{:S(2)}, u32[]{:S(2)}) collective-permute-start(f32[24,128]{1,0:T(8,128)S(1)} %add.3.chip), channel_id=1, source_target_pairs={{0,2},{1,3},{2,0},{3,1},{4,6},{5,7},{6,4},{7,5},{8,10},{9,11},{10,... | collective-permute-start | bytes 36872 | tf_op jit(solution)/shard_map/ppermute | solution.py:591

commit v10 on v9

--- a/solution.py
+++ b/solution.py
@@ -423,7 +423,7 @@
 
     high = own.astype(bf16).astype(f32)
     low = own - high
-    factor = jnp.concatenate([high, high, low, low], axis=1).astype(bf16)
+    factor = jnp.concatenate([high, high, low], axis=1).astype(bf16)
     stride = slabs.shape[2]
     copies = []
     for block in range(height // 8):
@@ -435,7 +435,7 @@
             x_high = x.astype(bf16).astype(f32)
             x_low = x - x_high
             value = dot_nn(
-                factor, jnp.concatenate([x_high, x_low, x_high, x_low], axis=0).astype(bf16)
+                factor, jnp.concatenate([x_high, x_low, x_high], axis=0).astype(bf16)
             )
             for c in range(sub_width // LANES):
                 flat = slabs.at[c].reshape(count * stride, LANES)
@@ -587,8 +587,7 @@
     from_1 = lax.ppermute(send_1, "patch", swaps(patches, 0))
     packed = call_product(left_in, left_edge, right_in, right_edge, from_1, from_2, send_1)
     chip = packed + lax.ppermute(packed, "quad", swaps(quads, 0))
-    half = quads // 2
-    other = lax.ppermute(chip, "quad", [(i, (i + half) % quads) for i in range(quads)])
+    other = lax.ppermute(chip, "quad", [(i, quads - 1 - i) for i in range(quads)])
     basis, coupling = call_final(chip, other, sub_in, sub_edge)
     return basis[None], coupling[None]
 

time: 44.8 us -> 44.7 us (level); the launches traced: 44 us -> 44.6 us
  no operation moved by 1% of the time
where the time goes in v10:
time: 44.7 us; the launch traced here: 44.6 us
  starting transfers between devices  18.8 us (42%)
  Pallas kernels  14.6 us (33%)
  waiting for transfers between devices  10.5 us (23%)
  between operations  0.67 us (1%)
    pallas_call x1, Pallas kernels, call_inner(): pl.pallas_call(functools.partial(inner_kernel, 'quad', 'patch'), out_shap...  8.08 us
    ppermute x1, starting transfers between devices, on_device(): halo_b = lax.ppermute(send_b, ('patch', 'quad'), middle + idle)  6.89 us
    ppermute x1, waiting for transfers between devices, on_device(): from_2 = lax.ppermute(send_2, ('patch', 'quad'), partners + idle)  5.97 us
    ppermute x1, starting transfers between devices, on_device(): from_2 = lax.ppermute(send_2, ('patch', 'quad'), partners + idle)  5.64 us
    ppermute x1, starting transfers between devices, on_device(): lax.ppermute(chip, 'quad', [(i, quads - 1 - i) for i in range(quads)])  5.5 us
    pallas_call x1, Pallas kernels, call_edge(): pl.pallas_call(functools.partial(edge_kernel, 'quad', 'patch'), out_shape...  2.34 us
    pallas_call x1, Pallas kernels, call_final(): pl.pallas_call(functools.partial(final_kernel, 'quad', 'patch'), out_shap...  2.33 us
    ppermute x1, waiting for transfers between devices, on_device(): from_1 = lax.ppermute(send_1, 'patch', swaps(patches, 0))  1.84 us
  transfers between devices with their start and end apart: 6, of which 4 were waited for; matrix products, arithmetic and copies ran while one was open for 0% of the time, Pallas kernels for 18%

profile of v10, /device:TPU:25, one launch (start us, length us, event | category | flops | bytes accessed | tf_op | source)
XLA Modules:
  0.0 44.6 jit_solution(15785105765165829927)
XLA Ops:
  0.6 0.0 copy-start.1
  0.6 0.0 copy-start
  0.6 1.3 %prepare.1 = (f32[25,8,512]{2,1,0:T(8,128)S(1)}, f32[25,8,512]{2,1,0:T(8,128)S(1)}) custom-call(f32[24,32,512]{2,1,0:T(8,128)} %bitcast.4, f32[32,512]{1,0:T(8,128)} %bitcast.6), custom_call_target="tpu_custom_call" | custom-call | tf_op jit(solution)/shard_map/prepare/pallas_call | solution.py:463
  2.0 0.8 %collective-permute-start = (f32[25,8,512]{2,1,0:T(8,128)S(1)}, f32[25,8,512]{2,1,0:T(8,128)S(1)}, u32[]{:S(2)}, u32[]{:S(2)}) collective-permute-start(f32[25,8,512]{2,1,0:T(8,128)S(1)} %get-tuple-element.21), channel_id=1, source_target_pairs={{0,1},{2,3},{1,0},{3,2},{4,5},{6,7},{5,4},{7,6},{8,9},{10,11},{9,8... | collective-permute-start | bytes 1228808 | tf_op jit(solution)/shard_map/ppermute | solution.py:570
  2.7 6.9 %collective-permute-start.1 = (f32[25,8,512]{2,1,0:T(8,128)S(1)}, f32[25,8,512]{2,1,0:T(8,128)S(1)}, u32[]{:S(2)}, u32[]{:S(2)}) collective-permute-start(f32[25,8,512]{2,1,0:T(8,128)S(1)} %get-tuple-element.23), channel_id=1, source_target_pairs={{1,2},{2,1},{5,6},{6,5},{9,10},{10,9},{13,14},{14,13},{17,18},{18,... | collective-permute-start | bytes 1228808 | tf_op jit(solution)/shard_map/ppermute | solution.py:575
  9.6 0.0 collective-permute-done.halo_a
  9.6 0.0 copy-done.1
  9.6 0.0 copy-done
  9.6 8.1 %inner.1 = (f32[24,24,128]{2,1,0:T(8,128)S(1)}, f32[24,24,128]{2,1,0:T(8,128)S(1)}, f32[24,24,256]{2,1,0:T(8,128)S(1)}, f32[24,24,128]{2,1,0:T(8,128)S(1)}, f32[...) custom-call(f32[24,32,512]{2,1,0:T(8,128)S(1)} %bitcast.5, ...), custom_call_target="tpu_custom_call" | custom-call | flops 37748736 | bytes 5242880 | tf_op jit(solution)/shard_map/inner/pallas_call | solution.py:481
  17.7 0.0 collective-permute-done.1.halo_b
  17.7 2.3 %edge.1 = (f32[8,24,128]{2,1,0:T(8,128)S(1)}, f32[8,24,128]{2,1,0:T(8,128)S(1)}, f32[8,24,256]{2,1,0:T(8,128)S(1)}, f32[33,24,128]{2,1,0:T(8,128)S(1)}, f32[33,24,128]{2,1,0:T(8,128)S(1)}) custom-call(f32[25,8,512]{2,1,0:T(8,128)S(1)} %collective-permute-done.1.halo_b, f32[32,512]{1,0:T(8,128)S(1)} %bitcast.8, ...), custom_call_target="tpu_custom_call" | custom-call | tf_op jit(solution)/shard_map/edge/pallas_call | solution.py:513
  20.1 5.6 %collective-permute-start.3 = (f32[33,24,128]{2,1,0:T(8,128)S(1)}, f32[33,24,128]{2,1,0:T(8,128)S(1)}, u32[]{:S(2)}, u32[]{:S(2)}) collective-permute-start(f32[33,24,128]{2,1,0:T(8,128)S(1)} %get-tuple-element.35), channel_id=1, source_target_pairs={{4,8},{5,9},{6,10},{7,11},{12,16},{13,17},{14,18},{15,19},{20,24},... | collective-permute-start | bytes 1216520 | tf_op jit(solution)/shard_map/ppermute | solution.py:586
  25.7 0.0 collective-permute-start.2
  25.7 6.0 %collective-permute-done.3.from_left_pair = f32[33,24,128]{2,1,0:T(8,128)S(1)} collective-permute-done((f32[33,24,128]{2,1,0:T(8,128)S(1)}, f32[33,24,128]{2,1,0:T(8,128)S(1)}, u32[]{:S(2)}, u32[]{:S(2)}) %collective-permute-start.3) | collective-permute-done | bytes 405536 | tf_op jit(solution)/shard_map/ppermute | solution.py:586
  31.7 1.8 %collective-permute-done.2.from_right_pair = f32[33,24,128]{2,1,0:T(8,128)S(1)} collective-permute-done((f32[33,24,128]{2,1,0:T(8,128)S(1)}, f32[33,24,128]{2,1,0:T(8,128)S(1)}, u32[]{:S(2)}, u32[]{:S(2)}) %collective-permute-start.2) | collective-permute-done | bytes 405536 | tf_op jit(solution)/shard_map/ppermute | solution.py:587
  33.5 0.5 %product.1 = f32[24,128]{1,0:T(8,128)S(1)} custom-call(f32[24,24,128]{2,1,0:T(8,128)S(1)} %get-tuple-element.22.left_in, f32[8,24,128]{2,1,0:T(8,128)S(1)} %get-tuple-element.31.left_edge, f32[24,24,128]{2,1,0:T(8,128)S(1)} %get-tuple-element.32.right_in, f32[8,24,128]{2,1,0:T(8,128)S(1)} %get-tuple-element.33.right_edge, ...), custom_call_target="tpu_custom_call" | custom-call | tf_op jit(solution)/shard_map/product/pallas_call | solution.py:537
  34.0 0.1 collective-permute-start.4
  34.1 1.2 %collective-permute-done.4 = f32[24,128]{1,0:T(8,128)S(1)} collective-permute-done((f32[24,128]{1,0:T(8,128)S(1)}, f32[24,128]{1,0:T(8,128)S(1)}, u32[]{:S(2)}, u32[]{:S(2)}) %collective-permute-start.4) | collective-permute-done | bytes 12320 | tf_op jit(solution)/shard_map/ppermute | solution.py:589
  35.2 5.5 %collective-permute-start.5 = (f32[24,128]{1,0:T(8,128)S(1)}, f32[24,128]{1,0:T(8,128)S(1)}, u32[]{:S(2)}, u32[]{:S(2)}) collective-permute-start(f32[24,128]{1,0:T(8,128)S(1)} %add.3.chip), channel_id=1, source_target_pairs={{0,3},{1,2},{2,1},{3,0},{4,7},{5,6},{6,5},{7,4},{8,11},{9,10},{10,... | collective-permute-start | bytes 36872 | tf_op jit(solution)/shard_map/ppermute | solution.py:590
  40.7 1.5 %collective-permute-done.5.other = f32[24,128]{1,0:T(8,128)S(1)} collective-permute-done((f32[24,128]{1,0:T(8,128)S(1)}, f32[24,128]{1,0:T(8,128)S(1)}, u32[]{:S(2)}, u32[]{:S(2)}) %collective-permute-start.5) | collective-permute-done | bytes 12320 | tf_op jit(solution)/shard_map/ppermute | solution.py:590
  42.3 2.3 %final.1 = (f32[24,32,256]{2,1,0:T(8,128)}, f32[2,24,24]{2,1,0:T(8,128)}) custom-call(f32[24,128]{1,0:T(8,128)S(1)} %add.3.chip, f32[24,128]{1,0:T(8,128)S(1)} %collective-permute-done.5.other, f32[24,24,256]{2,1,0:T(8,128)S(1)} %get-tuple-element.36.sub_in, f32[8,24,256]{2,1,0:T(8,128)S(1)} %get-tuple-element.37.sub_edge), custom_call_target="tpu_custom_call" | custom-call | tf_op jit(solution)/shard_map/final/pallas_call | solution.py:548
  (1 shorter events, 0.0 us)
Async XLA Ops:
  0.6 9.0 %copy-start.1 = (f32[1,32,512]{2,1,0:T(8,128)S(1)}, f32[1,32,512]{2,1,0:T(8,128)}, u32[]{:S(2)}) copy-start(f32[1,32,512]{2,1,0:T(8,128)} %param.3) | copy-start | bytes 196612
  0.6 9.0 %copy-start = (f32[1,24,32,512]{3,2,1,0:T(8,128)S(1)}, f32[1,24,32,512]{3,2,1,0:T(8,128)}, u32[]{:S(2)}) copy-start(f32[1,24,32,512]{3,2,1,0:T(8,128)} %param.2) | copy-start | bytes 4718596
  2.0 7.7 %collective-permute-start = (f32[25,8,512]{2,1,0:T(8,128)S(1)}, f32[25,8,512]{2,1,0:T(8,128)S(1)}, u32[]{:S(2)}, u32[]{:S(2)}) collective-permute-start(f32[25,8,512]{2,1,0:T(8,128)S(1)} %get-tuple-element.21), channel_id=1, source_target_pairs={{0,1},{2,3},{1,0},{3,2},{4,5},{6,7},{5,4},{7,6},{8,9},{10,11},{9,8... | collective-permute-start | bytes 1228808 | tf_op jit(solution)/shard_map/ppermute | solution.py:570
  2.7 15.0 %collective-permute-start.1 = (f32[25,8,512]{2,1,0:T(8,128)S(1)}, f32[25,8,512]{2,1,0:T(8,128)S(1)}, u32[]{:S(2)}, u32[]{:S(2)}) collective-permute-start(f32[25,8,512]{2,1,0:T(8,128)S(1)} %get-tuple-element.23), channel_id=1, source_target_pairs={{1,2},{2,1},{5,6},{6,5},{9,10},{10,9},{13,14},{14,13},{17,18},{18,... | collective-permute-start | bytes 1228808 | tf_op jit(solution)/shard_map/ppermute | solution.py:575
  20.1 11.6 %collective-permute-start.3 = (f32[33,24,128]{2,1,0:T(8,128)S(1)}, f32[33,24,128]{2,1,0:T(8,128)S(1)}, u32[]{:S(2)}, u32[]{:S(2)}) collective-permute-start(f32[33,24,128]{2,1,0:T(8,128)S(1)} %get-tuple-element.35), channel_id=1, source_target_pairs={{4,8},{5,9},{6,10},{7,11},{12,16},{13,17},{14,18},{15,19},{20,24},... | collective-permute-start | bytes 1216520 | tf_op jit(solution)/shard_map/ppermute | solution.py:586
  25.7 7.8 %collective-permute-start.2 = (f32[33,24,128]{2,1,0:T(8,128)S(1)}, f32[33,24,128]{2,1,0:T(8,128)S(1)}, u32[]{:S(2)}, u32[]{:S(2)}) collective-permute-start(f32[33,24,128]{2,1,0:T(8,128)S(1)} %get-tuple-element.34.sent), channel_id=1, source_target_pairs={{0,4},{8,12},{16,20},{24,28},{32,36},{40,44},{48,52},{56,60},{64,6... | collective-permute-start | bytes 1216520 | tf_op jit(solution)/shard_map/ppermute | solution.py:587
  34.0 1.2 %collective-permute-start.4 = (f32[24,128]{1,0:T(8,128)S(1)}, f32[24,128]{1,0:T(8,128)S(1)}, u32[]{:S(2)}, u32[]{:S(2)}) collective-permute-start(f32[24,128]{1,0:T(8,128)S(1)} %product.1), channel_id=1, source_target_pairs={{0,1},{2,3},{1,0},{3,2},{4,5},{6,7},{5,4},{7,6},{8,9},{10,11},{9,8... | collective-permute-start | bytes 36872 | tf_op jit(solution)/shard_map/ppermute | solution.py:589
  35.2 7.0 %collective-permute-start.5 = (f32[24,128]{1,0:T(8,128)S(1)}, f32[24,128]{1,0:T(8,128)S(1)}, u32[]{:S(2)}, u32[]{:S(2)}) collective-permute-start(f32[24,128]{1,0:T(8,128)S(1)} %add.3.chip), channel_id=1, source_target_pairs={{0,3},{1,2},{2,1},{3,0},{4,7},{5,6},{6,5},{7,4},{8,11},{9,10},{10,... | collective-permute-start | bytes 36872 | tf_op jit(solution)/shard_map/ppermute | solution.py:590
